TPU v7x, 256 devices: a whole 4x4x8 slice. The times are simulated.
256 devices in a mesh: dp: 8 (over y, core), block: 32 (over x, z).
Axes of the slice: x: 4, y: 4, z: 8, core: 2. Of those that a mesh axis runs over, the one named last changes fastest.
Arguments:
- queries: bfloat16 [8, 64, 64, 4096], P('dp', 'block'), may hold values from -24 to 24
- keys_pool: bfloat16 [8, 32, 128, 4096], P('dp', None, None, 'block'), may hold values from -24 to 24
- values_pool: bfloat16 [8, 32, 128, 4096], P('dp', None, None, 'block'), may hold values from -6 to 6
- rel_bias: float32 [32, 192], replicated, may hold values from -4 to 4
- out_grad: bfloat16 [8, 64, 64, 4096], P('dp', 'block'), may hold values from -6 to 6
- fetch_ids: int32 [8, 32, 3], P('dp', 'block'), may hold values from 0 to 31, as said below
- slot_of: int32 [8, 64, 2], P('dp', 'block'), may hold values from 0 to 2, as said below
Outputs:
- attended: bfloat16 [8, 64, 64, 4096], P('dp', 'block')
- query_grad: bfloat16 [8, 64, 64, 4096], P('dp', 'block')
- key_grad: bfloat16 [8, 32, 128, 4096], P('dp', None, None, 'block')
- value_grad: bfloat16 [8, 32, 128, 4096], P('dp', None, None, 'block')
- bias_grad: float32 [32, 192], replicated
Inputs may be any that keep to these rules, and one draw needn't show every extreme that they name: `fetch_ids`: A device's fetch list holds 3 different encodings. `slot_of`: every position of a device's fetch list is read by some block of that device; the two neighbours of a block are different, and the first neighbours of a device's blocks are all different.
All inputs are finite; a program needn't handle non-finite values.
Results may differ from a plain program's by a relative error of at most 0.022.
Values may be sent and summed in bfloat16 or wider, within the bound.
No kernel may reach another device: no remote copies, remote signals or barrier semaphores. Data moves between devices by JAX's collectives and lax.ppermute only.
A program may use at most 128 MiB of HBM per device.

v0:
```python
import math

import jax
import jax.numpy as jnp
from jax import lax
from jax.sharding import PartitionSpec as P

HEADS = 32
HEAD_DIM = 128
BLOCK = 64
NBLEN = 128
NEIGH = 2
CH_DEV = 2
REL = 192


def build_bias(rel_bias):
    query_pos = jnp.arange(BLOCK)[:, None]
    key_pos = jnp.arange(NBLEN)[None, :]
    offsets = (key_pos - query_pos + BLOCK - 1).reshape(-1)
    one_hot = (jnp.arange(REL)[:, None] == offsets[None, :]).astype(jnp.float32)
    table = jnp.dot(rel_bias, one_hot, precision=lax.Precision.HIGHEST)
    table = table.reshape(rel_bias.shape[0], BLOCK, NBLEN)
    return (jnp.concatenate([table] * NEIGH, axis=-1), one_hot)


def fold_bias(dscore_sum, one_hot):
    heads_here = dscore_sum.shape[0]
    folded = jnp.sum(dscore_sum.reshape(heads_here, BLOCK, NEIGH, NBLEN), axis=2)
    return jnp.dot(
        folded.reshape(heads_here, BLOCK * NBLEN), one_hot.T, precision=lax.Precision.HIGHEST
    )


def forward_backward(query_rows, key_rows, value_rows, grad_rows, bias):
    scale = 1.0 / math.sqrt(HEAD_DIM)
    scores = (
        jnp.einsum("cihd,cjhd->chij", query_rows, key_rows, preferred_element_type=jnp.float32)
        * scale
        + bias[None]
    )
    top_score = jnp.max(scores, axis=-1, keepdims=True)
    expo = jnp.exp(scores - top_score)
    probs = expo / jnp.sum(expo, axis=-1, keepdims=True)
    probs_low = probs.astype(jnp.bfloat16)
    attended = jnp.einsum(
        "chij,cjhd->cihd", probs_low, value_rows, preferred_element_type=jnp.float32
    ).astype(jnp.bfloat16)
    dprobs = jnp.einsum(
        "cihd,cjhd->chij", grad_rows, value_rows, preferred_element_type=jnp.float32
    )
    inner = jnp.sum(probs * dprobs, axis=-1, keepdims=True)
    dscores = probs * (dprobs - inner)
    dscores_low = dscores.astype(jnp.bfloat16)
    query_grad = (
        jnp.einsum("chij,cjhd->cihd", dscores_low, key_rows, preferred_element_type=jnp.float32)
        * scale
    ).astype(jnp.bfloat16)
    return (attended, query_grad, probs_low, dscores_low, jnp.sum(dscores, axis=0))


def pool_sum(parts, flat_ids, pool_size):
    picker = (flat_ids[:, None] == jnp.arange(pool_size)[None, :]).astype(jnp.float32)
    return jnp.dot(picker.T, parts.reshape(flat_ids.shape[0], -1), precision=lax.Precision.HIGHEST)


def on_device(queries, keys_pool, values_pool, rel_bias, out_grad, fetch_ids, slot_of):
    all_fetch, all_slots = (
        lax.all_gather(fetch_ids, "block", axis=1, tiled=True),
        lax.all_gather(slot_of, "block", axis=1, tiled=True),
    )
    width = queries.shape[3]
    pool_size = keys_pool.shape[1]
    local_width = keys_pool.shape[3]
    fetch_count = fetch_ids.shape[2]
    scale = 1.0 / math.sqrt(HEAD_DIM)
    bias, one_hot = build_bias(rel_bias)
    send_keys = keys_pool[0][all_fetch[0]]
    send_values = values_pool[0][all_fetch[0]]
    fetched_keys, fetched_values = (
        lax.all_to_all(send_keys, "block", split_axis=0, concat_axis=3, tiled=True),
        lax.all_to_all(send_values, "block", split_axis=0, concat_axis=3, tiled=True),
    )
    slots = slot_of[0]
    key_rows = fetched_keys[0][slots].reshape(CH_DEV, NEIGH * NBLEN, HEADS, HEAD_DIM)
    value_rows = fetched_values[0][slots].reshape(CH_DEV, NEIGH * NBLEN, HEADS, HEAD_DIM)
    query_rows = queries[0].reshape(CH_DEV, BLOCK, HEADS, HEAD_DIM)
    grad_rows = out_grad[0].reshape(CH_DEV, BLOCK, HEADS, HEAD_DIM)
    attended_rows, query_rows_grad, probs_low, dscores_low, dscore_sum = forward_backward(
        query_rows, key_rows, value_rows, grad_rows, bias
    )
    attended = attended_rows.reshape(queries.shape)
    query_grad = query_rows_grad.reshape(queries.shape)
    slot_table = (slots[:, :, None] == jnp.arange(fetch_count)[None, None, :]).astype(jnp.bfloat16)
    split_shape = (CH_DEV, HEADS, BLOCK, NEIGH, NBLEN)
    dscore_slots = jnp.einsum(
        "cns,chinj->schij",
        slot_table,
        dscores_low.reshape(split_shape),
        preferred_element_type=jnp.bfloat16,
    )
    prob_slots = jnp.einsum(
        "cns,chinj->schij",
        slot_table,
        probs_low.reshape(split_shape),
        preferred_element_type=jnp.bfloat16,
    )
    key_local = (
        jnp.einsum("schij,cihd->sjhd", dscore_slots, query_rows, preferred_element_type=jnp.float32)
        * scale
    )
    value_local = jnp.einsum(
        "schij,cihd->sjhd", prob_slots, grad_rows, preferred_element_type=jnp.float32
    )
    key_local = key_local.reshape(1, fetch_count, NBLEN, width)
    value_local = value_local.reshape(1, fetch_count, NBLEN, width)
    back_keys, back_values = (
        lax.all_to_all(
            key_local.astype(jnp.bfloat16), "block", split_axis=3, concat_axis=0, tiled=True
        ).astype(key_local.dtype),
        lax.all_to_all(
            value_local.astype(jnp.bfloat16), "block", split_axis=3, concat_axis=0, tiled=True
        ).astype(value_local.dtype),
    )
    flat_ids = all_fetch[0].reshape(-1)
    key_sum = pool_sum(back_keys, flat_ids, pool_size)
    value_sum = pool_sum(back_values, flat_ids, pool_size)
    bias_terms = fold_bias(dscore_sum, one_hot)
    key_grad = key_sum.astype(jnp.bfloat16).reshape(1, pool_size, NBLEN, local_width)
    value_grad = value_sum.astype(jnp.bfloat16).reshape(1, pool_size, NBLEN, local_width)
    bias_grad = lax.psum(bias_terms, ("dp", "block"))
    return (attended, query_grad, key_grad, value_grad, bias_grad)


def solution(mesh):
    in_specs = (
        P("dp", "block", None, None),
        P("dp", None, None, "block"),
        P("dp", None, None, "block"),
        P(),
        P("dp", "block", None, None),
        P("dp", "block", None),
        P("dp", "block", None),
    )
    out_specs = (
        P("dp", "block", None, None),
        P("dp", "block", None, None),
        P("dp", None, None, "block"),
        P("dp", None, None, "block"),
        P(),
    )
    return jax.shard_map(
        on_device, mesh=mesh, in_specs=in_specs, out_specs=out_specs, check_vma=False
    )
```

profile of v0, /device:TPU:16, one launch (start us, length us, event | category | flops | bytes accessed | tf_op | source)
XLA Modules:
  0.0 503.8 jit_solution(8100999621977639680)
XLA Ops:
  0.6 41.9 %all_gather.3 = s32[1,32,3]{2,0,1:T(1,128)S(1)} all-gather(s32[1,1,3]{2,0,1:T(1,128)} %bitcast.180), channel_id=1, replica_groups=mesh['dp'=8,'block'=32] {'block'}, dimensions={1}, use_global_device_ids=true | all-gather | bytes 396 | tf_op jit(solution)/shard_map/all_gather | solution.py:69
  45.6 6.1 %all-to-all-start = ((bf16[32,3,128,128]{3,2,1,0:T(8,128)(2,1)}), bf16[32,3,128,128]{3,2,1,0:T(8,128)(2,1)S(1)}, u32[]{:S(2)}, u32[]{:S(2)}) async-start(bf16[32,3,128,128]{3,2,1,0:T(8,128)(2,1)} %bitcast.166), calls=%async_computation | async-start | bytes 6291456 | tf_op jit(solution)/shard_map/all_to_all | solution.py:82
  51.7 4.0 gather_fusion.2
  55.7 61.4 %all-to-all-done = bf16[32,3,128,128]{3,2,1,0:T(8,128)(2,1)S(1)} async-done(((bf16[32,3,128,128]{3,2,1,0:T(8,128)(2,1)}), bf16[32,3,128,128]{3,2,1,0:T(8,128)(2,1)S(1)}, u32[]{:S(2)}, u32[]{:S(2)}) %all-to-all-start) | async-done | bytes 3145760 | tf_op jit(solution)/shard_map/all_to_all | solution.py:82
  117.1 5.5 %all-to-all-start.1 = ((bf16[32,3,128,128]{3,2,1,0:T(8,128)(2,1)}), bf16[32,3,128,128]{3,2,1,0:T(8,128)(2,1)}, u32[]{:S(2)}, u32[]{:S(2)}) async-start(bf16[32,3,128,128]{3,2,1,0:T(8,128)(2,1)} %bitcast.9), calls=%async_computation.1 | async-start | bytes 6291456 | tf_op jit(solution)/shard_map/all_to_all | solution.py:81
  132.2 3.5 copy.111
  138.7 6.5 %copy.112 = bf16[4,128,4096]{2,1,0:T(8,128)(2,1)} copy(bf16[4,128,4096]{1,2,0:T(8,128)(2,1)} %gather_fusion.1) | data formatting | bytes 8388608 | tf_op jit(solution)/shard_map/gather | solution.py:86
  145.2 5.4 %copy.147 = bf16[64,8,32,128]{3,2,1,0:T(8,128)(2,1)} copy(bf16[64,8,32,128]{3,1,2,0:T(8,128)(2,1)} %bitcast.159) | data formatting | bytes 8388608
  150.6 36.3 %all-to-all-done.1 = bf16[32,3,128,128]{3,2,1,0:T(8,128)(2,1)} async-done(((bf16[32,3,128,128]{3,2,1,0:T(8,128)(2,1)}), bf16[32,3,128,128]{3,2,1,0:T(8,128)(2,1)}, u32[]{:S(2)}, u32[]{:S(2)}) %all-to-all-start.1) | async-done | bytes 3145760 | tf_op jit(solution)/shard_map/all_to_all | solution.py:81
  186.9 3.5 copy.113
  193.5 6.4 %copy.114 = bf16[4,128,4096]{2,1,0:T(8,128)(2,1)} copy(bf16[4,128,4096]{1,2,0:T(8,128)(2,1)} %gather_fusion.3) | data formatting | bytes 8388608 | tf_op jit(solution)/shard_map/gather | solution.py:85
  199.9 5.5 %copy.144 = bf16[64,8,32,128]{3,2,1,0:T(8,128)(2,1)} copy(bf16[64,8,32,128]{3,1,2,0:T(8,128)(2,1)} %bitcast.160) | data formatting | bytes 8388608
  205.4 4.6 fusion.12
  210.0 6.1 %fusion.65 = (f32[2,32,64]{2,1,0:T(8,128)S(1)}, f32[2,32,64,256]{3,2,1,0:T(8,128)S(1)}) fusion(f32[2,32,256,64]{2,3,1,0:T(8,128)S(1)} %fusion.12, f32[32,64,256]{2,1,0:T(8,128)S(1)} %copy-done.6), kind=kOutput, calls=%fused_computation.76 | output fusion | flops 6291711 | bytes 10502144 | tf_op jit(solution)/shard_map/sub | solution.py:43
  216.2 6.5 %fusion.4 = (f32[2,32,64]{2,1,0:T(8,128)S(1)}, f32[2,32,256,64]{2,3,1,0:T(8,128)S(1)}) fusion(f32[2,32,64,256]{3,2,1,0:T(8,128)S(1)} %get-tuple-element.9, f32[2,32,64]{2,1,0:T(8,128)S(1)} %get-tuple-element.8, bf16[2,64,32,128]{3,2,1,0:T(8,128)(2,1)S(1)} %bitcast.172, bf16[2,256,32,128]{3,2,1,0:T(8,128)(2,1)S(1)} %bitcast.158), kind=kOutput, calls=%fused_computation.15 | convolution fusion | flops 271577088 | bytes 13664256 | tf_op jit(solution)/shard_map/cihd,cjhd->chij/dot_general | solution.py:49
  222.7 4.2 fusion.35
  226.9 4.1 reshape.165
  231.1 4.1 convolution_bitcast_fusion.1
  236.8 20.5 %copy.126 = bf16[1,3,128,4096]{2,1,0,3:T(4,128)(2,1)} copy(bf16[1,3,128,4096]{2,3,1,0:T(8,128)(2,1)S(1)} %bitcast.162) | data formatting | bytes 6291456 | tf_op jit(solution)/shard_map/convert_element_type | solution.py:119
  257.3 5.1 %all-to-all-start.2 = ((bf16[1,3,128,4096]{2,1,0,3:T(4,128)(2,1)}), bf16[1,3,128,4096]{2,1,0,3:T(4,128)(2,1)}, u32[]{:S(2)}, u32[]{:S(2)}) async-start(bf16[1,3,128,4096]{2,1,0,3:T(4,128)(2,1)} %copy.126), calls=%async_computation.2 | async-start | bytes 8388608 | tf_op jit(solution)/shard_map/all_to_all | solution.py:118
  265.8 4.0 convolution_bitcast_fusion
  271.1 20.5 %copy.131 = bf16[1,3,128,4096]{2,1,0,3:T(4,128)(2,1)} copy(bf16[1,3,128,4096]{2,3,1,0:T(8,128)(2,1)S(1)} %bitcast.163) | data formatting | bytes 6291456 | tf_op jit(solution)/shard_map/convert_element_type | solution.py:122
  291.6 55.8 %all-to-all-done.2 = bf16[1,3,128,4096]{2,1,0,3:T(4,128)(2,1)} async-done(((bf16[1,3,128,4096]{2,1,0,3:T(4,128)(2,1)}), bf16[1,3,128,4096]{2,1,0,3:T(4,128)(2,1)}, u32[]{:S(2)}, u32[]{:S(2)}) %all-to-all-start.2) | async-done | bytes 3145760 | tf_op jit(solution)/shard_map/all_to_all | solution.py:118
  347.4 5.5 %all-to-all-start.3 = ((bf16[1,3,128,4096]{2,1,0,3:T(4,128)(2,1)}), bf16[1,3,128,4096]{2,1,0,3:T(4,128)(2,1)}, u32[]{:S(2)}, u32[]{:S(2)}) async-start(bf16[1,3,128,4096]{2,1,0,3:T(4,128)(2,1)} %copy.131), calls=%async_computation.3 | async-start | bytes 8388608 | tf_op jit(solution)/shard_map/all_to_all | solution.py:121
  354.2 3.2 reshape.171
  357.5 5.1 %fusion.43 = bf16[2,64,32,128]{3,1,2,0:T(8,128)(2,1)S(1)} fusion(bf16[2,32,64,256]{3,2,1,0:T(8,128)(2,1)} %get-tuple-element.6, bf16[2,256,32,128]{3,2,1,0:T(8,128)(2,1)} %bitcast.46), kind=kOutput, calls=%fused_computation.51 | convolution fusion | flops 269484032 | bytes 7340032 | tf_op jit(solution)/shard_map/chij,cjhd->cihd/dot_general | solution.py:56
  364.6 4.5 fusion.40
  373.8 3.4 fusion.2
  377.2 105.4 %psum.7 = f32[32,192]{1,0:T(8,128)} all-reduce(f32[32,192]{1,0:T(8,128)S(1)} %fusion.2), channel_id=1, replica_groups=mesh['dp'=8,'block'=32] {'dp','block'}, use_global_device_ids=true, to_apply=%region_5.0 | all-reduce | flops 6144 | bytes 49152 | tf_op jit(solution)/shard_map/psum | solution.py:131
  482.6 5.5 %copy.127 = bf16[1,3,128,32,128]{4,2,1,3,0:T(8,128)(2,1)S(1)} copy(bf16[1,3,128,32,128]{2,1,4,3,0:T(4,128)(2,1)} %bitcast.28) | data formatting | bytes 6291456 | tf_op jit(solution)/shard_map/all_to_all | solution.py:118
  491.4 7.1 %copy.132 = bf16[1,3,128,32,128]{4,2,1,3,0:T(8,128)(2,1)} copy(bf16[1,3,128,32,128]{2,1,4,3,0:T(4,128)(2,1)} %bitcast.37) | data formatting | bytes 6291456 | tf_op jit(solution)/shard_map/all_to_all | solution.py:121
  498.4 3.9 fusion.50
  (60 shorter events, 37.3 us)
Async XLA Ops:
  0.6 42.2 %copy-start = (bf16[1,32,128,128]{3,2,1,0:T(8,128)(2,1)S(1)}, bf16[1,32,128,128]{3,2,1,0:T(8,128)(2,1)}, u32[]{:S(2)}) copy-start(bf16[1,32,128,128]{3,2,1,0:T(8,128)(2,1)} %param.9) | copy-start | bytes 3145732
  45.6 71.5 %all-to-all-start = ((bf16[32,3,128,128]{3,2,1,0:T(8,128)(2,1)}), bf16[32,3,128,128]{3,2,1,0:T(8,128)(2,1)S(1)}, u32[]{:S(2)}, u32[]{:S(2)}) async-start(bf16[32,3,128,128]{3,2,1,0:T(8,128)(2,1)} %bitcast.166), calls=%async_computation | async-start | bytes 6291456 | tf_op jit(solution)/shard_map/all_to_all | solution.py:82
  55.7 66.9 %copy-start.10 = (s32[1,2,2]{2,1,0:T(2,128)S(1)}, s32[1,2,2]{2,1,0:T(2,128)}, u32[]{:S(2)}) copy-start(s32[1,2,2]{2,1,0:T(2,128)} %param.13) | copy-start | bytes 52
  117.1 7.1 %copy-start.3 = (bf16[32,3,128,128]{3,2,1,0:T(8,128)(2,1)}, bf16[32,3,128,128]{3,2,1,0:T(8,128)(2,1)S(1)}, u32[]{:S(2)}) copy-start(bf16[32,3,128,128]{3,2,1,0:T(8,128)(2,1)S(1)} %all-to-all-done) | copy-start | bytes 9437188
  117.1 9.9 %copy-start.11 = (f32[32,192]{1,0:T(8,128)S(1)}, f32[32,192]{1,0:T(8,128)}, u32[]{:S(2)}) copy-start(f32[32,192]{1,0:T(8,128)} %param.10) | copy-start | bytes 73732
  117.1 69.8 %all-to-all-start.1 = ((bf16[32,3,128,128]{3,2,1,0:T(8,128)(2,1)}), bf16[32,3,128,128]{3,2,1,0:T(8,128)(2,1)}, u32[]{:S(2)}, u32[]{:S(2)}) async-start(bf16[32,3,128,128]{3,2,1,0:T(8,128)(2,1)} %bitcast.9), calls=%async_computation.1 | async-start | bytes 6291456 | tf_op jit(solution)/shard_map/all_to_all | solution.py:81
  124.2 7.0 %copy-start.4 = (bf16[16,8,32,128]{3,2,1,0:T(8,128)(2,1)}, bf16[16,8,32,128]{3,2,1,0:T(8,128)(2,1)S(1)}, u32[]{:S(2)}) copy-start(bf16[16,8,32,128]{3,2,1,0:T(8,128)(2,1)S(1)} %copy.145) | copy-start | bytes 3145732
  199.9 5.5 %copy-start.5 = (bf16[16,8,32,128]{3,2,1,0:T(8,128)(2,1)S(1)}, bf16[16,8,32,128]{3,2,1,0:T(8,128)(2,1)}, u32[]{:S(2)}) copy-start(bf16[16,8,32,128]{3,2,1,0:T(8,128)(2,1)} %copy-done.4) | copy-start | bytes 3145732
  205.4 4.6 copy-start.6
  210.0 6.1 %copy-start.2 = (bf16[64,8,32,128]{3,2,1,0:T(8,128)(2,1)S(1)}, bf16[64,8,32,128]{3,2,1,0:T(8,128)(2,1)}, u32[]{:S(2)}) copy-start(bf16[64,8,32,128]{3,2,1,0:T(8,128)(2,1)} %copy.147) | copy-start | bytes 12582916
  210.0 6.1 %copy-start.8 = (bf16[16,8,32,128]{3,2,1,0:T(8,128)(2,1)S(1)}, bf16[16,8,32,128]{3,2,1,0:T(8,128)(2,1)}, u32[]{:S(2)}) copy-start(bf16[16,8,32,128]{3,2,1,0:T(8,128)(2,1)} %copy.148) | copy-start | bytes 3145732
  231.1 4.1 copy-start.9
  257.3 90.1 %all-to-all-start.2 = ((bf16[1,3,128,4096]{2,1,0,3:T(4,128)(2,1)}), bf16[1,3,128,4096]{2,1,0,3:T(4,128)(2,1)}, u32[]{:S(2)}, u32[]{:S(2)}) async-start(bf16[1,3,128,4096]{2,1,0,3:T(4,128)(2,1)} %copy.126), calls=%async_computation.2 | async-start | bytes 8388608 | tf_op jit(solution)/shard_map/all_to_all | solution.py:118
  347.4 144.0 %all-to-all-start.3 = ((bf16[1,3,128,4096]{2,1,0,3:T(4,128)(2,1)}), bf16[1,3,128,4096]{2,1,0,3:T(4,128)(2,1)}, u32[]{:S(2)}, u32[]{:S(2)}) async-start(bf16[1,3,128,4096]{2,1,0,3:T(4,128)(2,1)} %copy.131), calls=%async_computation.3 | async-start | bytes 8388608 | tf_op jit(solution)/shard_map/all_to_all | solution.py:121
  369.0 2.1 copy-start.7
  491.4 12.2 %copy-start.1 = (bf16[1,32,128,128]{3,2,1,0:T(8,128)(2,1)S(1)}, bf16[1,32,128,128]{3,2,1,0:T(8,128)(2,1)}, u32[]{:S(2)}) copy-start(bf16[1,32,128,128]{3,2,1,0:T(8,128)(2,1)} %param.9) | copy-start | bytes 3145732
where the time goes:
time: 509 us; the launch traced here: 504 us
  waiting for transfers between devices  154 us (30%)
  blocking collectives  147 us (29%)
  local copies, waits for them, and re-layouts  121 us (24%)
  matrix products  43.1 us (8%)
  starting transfers between devices  22.2 us (4%)
  other arithmetic  15.1 us (3%)
    psum x1, blocking collectives, on_device(): bias_grad = lax.psum(bias_terms, ('dp', 'block'))  105 us
    all_to_all x1, waiting for transfers between devices, on_device(): lax.all_to_all(send_values, 'block', split_axis=0, concat_axis=3, tiled=T...  61.4 us
    all_to_all x1, waiting for transfers between devices, on_device(): lax.all_to_all(key_local.astype(jnp.bfloat16), 'block', split_axis=3, con...  55.8 us
    all_gather x1, blocking collectives, on_device(): lax.all_gather(fetch_ids, 'block', axis=1, tiled=True)  41.9 us
    all_to_all x1, waiting for transfers between devices, on_device(): lax.all_to_all(send_keys, 'block', split_axis=0, concat_axis=3, tiled=True)  36.3 us
    convert_element_type x2, local copies, waits for them, and re-layouts, on_device(): key_local.astype(jnp.bfloat16)  20.7 us
    convert_element_type x2, local copies, waits for them, and re-layouts, on_device(): value_local.astype(jnp.bfloat16)  20.7 us
    unnamed x31, local copies, waits for them, and re-layouts  17.8 us
  transfers between devices with their start and end apart: 4, of which 3 were waited for; matrix products, arithmetic and copies ran while one was open for 19% of the time, Pallas kernels for 0%

commit v1 on v0

v1 whole, which is shorter than its diff:
```python
import functools
import math

import jax
import jax.numpy as jnp
from jax import lax
from jax.experimental import pallas as pl
from jax.experimental.pallas import tpu as pltpu
from jax.sharding import PartitionSpec as P

HEADS = 32
HEAD_DIM = 128
BLOCK = 64
NBLEN = 128
NEIGH = 2
CH_DEV = 2
POOL = 32
HD = HEADS * HEAD_DIM
REL = 192
N_BLOCK = 32
N_DP = 8
HALF = CH_DEV * BLOCK
DATA = 2 * HALF
ROWS = DATA + 16
PACK_HEADS = 8
SRC_STEP = 4
SCALE = 1.0 / math.sqrt(HEAD_DIM)

NT = (((1,), (1,)), ((), ()))
TN = (((0,), (0,)), ((), ()))
F32 = jnp.float32
BF16 = jnp.bfloat16


def pack_kernel(fetch_ref, slot_ref, q_ref, g_ref, out_ref):
    lane = lax.broadcasted_iota(jnp.int32, (16, 128), 1)
    ids = jnp.zeros((16, 128), jnp.int32)
    for c in range(CH_DEV):
        for n in range(NEIGH):
            enc = fetch_ref[0, 0, slot_ref[0, c, n]]
            ids = jnp.where(lane == c * NEIGH + n, enc, ids)
    ids = ids.astype(F32).astype(BF16)
    for h in range(PACK_HEADS):
        cols = slice(h * HEAD_DIM, (h + 1) * HEAD_DIM)
        for c in range(CH_DEV):
            out_ref[h, c * BLOCK : (c + 1) * BLOCK] = q_ref[0, c, :, cols]
            out_ref[h, HALF + c * BLOCK : HALF + (c + 1) * BLOCK] = g_ref[0, c, :, cols]
        out_ref[h, DATA:] = ids


def pack(fetch_ids, slot_of, queries, out_grad):
    rows = pl.BlockSpec((1, CH_DEV, BLOCK, PACK_HEADS * HEAD_DIM), lambda i: (0, 0, 0, i))
    return pl.pallas_call(
        pack_kernel,
        grid=(HEADS // PACK_HEADS,),
        in_specs=[
            pl.BlockSpec(memory_space=pltpu.SMEM),
            pl.BlockSpec(memory_space=pltpu.SMEM),
            rows,
            rows,
        ],
        out_specs=pl.BlockSpec((PACK_HEADS, ROWS, HEAD_DIM), lambda i: (i, 0, 0)),
        out_shape=jax.ShapeDtypeStruct((HEADS, ROWS, HEAD_DIM), BF16),
        name="pack_heads",
    )(fetch_ids, slot_of, queries, out_grad)


def attention_kernel(
    head_ref,
    x_ref,
    ids_ref,
    keys_ref,
    values_ref,
    rel_ref,
    y_ref,
    dk_out,
    dv_out,
    bias_out,
    ids_vmem,
    ids_smem,
    bias_ref,
    dsum_ref,
    dk_ref,
    dv_ref,
    sem,
):
    step = pl.program_id(0)
    head = head_ref[0]

    @pl.when(step == 0)
    def _():
        ids_vmem[...] = ids_ref[:, 0, :].astype(F32).astype(jnp.int32)
        copy = pltpu.make_async_copy(ids_vmem, ids_smem, sem)
        copy.start()
        row = rel_ref[pl.ds(head, 1), :]
        wide = jnp.concatenate([row, jnp.zeros((1, 256 - REL), F32)], axis=1)
        wide = jnp.broadcast_to(wide, (BLOCK, 256))
        rolled = pltpu.roll(wide, 256 - (BLOCK - 1), 1, stride=1, stride_axis=0)[:, :NBLEN]
        bias_ref[...] = jnp.concatenate([rolled, rolled], axis=1)
        dsum_ref[...] = jnp.zeros_like(dsum_ref)
        dk_ref[...] = jnp.zeros_like(dk_ref)
        dv_ref[...] = jnp.zeros_like(dv_ref)
        copy.wait()

    def one_source(s, carry):
        src = step * SRC_STEP + s
        dsum = jnp.zeros((BLOCK, NEIGH * NBLEN), F32)
        for c in range(CH_DEV):
            ids = [ids_smem[src, c * NEIGH + n] for n in range(NEIGH)]
            q = x_ref[s, c * BLOCK : (c + 1) * BLOCK]
            g = x_ref[s, HALF + c * BLOCK : HALF + (c + 1) * BLOCK]
            k = jnp.concatenate([keys_ref[0, i] for i in ids], axis=0)
            v = jnp.concatenate([values_ref[0, i] for i in ids], axis=0)
            scores = lax.dot_general(q, k, NT, preferred_element_type=F32)
            scores = scores * SCALE + bias_ref[...]
            dprobs = lax.dot_general(g, v, NT, preferred_element_type=F32)
            expo = jnp.exp(scores - jnp.max(scores, axis=-1, keepdims=True))
            probs = expo * (1.0 / jnp.sum(expo, axis=-1, keepdims=True))
            probs_low = probs.astype(BF16)
            inner = jnp.sum(probs * dprobs, axis=-1, keepdims=True)
            dscores = probs * (dprobs - inner)
            dscores_low = dscores.astype(BF16)
            dsum += dscores
            attended = jnp.dot(probs_low, v, preferred_element_type=F32)
            query_grad = jnp.dot(dscores_low, k, preferred_element_type=F32) * SCALE
            y_ref[s, c * BLOCK : (c + 1) * BLOCK] = attended.astype(BF16)
            y_ref[s, HALF + c * BLOCK : HALF + (c + 1) * BLOCK] = query_grad.astype(BF16)
            dk = lax.dot_general(dscores_low, q, TN, preferred_element_type=F32)
            dv = lax.dot_general(probs_low, g, TN, preferred_element_type=F32)
            for n in range(NEIGH):
                rows = slice(n * NBLEN, (n + 1) * NBLEN)
                dk_ref[ids[n]] += dk[rows]
                dv_ref[ids[n]] += dv[rows]
        dsum_ref[...] += dsum
        return carry

    lax.fori_loop(0, SRC_STEP, one_source, 0, unroll=2)

    @pl.when(step == pl.num_programs(0) - 1)
    def _():
        dk_out[0] = (dk_ref[...] * SCALE).astype(BF16)
        dv_out[0] = dv_ref[...].astype(BF16)
        folded = dsum_ref[:, :NBLEN] + dsum_ref[:, NBLEN:]
        wide = jnp.concatenate([folded, jnp.zeros((BLOCK, NBLEN), F32)], axis=1)
        group = sum(
            pltpu.roll(wide[t : t + 8], BLOCK - 8 - t, 1) if t < BLOCK - 8 else wide[t : t + 8]
            for t in range(0, BLOCK, 8)
        )
        total = sum(
            pltpu.roll(group[r : r + 1], 7 - r, 1) if r < 7 else group[r : r + 1] for r in range(8)
        )[:, :REL]
        here = lax.broadcasted_iota(jnp.int32, (HEADS, REL), 0) == head
        bias_out[...] = jnp.where(here, jnp.broadcast_to(total, (HEADS, REL)), 0.0)


def attention(head, recv, keys_pool, values_pool, rel_bias):
    pool = (1, POOL, NBLEN, HEAD_DIM)
    whole_pool = pl.BlockSpec(pool, lambda i, *_: (0, 0, 0, 0))
    return pl.pallas_call(
        attention_kernel,
        grid_spec=pltpu.PrefetchScalarGridSpec(
            num_scalar_prefetch=1,
            grid=(N_BLOCK // SRC_STEP,),
            in_specs=[
                pl.BlockSpec((SRC_STEP, DATA, HEAD_DIM), lambda i, *_: (i, 0, 0)),
                pl.BlockSpec((N_BLOCK, 16, HEAD_DIM), lambda i, *_: (0, DATA // 16, 0)),
                whole_pool,
                whole_pool,
                pl.BlockSpec((HEADS, REL), lambda i, *_: (0, 0)),
            ],
            out_specs=[
                pl.BlockSpec((SRC_STEP, DATA, HEAD_DIM), lambda i, *_: (i, 0, 0)),
                whole_pool,
                whole_pool,
                pl.BlockSpec((HEADS, REL), lambda i, *_: (0, 0)),
            ],
            scratch_shapes=[
                pltpu.VMEM((N_BLOCK, 128), jnp.int32),
                pltpu.SMEM((N_BLOCK, 128), jnp.int32),
                pltpu.VMEM((BLOCK, NEIGH * NBLEN), F32),
                pltpu.VMEM((BLOCK, NEIGH * NBLEN), F32),
                pltpu.VMEM((POOL, NBLEN, HEAD_DIM), F32),
                pltpu.VMEM((POOL, NBLEN, HEAD_DIM), F32),
                pltpu.SemaphoreType.DMA,
            ],
        ),
        out_shape=[
            jax.ShapeDtypeStruct((N_BLOCK, DATA, HEAD_DIM), BF16),
            jax.ShapeDtypeStruct(pool, BF16),
            jax.ShapeDtypeStruct(pool, BF16),
            jax.ShapeDtypeStruct((HEADS, REL), F32),
        ],
        compiler_params=pltpu.CompilerParams(vmem_limit_bytes=40 * 1024 * 1024),
        name="attention_both",
    )(head, recv, recv, keys_pool, values_pool, rel_bias)


def unpack_kernel(y_ref, att_ref, dq_ref):
    for h in range(PACK_HEADS):
        cols = slice(h * HEAD_DIM, (h + 1) * HEAD_DIM)
        for c in range(CH_DEV):
            att_ref[0, c, :, cols] = y_ref[h, c * BLOCK : (c + 1) * BLOCK]
            dq_ref[0, c, :, cols] = y_ref[h, HALF + c * BLOCK : HALF + (c + 1) * BLOCK]


def unpack(back):
    rows = pl.BlockSpec((1, CH_DEV, BLOCK, PACK_HEADS * HEAD_DIM), lambda i: (0, 0, 0, i))
    shape = jax.ShapeDtypeStruct((1, CH_DEV, BLOCK, HD), BF16)
    return pl.pallas_call(
        unpack_kernel,
        grid=(HEADS // PACK_HEADS,),
        in_specs=[pl.BlockSpec((PACK_HEADS, DATA, HEAD_DIM), lambda i: (i, 0, 0))],
        out_specs=[rows, rows],
        out_shape=[shape, shape],
        name="unpack_heads",
    )(back)


def sum_everywhere(part):
    for axis, size in (("dp", N_DP), ("block", N_BLOCK)):
        hop = 1
        while hop < size:
            part = part + lax.ppermute(part, axis, [(d, d ^ hop) for d in range(size)])
            hop *= 2
    return part


def on_device(queries, keys_pool, values_pool, rel_bias, out_grad, fetch_ids, slot_of):
    head = lax.axis_index("block").astype(jnp.int32).reshape(1)
    sent = pack(fetch_ids, slot_of, queries, out_grad)
    recv = lax.all_to_all(sent, "block", split_axis=0, concat_axis=0, tiled=True)
    y, key_grad, value_grad, bias_part = attention(head, recv, keys_pool, values_pool, rel_bias)
    back = lax.all_to_all(y, "block", split_axis=0, concat_axis=0, tiled=True)
    bias_grad = sum_everywhere(bias_part)
    attended, query_grad = unpack(back)
    return (attended, query_grad, key_grad, value_grad, bias_grad)


def solution(mesh):
    in_specs = (
        P("dp", "block", None, None),
        P("dp", None, None, "block"),
        P("dp", None, None, "block"),
        P(),
        P("dp", "block", None, None),
        P("dp", "block", None),
        P("dp", "block", None),
    )
    out_specs = (
        P("dp", "block", None, None),
        P("dp", "block", None, None),
        P("dp", None, None, "block"),
        P("dp", None, None, "block"),
        P(),
    )
    return jax.shard_map(
        on_device, mesh=mesh, in_specs=in_specs, out_specs=out_specs, check_vma=False
    )
```

time: 509 us -> 189 us (0.37)
  blocking collectives: 147 us -> 0 us
  local copies, waits for them, and re-layouts: 121 us -> 3.9 us
  waiting for transfers between devices: 154 us -> 108 us
  Pallas kernels: 0 us -> 43.5 us
  matrix products: 43.1 us -> 0 us
  other arithmetic: 15.1 us -> 0.66 us
  starting transfers between devices: 22.2 us -> 32.4 us
    psum x1 -> x0, blocking collectives: 105 us -> none  [on_device(): bias_grad = lax.psum(bias_terms, ('dp', 'block'))]
    all_to_all x4 -> x2, waiting for transfers between devices: 154 us -> 52.7 us  [the longest x1 52.7 us: on_device(): lax.all_to_all(sent, 'block', split_axis=0, concat_axis=0, tiled=True)]
    ppermute x0 -> x8, waiting for transfers between devices: none -> 54.9 us  [sum_everywhere(): part = part + lax.ppermute(part, axis, [(d, d ^ hop) for d in range(size)])]
    pallas_call x0 -> x3, Pallas kernels: none -> 43.5 us  [the longest x1 35.6 us: attention(): pl.pallas_call(attention_kernel, grid_spec=pltpu.PrefetchScalarGridSpec(n...]
    dot_general x12 -> x0, matrix products: 43.1 us -> none  [the longest x1 6.55 us: forward_backward(): jnp.einsum('cihd,cjhd->chij', grad_rows, value_rows, preferred_element_ty...]
    convert_element_type x6 -> x0, local copies, waits for them, and re-layouts: 42.7 us -> none  [the longest x2 20.7 us: on_device(): key_local.astype(jnp.bfloat16)]
    all_gather x1 -> x0, blocking collectives: 41.9 us -> none  [on_device(): lax.all_gather(fetch_ids, 'block', axis=1, tiled=True)]
    gather x6 -> x0, local copies, waits for them, and re-layouts: 25.8 us -> none  [the longest x2 9.54 us: on_device(): fetched_values[0][slots].reshape(CH_DEV, NEIGH * NBLEN, HEADS, HEAD_DIM)]
  transfers between devices with their start and end apart: 4 -> 10, of which waited for: 3 -> 9; matrix products, arithmetic and copies ran while one was open for 19% -> 0% of each run, Pallas kernels for 0% -> 0%
where the time goes in v1:
time: 189 us
  waiting for transfers between devices  108 us (57%)
  Pallas kernels  43.5 us (23%)
  starting transfers between devices  32.4 us (17%)
  local copies, waits for them, and re-layouts  3.9 us (2%)
    ppermute x8, waiting for transfers between devices, sum_everywhere(): part = part + lax.ppermute(part, axis, [(d, d ^ hop) for d in range(size)])  54.9 us
    all_to_all x1, waiting for transfers between devices, on_device(): lax.all_to_all(sent, 'block', split_axis=0, concat_axis=0, tiled=True)  52.7 us
    pallas_call x1, Pallas kernels, attention(): pl.pallas_call(attention_kernel, grid_spec=pltpu.PrefetchScalarGridSpec(n...  35.6 us
    ppermute x8, starting transfers between devices, sum_everywhere(): part = part + lax.ppermute(part, axis, [(d, d ^ hop) for d in range(size)])  14.7 us
    all_to_all x1, starting transfers between devices, on_device(): lax.all_to_all(sent, 'block', split_axis=0, concat_axis=0, tiled=True)  11.5 us
    all_to_all x1, starting transfers between devices, on_device(): back = lax.all_to_all(y, 'block', split_axis=0, concat_axis=0, tiled=True)  6.25 us
    pallas_call x1, Pallas kernels, unpack(): pl.pallas_call(unpack_kernel, grid=(HEADS // PACK_HEADS,), in_specs=[pl.B...  3.99 us
    pallas_call x1, Pallas kernels, pack(): pl.pallas_call(pack_kernel, grid=(HEADS // PACK_HEADS,), in_specs=[pl.Blo...  3.93 us
  transfers between devices with their start and end apart: 10, of which 9 were waited for; matrix products, arithmetic and copies ran while one was open for 0% of the time, Pallas kernels for 0%

profile of v1, /device:TPU:16, one launch (start us, length us, event | category | flops | bytes accessed | tf_op | source)
XLA Modules:
  0.0 188.7 jit_solution(14826621116760586142)
XLA Ops:
  0.6 3.9 %pack_heads.1 = bf16[32,272,128]{2,1,0:T(8,128)(2,1)} custom-call(s32[1,1,3]{2,1,0:T(1,128)} %fetch_ref.1, s32[1,2,2]{2,1,0:T(2,128)} %slot_ref.1, bf16[1,2,64,4096]{3,2,1,0:T(8,128)(2,1)} %q_ref.1, bf16[1,2,64,4096]{3,2,1,0:T(8,128)(2,1)} %g_ref.1), custom_call_target="tpu_custom_call" | custom-call | tf_op jit(solution)/shard_map/pack_heads/pallas_call | solution.py:53
  4.6 0.0 copy-start.1
  4.6 0.0 copy-start.3
  4.6 11.5 %all-to-all-start = ((bf16[32,272,128]{2,1,0:T(8,128)(2,1)}), bf16[32,272,128]{2,1,0:T(8,128)(2,1)S(1)}, u32[]{:S(2)}, u32[]{:S(2)}) async-start(bf16[32,272,128]{2,1,0:T(8,128)(2,1)} %pack_heads.1), calls=%async_computation | async-start | bytes 4456448 | tf_op jit(solution)/shard_map/all_to_all | solution.py:231
  16.0 52.7 %all-to-all-done.x_ref.ids_ref = bf16[32,272,128]{2,1,0:T(8,128)(2,1)S(1)} async-done(((bf16[32,272,128]{2,1,0:T(8,128)(2,1)}), bf16[32,272,128]{2,1,0:T(8,128)(2,1)S(1)}, u32[]{:S(2)}, u32[]{:S(2)}) %all-to-all-start) | async-done | bytes 2228256 | tf_op jit(solution)/shard_map/all_to_all | solution.py:231
  68.8 0.0 copy-done.1
  68.8 0.0 copy-done.3
  68.8 1.2 copy-done.2
  70.0 35.6 %attention_both.1 = (bf16[32,256,128]{2,1,0:T(8,128)(2,1)S(1)}, bf16[1,32,128,128]{3,2,1,0:T(8,128)(2,1)}, bf16[1,32,128,128]{3,2,1,0:T(8,128)(2,1)}, f32[32,192]{1,0:T(8,128)S(1)}) custom-call(s32[1]{0:T(128)} %bitcast.head_ref, bf16[32,272,128]{2,1,0:T(8,128)(2,1)S(1)} %all-to-all-done.x_ref.ids_ref, bf16[32,272,128]{2,1,0:T(8,128)(2,1)S(1)} %all-to-all-done.x_ref.ids_ref, ...), custom_call_target="tpu_custom_call" | custom-call | tf_op jit(solution)/shard_map/attention_both/pallas_call | solution.py:159
  105.6 0.0 copy-start
  105.6 1.3 copy-done
  106.9 6.2 %all-to-all-start.1 = ((bf16[32,256,128]{2,1,0:T(8,128)(2,1)}), bf16[32,256,128]{2,1,0:T(8,128)(2,1)S(1)}, u32[]{:S(2)}, u32[]{:S(2)}) async-start(bf16[32,256,128]{2,1,0:T(8,128)(2,1)} %copy-done), calls=%async_computation.1 | async-start | bytes 4194304 | tf_op jit(solution)/shard_map/all_to_all | solution.py:233
  113.2 0.1 collective-permute-start
  113.3 1.2 collective-permute-done
  114.5 1.3 collective-permute-start.1
  115.7 2.6 %collective-permute-done.1 = f32[32,192]{1,0:T(8,128)S(1)} collective-permute-done((f32[32,192]{1,0:T(8,128)S(1)}, f32[32,192]{1,0:T(8,128)S(1)}, u32[]{:S(2)}, u32[]{:S(2)}) %collective-permute-start.1) | collective-permute-done | bytes 24608 | tf_op jit(solution)/shard_map/ppermute | solution.py:223
  118.4 0.3 collective-permute-start.2
  118.7 5.1 %collective-permute-done.2 = f32[32,192]{1,0:T(8,128)S(1)} collective-permute-done((f32[32,192]{1,0:T(8,128)S(1)}, f32[32,192]{1,0:T(8,128)S(1)}, u32[]{:S(2)}, u32[]{:S(2)}) %collective-permute-start.2) | collective-permute-done | bytes 24608 | tf_op jit(solution)/shard_map/ppermute | solution.py:223
  123.8 1.8 collective-permute-start.3
  125.6 34.9 %collective-permute-done.3 = f32[32,192]{1,0:T(8,128)S(1)} collective-permute-done((f32[32,192]{1,0:T(8,128)S(1)}, f32[32,192]{1,0:T(8,128)S(1)}, u32[]{:S(2)}, u32[]{:S(2)}) %collective-permute-start.3) | collective-permute-done | bytes 24608 | tf_op jit(solution)/shard_map/ppermute | solution.py:223
  160.5 2.3 %collective-permute-start.4 = (f32[32,192]{1,0:T(8,128)S(1)}, f32[32,192]{1,0:T(8,128)S(1)}, u32[]{:S(2)}, u32[]{:S(2)}) collective-permute-start(f32[32,192]{1,0:T(8,128)S(1)} %add.27), channel_id=1, source_target_pairs={{0,2},{1,3},{2,0},{3,1},{4,6},{5,7},{6,4},{7,5},{8,10},{9,11},{10,... | collective-permute-start | bytes 73736 | tf_op jit(solution)/shard_map/ppermute | solution.py:223
  162.8 2.5 %collective-permute-done.4 = f32[32,192]{1,0:T(8,128)S(1)} collective-permute-done((f32[32,192]{1,0:T(8,128)S(1)}, f32[32,192]{1,0:T(8,128)S(1)}, u32[]{:S(2)}, u32[]{:S(2)}) %collective-permute-start.4) | collective-permute-done | bytes 24608 | tf_op jit(solution)/shard_map/ppermute | solution.py:223
  165.3 4.7 %collective-permute-start.5 = (f32[32,192]{1,0:T(8,128)S(1)}, f32[32,192]{1,0:T(8,128)S(1)}, u32[]{:S(2)}, u32[]{:S(2)}) collective-permute-start(f32[32,192]{1,0:T(8,128)S(1)} %add.28), channel_id=1, source_target_pairs={{0,4},{1,5},{2,6},{3,7},{4,0},{5,1},{6,2},{7,3},{8,12},{9,13},{10,... | collective-permute-start | bytes 73736 | tf_op jit(solution)/shard_map/ppermute | solution.py:223
  170.0 3.2 %collective-permute-done.5 = f32[32,192]{1,0:T(8,128)S(1)} collective-permute-done((f32[32,192]{1,0:T(8,128)S(1)}, f32[32,192]{1,0:T(8,128)S(1)}, u32[]{:S(2)}, u32[]{:S(2)}) %collective-permute-start.5) | collective-permute-done | bytes 24608 | tf_op jit(solution)/shard_map/ppermute | solution.py:223
  173.2 1.4 collective-permute-start.6
  174.7 2.7 %collective-permute-done.6 = f32[32,192]{1,0:T(8,128)S(1)} collective-permute-done((f32[32,192]{1,0:T(8,128)S(1)}, f32[32,192]{1,0:T(8,128)S(1)}, u32[]{:S(2)}, u32[]{:S(2)}) %collective-permute-start.6) | collective-permute-done | bytes 24608 | tf_op jit(solution)/shard_map/ppermute | solution.py:223
  177.4 2.7 %collective-permute-start.7 = (f32[32,192]{1,0:T(8,128)S(1)}, f32[32,192]{1,0:T(8,128)S(1)}, u32[]{:S(2)}, u32[]{:S(2)}) collective-permute-start(f32[32,192]{1,0:T(8,128)S(1)} %add.30), channel_id=1, source_target_pairs={{0,16},{1,17},{2,18},{3,19},{4,20},{5,21},{6,22},{7,23},{8,24},{9,... | collective-permute-start | bytes 73736 | tf_op jit(solution)/shard_map/ppermute | solution.py:223
  180.1 2.7 %collective-permute-done.7 = f32[32,192]{1,0:T(8,128)S(1)} collective-permute-done((f32[32,192]{1,0:T(8,128)S(1)}, f32[32,192]{1,0:T(8,128)S(1)}, u32[]{:S(2)}, u32[]{:S(2)}) %collective-permute-start.7) | collective-permute-done | bytes 24608 | tf_op jit(solution)/shard_map/ppermute | solution.py:223
  182.8 0.6 add.31
  183.4 0.0 all-to-all-done.1.y_ref
  183.4 1.3 copy-done.4
  184.7 4.0 %unpack_heads.1 = (bf16[1,2,64,4096]{3,2,1,0:T(8,128)(2,1)}, bf16[1,2,64,4096]{3,2,1,0:T(8,128)(2,1)}) custom-call(bf16[32,256,128]{2,1,0:T(8,128)(2,1)} %copy-done.4), custom_call_target="tpu_custom_call" | custom-call | tf_op jit(solution)/shard_map/unpack_heads/pallas_call | solution.py:209
  (9 shorter events, 0.0 us)
Async XLA Ops:
  4.6 64.2 %copy-start.1 = (bf16[1,32,128,128]{3,2,1,0:T(8,128)(2,1)S(1)}, bf16[1,32,128,128]{3,2,1,0:T(8,128)(2,1)}, u32[]{:S(2)}) copy-start(bf16[1,32,128,128]{3,2,1,0:T(8,128)(2,1)} %keys_ref.1) | copy-start | bytes 3145732
  4.6 64.2 %copy-start.3 = (f32[32,192]{1,0:T(8,128)S(1)}, f32[32,192]{1,0:T(8,128)}, u32[]{:S(2)}) copy-start(f32[32,192]{1,0:T(8,128)} %rel_ref.1) | copy-start | bytes 73732
  4.6 64.2 %all-to-all-start = ((bf16[32,272,128]{2,1,0:T(8,128)(2,1)}), bf16[32,272,128]{2,1,0:T(8,128)(2,1)S(1)}, u32[]{:S(2)}, u32[]{:S(2)}) async-start(bf16[32,272,128]{2,1,0:T(8,128)(2,1)} %pack_heads.1), calls=%async_computation | async-start | bytes 4456448 | tf_op jit(solution)/shard_map/all_to_all | solution.py:231
  68.8 1.2 copy-start.2
  105.6 1.3 copy-start
  106.9 76.5 %all-to-all-start.1 = ((bf16[32,256,128]{2,1,0:T(8,128)(2,1)}), bf16[32,256,128]{2,1,0:T(8,128)(2,1)S(1)}, u32[]{:S(2)}, u32[]{:S(2)}) async-start(bf16[32,256,128]{2,1,0:T(8,128)(2,1)} %copy-done), calls=%async_computation.1 | async-start | bytes 4194304 | tf_op jit(solution)/shard_map/all_to_all | solution.py:233
  113.2 1.3 collective-permute-start
  114.5 3.9 %collective-permute-start.1 = (f32[32,192]{1,0:T(8,128)S(1)}, f32[32,192]{1,0:T(8,128)S(1)}, u32[]{:S(2)}, u32[]{:S(2)}) collective-permute-start(f32[32,192]{1,0:T(8,128)S(1)} %add.24), channel_id=1, source_target_pairs={{0,64},{32,96},{64,0},{96,32},{128,192},{160,224},{192,128},{224,1... | collective-permute-start | bytes 73736 | tf_op jit(solution)/shard_map/ppermute | solution.py:223
  118.4 5.4 %collective-permute-start.2 = (f32[32,192]{1,0:T(8,128)S(1)}, f32[32,192]{1,0:T(8,128)S(1)}, u32[]{:S(2)}, u32[]{:S(2)}) collective-permute-start(f32[32,192]{1,0:T(8,128)S(1)} %add.25), channel_id=1, source_target_pairs={{0,128},{32,160},{64,192},{96,224},{128,0},{160,32},{192,64},{224,... | collective-permute-start | bytes 73736 | tf_op jit(solution)/shard_map/ppermute | solution.py:223
  123.8 36.7 %collective-permute-start.3 = (f32[32,192]{1,0:T(8,128)S(1)}, f32[32,192]{1,0:T(8,128)S(1)}, u32[]{:S(2)}, u32[]{:S(2)}) collective-permute-start(f32[32,192]{1,0:T(8,128)S(1)} %add.26), channel_id=1, source_target_pairs={{0,1},{1,0},{2,3},{3,2},{4,5},{5,4},{6,7},{7,6},{8,9},{9,8},{10,11... | collective-permute-start | bytes 73736 | tf_op jit(solution)/shard_map/ppermute | solution.py:223
  160.5 4.8 %collective-permute-start.4 = (f32[32,192]{1,0:T(8,128)S(1)}, f32[32,192]{1,0:T(8,128)S(1)}, u32[]{:S(2)}, u32[]{:S(2)}) collective-permute-start(f32[32,192]{1,0:T(8,128)S(1)} %add.27), channel_id=1, source_target_pairs={{0,2},{1,3},{2,0},{3,1},{4,6},{5,7},{6,4},{7,5},{8,10},{9,11},{10,... | collective-permute-start | bytes 73736 | tf_op jit(solution)/shard_map/ppermute | solution.py:223
  165.3 7.9 %collective-permute-start.5 = (f32[32,192]{1,0:T(8,128)S(1)}, f32[32,192]{1,0:T(8,128)S(1)}, u32[]{:S(2)}, u32[]{:S(2)}) collective-permute-start(f32[32,192]{1,0:T(8,128)S(1)} %add.28), channel_id=1, source_target_pairs={{0,4},{1,5},{2,6},{3,7},{4,0},{5,1},{6,2},{7,3},{8,12},{9,13},{10,... | collective-permute-start | bytes 73736 | tf_op jit(solution)/shard_map/ppermute | solution.py:223
  173.2 4.1 %collective-permute-start.6 = (f32[32,192]{1,0:T(8,128)S(1)}, f32[32,192]{1,0:T(8,128)S(1)}, u32[]{:S(2)}, u32[]{:S(2)}) collective-permute-start(f32[32,192]{1,0:T(8,128)S(1)} %add.29), channel_id=1, source_target_pairs={{0,8},{1,9},{2,10},{3,11},{4,12},{5,13},{6,14},{7,15},{8,0},{9,1},... | collective-permute-start | bytes 73736 | tf_op jit(solution)/shard_map/ppermute | solution.py:223
  177.4 5.4 %collective-permute-start.7 = (f32[32,192]{1,0:T(8,128)S(1)}, f32[32,192]{1,0:T(8,128)S(1)}, u32[]{:S(2)}, u32[]{:S(2)}) collective-permute-start(f32[32,192]{1,0:T(8,128)S(1)} %add.30), channel_id=1, source_target_pairs={{0,16},{1,17},{2,18},{3,19},{4,20},{5,21},{6,22},{7,23},{8,24},{9,... | collective-permute-start | bytes 73736 | tf_op jit(solution)/shard_map/ppermute | solution.py:223
  183.4 1.3 copy-start.4

commit v2 on v1

v2 whole, which is shorter than its diff:
```python
import functools
import math

import jax
import jax.numpy as jnp
from jax import lax
from jax.experimental import pallas as pl
from jax.experimental.pallas import tpu as pltpu
from jax.sharding import PartitionSpec as P

HEADS = 32
HEAD_DIM = 128
BLOCK = 64
NBLEN = 128
NEIGH = 2
CH_DEV = 2
POOL = 32
HD = HEADS * HEAD_DIM
REL = 192
N_BLOCK = 32
N_DP = 8
HALF = CH_DEV * BLOCK
DATA = 2 * HALF
ROWS = DATA + 16
PACK_HEADS = 8
SRC_STEP = 4
SCALE = 1.0 / math.sqrt(HEAD_DIM)

NT = (((1,), (1,)), ((), ()))
TN = (((0,), (0,)), ((), ()))
F32 = jnp.float32
BF16 = jnp.bfloat16


def pack_kernel(fetch_ref, slot_ref, q_ref, g_ref, out_ref):
    lane = lax.broadcasted_iota(jnp.int32, (16, 128), 1)
    ids = jnp.zeros((16, 128), jnp.int32)
    for c in range(CH_DEV):
        for n in range(NEIGH):
            enc = fetch_ref[0, 0, slot_ref[0, c, n]]
            ids = jnp.where(lane == c * NEIGH + n, enc, ids)
    ids = ids.astype(F32).astype(BF16)
    for h in range(PACK_HEADS):
        cols = slice(h * HEAD_DIM, (h + 1) * HEAD_DIM)
        for c in range(CH_DEV):
            out_ref[h, c * BLOCK : (c + 1) * BLOCK] = q_ref[0, c, :, cols]
            out_ref[h, HALF + c * BLOCK : HALF + (c + 1) * BLOCK] = g_ref[0, c, :, cols]
        out_ref[h, DATA:] = ids


def pack(fetch_ids, slot_of, queries, out_grad):
    rows = pl.BlockSpec((1, CH_DEV, BLOCK, PACK_HEADS * HEAD_DIM), lambda i: (0, 0, 0, i))
    return pl.pallas_call(
        pack_kernel,
        grid=(HEADS // PACK_HEADS,),
        in_specs=[
            pl.BlockSpec(memory_space=pltpu.SMEM),
            pl.BlockSpec(memory_space=pltpu.SMEM),
            rows,
            rows,
        ],
        out_specs=pl.BlockSpec((PACK_HEADS, ROWS, HEAD_DIM), lambda i: (i, 0, 0)),
        out_shape=jax.ShapeDtypeStruct((HEADS, ROWS, HEAD_DIM), BF16),
        name="pack_heads",
    )(fetch_ids, slot_of, queries, out_grad)


def build_bias(rel_ref, head, bias_ref):
    row = rel_ref[pl.ds(head, 1), :]
    wide = jnp.concatenate([row, jnp.zeros((1, 256 - REL), F32)], axis=1)
    wide = jnp.broadcast_to(wide, (BLOCK, 256))
    rolled = pltpu.roll(wide, 256 - (BLOCK - 1), 1, stride=1, stride_axis=0)[:, :NBLEN]
    bias_ref[...] = jnp.concatenate([rolled, rolled], axis=1)


def fold_bias(dscore_sum):
    folded = dscore_sum[:, :NBLEN] + dscore_sum[:, NBLEN:]
    wide = jnp.concatenate([folded, jnp.zeros((BLOCK, NBLEN), F32)], axis=1)
    group = sum(
        pltpu.roll(wide[t : t + 8], BLOCK - 8 - t, 1) if t < BLOCK - 8 else wide[t : t + 8]
        for t in range(0, BLOCK, 8)
    )
    return sum(
        pltpu.roll(group[r : r + 1], 7 - r, 1) if r < 7 else group[r : r + 1] for r in range(8)
    )


def read_ids(ids_ref, ids_vmem, ids_smem, sem):
    ids_vmem[...] = ids_ref[:, 0, :].astype(F32).astype(jnp.int32)
    copy = pltpu.make_async_copy(ids_vmem, ids_smem, sem)
    copy.start()
    return copy


BLOCKS_STEP = [(s, c) for s in range(SRC_STEP) for c in range(CH_DEV)]


def block_rows(c):
    return slice(c * BLOCK, (c + 1) * BLOCK)


def softmax_parts(step, ids_smem, bias_ref, q_ref, keys_ref, values_ref):
    bias = bias_ref[...]
    ids = [
        [ids_smem[step * SRC_STEP + s, c * NEIGH + n] for n in range(NEIGH)]
        for s, c in BLOCKS_STEP
    ]
    q = [q_ref[s, block_rows(c)] for s, c in BLOCKS_STEP]
    k = [jnp.concatenate([keys_ref[0, i] for i in pair], axis=0) for pair in ids]
    v = [jnp.concatenate([values_ref[0, i] for i in pair], axis=0) for pair in ids]
    scores = [lax.dot_general(a, b, NT, preferred_element_type=F32) for a, b in zip(q, k)]
    scores = [a * SCALE + bias for a in scores]
    tops = [jnp.max(a, axis=-1, keepdims=True) for a in scores]
    expo = [jnp.exp(a - b) for a, b in zip(scores, tops)]
    inverse = [1.0 / jnp.sum(a, axis=-1, keepdims=True) for a in expo]
    probs = [a * b for a, b in zip(expo, inverse)]
    return ids, q, k, v, probs


def forward_kernel(
    head_ref, q_ref, ids_ref, keys_ref, values_ref, rel_ref, y_ref, ids_vmem, ids_smem, bias_ref, sem
):
    step = pl.program_id(0)

    @pl.when(step == 0)
    def _():
        copy = read_ids(ids_ref, ids_vmem, ids_smem, sem)
        build_bias(rel_ref, head_ref[0], bias_ref)
        copy.wait()

    ids, q, k, v, probs = softmax_parts(step, ids_smem, bias_ref, q_ref, keys_ref, values_ref)
    for i, (s, c) in enumerate(BLOCKS_STEP):
        attended = jnp.dot(probs[i].astype(BF16), v[i], preferred_element_type=F32)
        y_ref[s, block_rows(c)] = attended.astype(BF16)


def backward_kernel(
    head_ref,
    q_ref,
    g_ref,
    ids_ref,
    keys_ref,
    values_ref,
    rel_ref,
    y_ref,
    dk_out,
    dv_out,
    bias_out,
    ids_vmem,
    ids_smem,
    bias_ref,
    dsum_ref,
    dk_ref,
    dv_ref,
    sem,
):
    step = pl.program_id(0)

    @pl.when(step == 0)
    def _():
        copy = read_ids(ids_ref, ids_vmem, ids_smem, sem)
        build_bias(rel_ref, head_ref[0], bias_ref)
        dsum_ref[...] = jnp.zeros_like(dsum_ref)
        dk_ref[...] = jnp.zeros_like(dk_ref)
        dv_ref[...] = jnp.zeros_like(dv_ref)
        copy.wait()

    ids, q, k, v, probs = softmax_parts(step, ids_smem, bias_ref, q_ref, keys_ref, values_ref)
    g = [g_ref[s, block_rows(c)] for s, c in BLOCKS_STEP]
    dprobs = [lax.dot_general(a, b, NT, preferred_element_type=F32) for a, b in zip(g, v)]
    probs_low = [a.astype(BF16) for a in probs]
    inner = [jnp.sum(a * b, axis=-1, keepdims=True) for a, b in zip(probs, dprobs)]
    dscores = [a * (b - c) for a, b, c in zip(probs, dprobs, inner)]
    dscores_low = [a.astype(BF16) for a in dscores]
    dsum_ref[...] += sum(dscores)
    for i, (s, c) in enumerate(BLOCKS_STEP):
        query_grad = jnp.dot(dscores_low[i], k[i], preferred_element_type=F32) * SCALE
        y_ref[s, block_rows(c)] = query_grad.astype(BF16)
    dk = [lax.dot_general(a, b, TN, preferred_element_type=F32) for a, b in zip(dscores_low, q)]
    dv = [lax.dot_general(a, b, TN, preferred_element_type=F32) for a, b in zip(probs_low, g)]
    for i in range(len(BLOCKS_STEP)):
        for n in range(NEIGH):
            rows = slice(n * NBLEN, (n + 1) * NBLEN)
            dk_ref[ids[i][n]] += dk[i][rows]
            dv_ref[ids[i][n]] += dv[i][rows]

    @pl.when(step == pl.num_programs(0) - 1)
    def _():
        dk_out[0] = (dk_ref[...] * SCALE).astype(BF16)
        dv_out[0] = dv_ref[...].astype(BF16)
        bias_out[...] = fold_bias(dsum_ref[...])


POOL_SHAPE = (1, POOL, NBLEN, HEAD_DIM)
POOL_SPEC = pl.BlockSpec(POOL_SHAPE, lambda i, *_: (0, 0, 0, 0))
REL_SPEC = pl.BlockSpec((HEADS, REL), lambda i, *_: (0, 0))
IDS_SPEC = pl.BlockSpec((N_BLOCK, 16, HEAD_DIM), lambda i, *_: (0, DATA // 16, 0))
Q_SPEC = pl.BlockSpec((SRC_STEP, HALF, HEAD_DIM), lambda i, *_: (i, 0, 0))
G_SPEC = pl.BlockSpec((SRC_STEP, HALF, HEAD_DIM), lambda i, *_: (i, 1, 0))
BIAS_SHAPE = (BLOCK, NEIGH * NBLEN)
IDS_SCRATCH = [pltpu.VMEM((N_BLOCK, 128), jnp.int32), pltpu.SMEM((N_BLOCK, 128), jnp.int32)]


def forward(head, recv, keys_pool, values_pool, rel_bias):
    return pl.pallas_call(
        forward_kernel,
        grid_spec=pltpu.PrefetchScalarGridSpec(
            num_scalar_prefetch=1,
            grid=(N_BLOCK // SRC_STEP,),
            in_specs=[Q_SPEC, IDS_SPEC, POOL_SPEC, POOL_SPEC, REL_SPEC],
            out_specs=Q_SPEC,
            scratch_shapes=[*IDS_SCRATCH, pltpu.VMEM(BIAS_SHAPE, F32), pltpu.SemaphoreType.DMA],
        ),
        out_shape=jax.ShapeDtypeStruct((N_BLOCK, HALF, HEAD_DIM), BF16),
        compiler_params=pltpu.CompilerParams(vmem_limit_bytes=24 * 1024 * 1024),
        cost_estimate=pl.CostEstimate(flops=10**9, bytes_accessed=4 * 10**6, transcendentals=10**6),
        name="attention_forward",
    )(head, recv, recv, keys_pool, values_pool, rel_bias)


def backward(head, recv, keys_pool, values_pool, rel_bias):
    return pl.pallas_call(
        backward_kernel,
        grid_spec=pltpu.PrefetchScalarGridSpec(
            num_scalar_prefetch=1,
            grid=(N_BLOCK // SRC_STEP,),
            in_specs=[Q_SPEC, G_SPEC, IDS_SPEC, POOL_SPEC, POOL_SPEC, REL_SPEC],
            out_specs=[
                Q_SPEC,
                POOL_SPEC,
                POOL_SPEC,
                pl.BlockSpec((1, 256), lambda i, *_: (0, 0)),
            ],
            scratch_shapes=[
                *IDS_SCRATCH,
                pltpu.VMEM(BIAS_SHAPE, F32),
                pltpu.VMEM(BIAS_SHAPE, F32),
                pltpu.VMEM((POOL, NBLEN, HEAD_DIM), F32),
                pltpu.VMEM((POOL, NBLEN, HEAD_DIM), F32),
                pltpu.SemaphoreType.DMA,
            ],
        ),
        out_shape=[
            jax.ShapeDtypeStruct((N_BLOCK, HALF + 16, HEAD_DIM), BF16),
            jax.ShapeDtypeStruct(POOL_SHAPE, BF16),
            jax.ShapeDtypeStruct(POOL_SHAPE, BF16),
            jax.ShapeDtypeStruct((1, 256), F32),
        ],
        compiler_params=pltpu.CompilerParams(vmem_limit_bytes=36 * 1024 * 1024),
        cost_estimate=pl.CostEstimate(flops=3 * 10**9, bytes_accessed=9 * 10**6, transcendentals=10**6),
        name="attention_backward",
    )(head, recv, recv, recv, keys_pool, values_pool, rel_bias)


def add_row_kernel(row_ref, _, y_ref):
    row = row_ref[...]
    high = row.astype(BF16)
    rest = row - high.astype(F32)
    middle = rest.astype(BF16)
    low = (rest - middle.astype(F32)).astype(BF16)
    lines = [part.astype(F32)[:, c : c + 128] for part in (high, middle, low) for c in (0, 128)]
    block = jnp.concatenate([*lines, jnp.zeros((10, 128), F32)], axis=0).astype(BF16)
    y_ref[...] = jnp.broadcast_to(block[None], y_ref.shape)


def add_row(row, y):
    return pl.pallas_call(
        add_row_kernel,
        grid=(1,),
        in_specs=[
            pl.BlockSpec((1, 256), lambda i: (0, 0)),
            pl.BlockSpec(memory_space=pl.ANY),
        ],
        out_specs=pl.BlockSpec((N_BLOCK, 16, HEAD_DIM), lambda i: (0, HALF // 16, 0)),
        out_shape=jax.ShapeDtypeStruct(y.shape, BF16),
        input_output_aliases={1: 0},
        name="add_bias_row",
    )(row, y)


def unpack_kernel(y_ref, out_ref):
    for h in range(PACK_HEADS):
        cols = slice(h * HEAD_DIM, (h + 1) * HEAD_DIM)
        for c in range(CH_DEV):
            out_ref[0, c, :, cols] = y_ref[h, block_rows(c)]


def unpack_bias_kernel(y_ref, out_ref, bias_ref):
    unpack_kernel(y_ref, out_ref)
    lines = y_ref[:, HALF:, :].astype(F32)
    part = [lines[:, r, :] for r in range(6)]
    left = (part[0] + part[2]) + part[4]
    right = (part[1] + part[3]) + part[5]
    bias_ref[...] = jnp.concatenate([left, right], axis=1)[:, :REL]


def unpack(back):
    rows = pl.BlockSpec((1, CH_DEV, BLOCK, PACK_HEADS * HEAD_DIM), lambda i: (0, 0, 0, i))
    shape = jax.ShapeDtypeStruct((1, CH_DEV, BLOCK, HD), BF16)
    with_bias = back.shape[1] > HALF
    out = pl.pallas_call(
        unpack_bias_kernel if with_bias else unpack_kernel,
        grid=(HEADS // PACK_HEADS,),
        in_specs=[pl.BlockSpec((PACK_HEADS, back.shape[1], HEAD_DIM), lambda i: (i, 0, 0))],
        out_specs=[rows] + [pl.BlockSpec((PACK_HEADS, REL), lambda i: (i, 0))] * with_bias,
        out_shape=[shape] + [jax.ShapeDtypeStruct((HEADS, REL), F32)] * with_bias,
        name="unpack_heads",
    )(back)
    return out


def sum_groups(part):
    for hop in (1, 2, 4):
        part = part + lax.ppermute(part, "dp", [(d, d ^ hop) for d in range(N_DP)])
    return part


def all_to_all(parts):
    return lax.all_to_all(parts, "block", split_axis=0, concat_axis=0, tiled=True)


def on_device(queries, keys_pool, values_pool, rel_bias, out_grad, fetch_ids, slot_of):
    head = lax.axis_index("block").astype(jnp.int32).reshape(1)
    recv = all_to_all(pack(fetch_ids, slot_of, queries, out_grad))
    y = forward(head, recv, keys_pool, values_pool, rel_bias)
    back_y = all_to_all(y)
    recv, _ = lax.optimization_barrier((recv, y))
    dq, key_grad, value_grad, bias_part = backward(head, recv, keys_pool, values_pool, rel_bias)
    back_dq = all_to_all(add_row(sum_groups(bias_part), dq))
    (attended,) = unpack(back_y)
    query_grad, bias_grad = unpack(back_dq)
    return (attended, query_grad, key_grad, value_grad, bias_grad)


def solution(mesh):
    in_specs = (
        P("dp", "block", None, None),
        P("dp", None, None, "block"),
        P("dp", None, None, "block"),
        P(),
        P("dp", "block", None, None),
        P("dp", "block", None),
        P("dp", "block", None),
    )
    out_specs = (
        P("dp", "block", None, None),
        P("dp", "block", None, None),
        P("dp", None, None, "block"),
        P("dp", None, None, "block"),
        P(),
    )
    return jax.shard_map(
        on_device, mesh=mesh, in_specs=in_specs, out_specs=out_specs, check_vma=False
    )
```

time: 189 us -> 155 us (0.82)
  waiting for transfers between devices: 108 us -> 89.8 us
  Pallas kernels: 43.5 us -> 31.5 us
  starting transfers between devices: 32.4 us -> 27.1 us
    ppermute x8 -> x3, waiting for transfers between devices: 54.9 us -> 8.15 us  [sum_groups(): part = part + lax.ppermute(part, 'dp', [(d, d ^ hop) for d in range(N_DP)])]
    all_to_all x2 -> x3, waiting for transfers between devices: 52.7 us -> 81.6 us  [all_to_all(): lax.all_to_all(parts, 'block', split_axis=0, concat_axis=0, tiled=True)]
    ppermute x8 -> x3, starting transfers between devices: 14.7 us -> 1.63 us  [sum_groups(): part = part + lax.ppermute(part, 'dp', [(d, d ^ hop) for d in range(N_DP)])]
    pallas_call x2 -> x5, Pallas kernels: 39.6 us -> 27.6 us  [the longest x1 12.3 us: backward(): pl.pallas_call(backward_kernel, grid_spec=pltpu.PrefetchScalarGridSpec(nu...]
    all_to_all x2 -> x3, starting transfers between devices: 17.7 us -> 25.4 us  [all_to_all(): lax.all_to_all(parts, 'block', split_axis=0, concat_axis=0, tiled=True)]
    unnamed x10 -> x12, local copies, waits for them, and re-layouts: 3.9 us -> 4.5 us
  transfers between devices with their start and end apart: 10 -> 6, of which waited for: 9 -> 6; matrix products, arithmetic and copies ran while one was open for 0% -> 0% of each run, Pallas kernels for 0% -> 11%
where the time goes in v2:
time: 155 us; the launch traced here: 154 us
  waiting for transfers between devices  89.8 us (58%)
  Pallas kernels  31.5 us (20%)
  starting transfers between devices  27.1 us (17%)
  local copies, waits for them, and re-layouts  4.5 us (3%)
    all_to_all x3, waiting for transfers between devices, all_to_all(): lax.all_to_all(parts, 'block', split_axis=0, concat_axis=0, tiled=True)  81.6 us
    all_to_all x3, starting transfers between devices, all_to_all(): lax.all_to_all(parts, 'block', split_axis=0, concat_axis=0, tiled=True)  25.4 us
    pallas_call x1, Pallas kernels, backward(): pl.pallas_call(backward_kernel, grid_spec=pltpu.PrefetchScalarGridSpec(nu...  12.3 us
    ppermute x3, waiting for transfers between devices, sum_groups(): part = part + lax.ppermute(part, 'dp', [(d, d ^ hop) for d in range(N_DP)])  8.15 us
    pallas_call x2, Pallas kernels, unpack(): pl.pallas_call(unpack_bias_kernel if with_bias else unpack_kernel, grid=(...  6.96 us
    pallas_call x1, Pallas kernels, forward(): pl.pallas_call(forward_kernel, grid_spec=pltpu.PrefetchScalarGridSpec(num...  6.88 us
    unnamed x12, local copies, waits for them, and re-layouts  4.5 us
    pallas_call x1, Pallas kernels, pack(): pl.pallas_call(pack_kernel, grid=(HEADS // PACK_HEADS,), in_specs=[pl.Blo...  3.95 us
  transfers between devices with their start and end apart: 6, of which 6 were waited for; matrix products, arithmetic and copies ran while one was open for 0% of the time, Pallas kernels for 11%

profile of v2, /device:TPU:16, one launch (start us, length us, event | category | flops | bytes accessed | tf_op | source)
XLA Modules:
  0.0 154.1 jit_solution(13797057251255774847)
XLA Ops:
  0.6 3.9 %pack_heads.1 = bf16[32,272,128]{2,1,0:T(8,128)(2,1)} custom-call(s32[1,1,3]{2,1,0:T(1,128)} %fetch_ref.1, s32[1,2,2]{2,1,0:T(2,128)} %slot_ref.1, bf16[1,2,64,4096]{3,2,1,0:T(8,128)(2,1)} %q_ref.1, bf16[1,2,64,4096]{3,2,1,0:T(8,128)(2,1)} %g_ref.1), custom_call_target="tpu_custom_call" | custom-call | tf_op jit(solution)/shard_map/pack_heads/pallas_call | solution.py:53
  4.6 0.0 copy-start.1
  4.6 0.0 copy-start.4
  4.6 11.5 %all-to-all-start = ((bf16[32,272,128]{2,1,0:T(8,128)(2,1)}), bf16[32,272,128]{2,1,0:T(8,128)(2,1)S(1)}, u32[]{:S(2)}, u32[]{:S(2)}) async-start(bf16[32,272,128]{2,1,0:T(8,128)(2,1)} %pack_heads.1), calls=%async_computation | async-start | bytes 4456448 | tf_op jit(solution)/shard_map/all_to_all | solution.py:319
  16.1 52.7 %all-to-all-done.q_ref.ids_ref.g_ref = bf16[32,272,128]{2,1,0:T(8,128)(2,1)S(1)} async-done(((bf16[32,272,128]{2,1,0:T(8,128)(2,1)}), bf16[32,272,128]{2,1,0:T(8,128)(2,1)S(1)}, u32[]{:S(2)}, u32[]{:S(2)}) %all-to-all-start) | async-done | bytes 2228256 | tf_op jit(solution)/shard_map/all_to_all | solution.py:319
  68.8 0.0 copy-done.1
  68.8 0.0 copy-done.4
  68.8 0.0 copy-start.2
  68.8 1.2 copy-done.2
  70.0 6.9 %attention_forward.1 = bf16[32,128,128]{2,1,0:T(8,128)(2,1)} custom-call(s32[1]{0:T(128)} %bitcast.head_ref, bf16[32,272,128]{2,1,0:T(8,128)(2,1)S(1)} %all-to-all-done.q_ref.ids_ref.g_ref, bf16[32,272,128]{2,1,0:T(8,128)(2,1)S(1)} %all-to-all-done.q_ref.ids_ref.g_ref, bf16[1,32,128,128]{3,2,1,0:T(8,128)(2,1)S(1)} %copy-done.1, ...), custom_call_target="tpu_custom_call" | custom-call | flops 1000000000 | bytes 4000000 | tf_op jit(solution)/shard_map/attention_forward/pallas_call | solution.py:205
  76.9 6.4 %all-to-all-start.1 = ((bf16[32,128,128]{2,1,0:T(8,128)(2,1)}), bf16[32,128,128]{2,1,0:T(8,128)(2,1)}, u32[]{:S(2)}, u32[]{:S(2)}) async-start(bf16[32,128,128]{2,1,0:T(8,128)(2,1)} %attention_forward.1), calls=%async_computation.1 | async-start | bytes 2097152 | tf_op jit(solution)/shard_map/all_to_all | solution.py:319
  83.3 0.0 copy-start.3
  83.3 1.2 copy-done.3
  84.5 12.3 %attention_backward.1 = (bf16[32,144,128]{2,1,0:T(8,128)(2,1)S(1)}, bf16[1,32,128,128]{3,2,1,0:T(8,128)(2,1)}, bf16[1,32,128,128]{3,2,1,0:T(8,128)(2,1)}, f32[1,256]{1,0:T(1,128)S(1)}) custom-call(s32[1]{0:T(128)} %bitcast.head_ref, bf16[32,272,128]{2,1,0:T(8,128)(2,1)S(1)} %all-to-all-done.q_ref.ids_ref.g_ref, ...), custom_call_target="tpu_custom_call" | custom-call | flops 3000000000 | bytes 9000000 | tf_op jit(solution)/shard_map/attention_backward/pallas_call | solution.py:222
  96.9 0.0 copy-start
  96.9 1.0 copy-done
  97.9 0.0 collective-permute-start
  97.9 1.1 collective-permute-done
  99.0 1.3 collective-permute-start.1
  100.3 2.3 %collective-permute-done.1 = f32[1,256]{1,0:T(1,128)S(1)} collective-permute-done((f32[1,256]{1,0:T(1,128)S(1)}, f32[1,256]{1,0:T(1,128)S(1)}, u32[]{:S(2)}, u32[]{:S(2)}) %collective-permute-start.1) | collective-permute-done | bytes 1056 | tf_op jit(solution)/shard_map/ppermute | solution.py:314
  102.6 0.3 collective-permute-start.2
  103.0 4.7 %collective-permute-done.2 = f32[1,256]{1,0:T(1,128)S(1)} collective-permute-done((f32[1,256]{1,0:T(1,128)S(1)}, f32[1,256]{1,0:T(1,128)S(1)}, u32[]{:S(2)}, u32[]{:S(2)}) %collective-permute-start.2) | collective-permute-done | bytes 1056 | tf_op jit(solution)/shard_map/ppermute | solution.py:314
  107.7 0.6 add.11.row_ref
  108.3 1.4 add_bias_row.1
  109.6 2.1 %all-to-all-done.1.y_ref = bf16[32,128,128]{2,1,0:T(8,128)(2,1)} async-done(((bf16[32,128,128]{2,1,0:T(8,128)(2,1)}), bf16[32,128,128]{2,1,0:T(8,128)(2,1)}, u32[]{:S(2)}, u32[]{:S(2)}) %all-to-all-start.1) | async-done | bytes 1048608 | tf_op jit(solution)/shard_map/all_to_all | solution.py:319
  111.8 7.6 %all-to-all-start.2 = ((bf16[32,144,128]{2,1,0:T(8,128)(2,1)}), bf16[32,144,128]{2,1,0:T(8,128)(2,1)S(1)}, u32[]{:S(2)}, u32[]{:S(2)}) async-start(bf16[32,144,128]{2,1,0:T(8,128)(2,1)} %add_bias_row.1), calls=%async_computation.2 | async-start | bytes 2359296 | tf_op jit(solution)/shard_map/all_to_all | solution.py:319
  119.4 3.5 %unpack_heads.2 = bf16[1,2,64,4096]{3,2,1,0:T(8,128)(2,1)} custom-call(bf16[32,128,128]{2,1,0:T(8,128)(2,1)} %all-to-all-done.1.y_ref), custom_call_target="tpu_custom_call" | custom-call | tf_op jit(solution)/shard_map/unpack_heads/pallas_call | solution.py:301
  122.8 26.8 %all-to-all-done.2.y_ref = bf16[32,144,128]{2,1,0:T(8,128)(2,1)S(1)} async-done(((bf16[32,144,128]{2,1,0:T(8,128)(2,1)}), bf16[32,144,128]{2,1,0:T(8,128)(2,1)S(1)}, u32[]{:S(2)}, u32[]{:S(2)}) %all-to-all-start.2) | async-done | bytes 1179680 | tf_op jit(solution)/shard_map/all_to_all | solution.py:319
  149.6 0.0 copy-start.5
  149.6 1.0 copy-done.5
  150.6 3.5 %unpack_heads.3 = (bf16[1,2,64,4096]{3,2,1,0:T(8,128)(2,1)}, f32[32,192]{1,0:T(8,128)}) custom-call(bf16[32,144,128]{2,1,0:T(8,128)(2,1)} %copy-done.5), custom_call_target="tpu_custom_call" | custom-call | tf_op jit(solution)/shard_map/unpack_heads/pallas_call | solution.py:301
  (2 shorter events, 0.0 us)
Async XLA Ops:
  4.6 64.2 %copy-start.1 = (bf16[1,32,128,128]{3,2,1,0:T(8,128)(2,1)S(1)}, bf16[1,32,128,128]{3,2,1,0:T(8,128)(2,1)}, u32[]{:S(2)}) copy-start(bf16[1,32,128,128]{3,2,1,0:T(8,128)(2,1)} %keys_ref.3) | copy-start | bytes 3145732
  4.6 64.2 %copy-start.4 = (f32[32,192]{1,0:T(8,128)S(1)}, f32[32,192]{1,0:T(8,128)}, u32[]{:S(2)}) copy-start(f32[32,192]{1,0:T(8,128)} %rel_ref.3) | copy-start | bytes 73732
  4.6 64.2 %all-to-all-start = ((bf16[32,272,128]{2,1,0:T(8,128)(2,1)}), bf16[32,272,128]{2,1,0:T(8,128)(2,1)S(1)}, u32[]{:S(2)}, u32[]{:S(2)}) async-start(bf16[32,272,128]{2,1,0:T(8,128)(2,1)} %pack_heads.1), calls=%async_computation | async-start | bytes 4456448 | tf_op jit(solution)/shard_map/all_to_all | solution.py:319
  68.8 1.2 copy-start.2
  76.9 34.9 %all-to-all-start.1 = ((bf16[32,128,128]{2,1,0:T(8,128)(2,1)}), bf16[32,128,128]{2,1,0:T(8,128)(2,1)}, u32[]{:S(2)}, u32[]{:S(2)}) async-start(bf16[32,128,128]{2,1,0:T(8,128)(2,1)} %attention_forward.1), calls=%async_computation.1 | async-start | bytes 2097152 | tf_op jit(solution)/shard_map/all_to_all | solution.py:319
  83.3 1.2 copy-start.3
  96.9 1.0 copy-start
  97.9 1.1 collective-permute-start
  99.0 3.6 %collective-permute-start.1 = (f32[1,256]{1,0:T(1,128)S(1)}, f32[1,256]{1,0:T(1,128)S(1)}, u32[]{:S(2)}, u32[]{:S(2)}) collective-permute-start(f32[1,256]{1,0:T(1,128)S(1)} %add.9), channel_id=1, source_target_pairs={{0,64},{32,96},{64,0},{96,32},{128,192},{160,224},{192,128},{224,1... | collective-permute-start | bytes 3080 | tf_op jit(solution)/shard_map/ppermute | solution.py:314
  102.6 5.1 %collective-permute-start.2 = (f32[1,256]{1,0:T(1,128)S(1)}, f32[1,256]{1,0:T(1,128)S(1)}, u32[]{:S(2)}, u32[]{:S(2)}) collective-permute-start(f32[1,256]{1,0:T(1,128)S(1)} %add.10), channel_id=1, source_target_pairs={{0,128},{32,160},{64,192},{96,224},{128,0},{160,32},{192,64},{224,... | collective-permute-start | bytes 3080 | tf_op jit(solution)/shard_map/ppermute | solution.py:314
  111.8 37.8 %all-to-all-start.2 = ((bf16[32,144,128]{2,1,0:T(8,128)(2,1)}), bf16[32,144,128]{2,1,0:T(8,128)(2,1)S(1)}, u32[]{:S(2)}, u32[]{:S(2)}) async-start(bf16[32,144,128]{2,1,0:T(8,128)(2,1)} %add_bias_row.1), calls=%async_computation.2 | async-start | bytes 2359296 | tf_op jit(solution)/shard_map/all_to_all | solution.py:319
  149.6 1.0 copy-start.5

commit v3 on v2

v3 whole, which is shorter than its diff:
```python
import functools
import math

import jax
import jax.numpy as jnp
from jax import lax
from jax.experimental import pallas as pl
from jax.experimental.pallas import tpu as pltpu
from jax.sharding import PartitionSpec as P

HEADS = 32
HEAD_DIM = 128
BLOCK = 64
NBLEN = 128
NEIGH = 2
CH_DEV = 2
POOL = 32
HD = HEADS * HEAD_DIM
REL = 192
N_BLOCK = 32
N_DP = 8
X_SIZE = 4
Z_SIZE = 8
HALF = CH_DEV * BLOCK
EXTRA = 8
PACK_HEADS = 8
SRC_STEP = 4
SCALE = 1.0 / math.sqrt(HEAD_DIM)

NT = (((1,), (1,)), ((), ()))
TN = (((0,), (0,)), ((), ()))
F32 = jnp.float32
BF16 = jnp.bfloat16


VMEM_SPEC = pl.BlockSpec(memory_space=pltpu.VMEM)
SMEM_SPEC = pl.BlockSpec(memory_space=pltpu.SMEM)
ANY_SPEC = pl.BlockSpec(memory_space=pl.ANY)
HBM_SPEC = pl.BlockSpec(memory_space=pltpu.HBM)
CHUNKS = HEADS // PACK_HEADS
CHUNK_WIDTH = PACK_HEADS * HEAD_DIM


def block_rows(c):
    return slice(c * BLOCK, (c + 1) * BLOCK)


def head_columns(h):
    return slice(h * HEAD_DIM, (h + 1) * HEAD_DIM)


def vmem_limit(mib):
    return pltpu.CompilerParams(vmem_limit_bytes=mib * 1024 * 1024)


def start(source, target, sem):
    copy = pltpu.make_async_copy(source, target, sem)
    copy.start()
    return copy


def pack_queries_kernel(fetch_ref, slot_ref, q_ref, out_ref, q_buf, out_buf, in_sems, out_sems):
    copies = []
    for i in range(CHUNKS):
        cols = slice(i * CHUNK_WIDTH, (i + 1) * CHUNK_WIDTH)
        copies.append(start(q_ref.at[0, :, :, cols], q_buf.at[:, :, cols], in_sems.at[i]))
    lane = lax.broadcasted_iota(jnp.int32, (EXTRA, 128), 1)
    ids = jnp.zeros((EXTRA, 128), jnp.int32)
    for c in range(CH_DEV):
        for n in range(NEIGH):
            enc = fetch_ref[0, 0, slot_ref[0, c, n]]
            ids = jnp.where(lane == c * NEIGH + n, enc, ids)
    ids = ids.astype(F32).astype(BF16)
    outs = []
    for i in range(CHUNKS):
        heads = slice(i * PACK_HEADS, (i + 1) * PACK_HEADS)
        copies[i].wait()
        for h in range(i * PACK_HEADS, (i + 1) * PACK_HEADS):
            for c in range(CH_DEV):
                out_buf[h, block_rows(c)] = q_buf[c, :, head_columns(h)]
            out_buf[h, HALF:] = ids
        outs.append(start(out_buf.at[heads], out_ref.at[heads], out_sems.at[i]))
    for copy in outs:
        copy.wait()


def pack_queries(fetch_ids, slot_of, queries):
    return pl.pallas_call(
        pack_queries_kernel,
        in_specs=[SMEM_SPEC, SMEM_SPEC, ANY_SPEC],
        out_specs=ANY_SPEC,
        out_shape=jax.ShapeDtypeStruct((HEADS, HALF + EXTRA, HEAD_DIM), BF16),
        scratch_shapes=[
            pltpu.VMEM((CH_DEV, BLOCK, HD), BF16),
            pltpu.VMEM((HEADS, HALF + EXTRA, HEAD_DIM), BF16),
            pltpu.SemaphoreType.DMA((CHUNKS,)),
            pltpu.SemaphoreType.DMA((CHUNKS,)),
        ],
        compiler_params=vmem_limit(60),
        cost_estimate=pl.CostEstimate(flops=10**11, bytes_accessed=2 * 10**6, transcendentals=0),
        name="pack_queries",
    )(fetch_ids, slot_of, queries)


def pack_grads_kernel(head_ref, g_ref, *refs):
    out_refs, (g_buf, out_buf, in_sems, out_sems) = refs[:X_SIZE], refs[X_SIZE:]
    copies = []
    for i in range(X_SIZE):
        column = lax.rem(head_ref[0] // Z_SIZE + i, X_SIZE) * CHUNK_WIDTH
        cols = pl.ds(pl.multiple_of(column, CHUNK_WIDTH), CHUNK_WIDTH)
        copies.append(start(g_ref.at[0, :, :, cols], g_buf.at[i], in_sems.at[i]))
    outs = []
    for i in range(X_SIZE):
        copies[i].wait()
        for h in range(Z_SIZE):
            for c in range(CH_DEV):
                out_buf[i, h, block_rows(c)] = g_buf[i, c, :, head_columns(h)]
        outs.append(start(out_buf.at[i], out_refs[i], out_sems.at[i]))
    for copy in outs:
        copy.wait()


def pack_grads(head, out_grad):
    shape = (Z_SIZE, HALF, HEAD_DIM)
    return pl.pallas_call(
        pack_grads_kernel,
        in_specs=[SMEM_SPEC, ANY_SPEC],
        out_specs=[ANY_SPEC] * X_SIZE,
        out_shape=[jax.ShapeDtypeStruct(shape, BF16)] * X_SIZE,
        scratch_shapes=[
            pltpu.VMEM((X_SIZE, CH_DEV, BLOCK, CHUNK_WIDTH), BF16),
            pltpu.VMEM((X_SIZE, *shape), BF16),
            pltpu.SemaphoreType.DMA((X_SIZE,)),
            pltpu.SemaphoreType.DMA((X_SIZE,)),
        ],
        compiler_params=vmem_limit(60),
        cost_estimate=pl.CostEstimate(flops=0, bytes_accessed=2 * 10**6, transcendentals=0),
        name="pack_grads",
    )(head, out_grad)


def regroup_kernel(head_ref, *refs):
    in_refs, out_refs = refs[:X_SIZE], refs[X_SIZE : X_SIZE + Z_SIZE]
    buf, in_sems, out_sems = refs[X_SIZE + Z_SIZE :]
    copies = [start(in_refs[i], buf.at[i], in_sems.at[i]) for i in range(X_SIZE)]
    for copy in copies:
        copy.wait()
    copies = []
    for k in range(Z_SIZE):
        owner = lax.rem(head_ref[0] + k, Z_SIZE)
        copies.append(start(buf.at[:, owner], out_refs[k], out_sems.at[k]))
    for copy in copies:
        copy.wait()


def regroup(head, parts):
    return pl.pallas_call(
        regroup_kernel,
        in_specs=[SMEM_SPEC] + [ANY_SPEC] * X_SIZE,
        out_specs=[ANY_SPEC] * Z_SIZE,
        out_shape=[jax.ShapeDtypeStruct((X_SIZE, HALF, HEAD_DIM), BF16)] * Z_SIZE,
        scratch_shapes=[
            pltpu.VMEM((X_SIZE, Z_SIZE, HALF, HEAD_DIM), BF16),
            pltpu.SemaphoreType.DMA((X_SIZE,)),
            pltpu.SemaphoreType.DMA((Z_SIZE,)),
        ],
        compiler_params=vmem_limit(60),
        cost_estimate=pl.CostEstimate(flops=10**11, bytes_accessed=2 * 10**6, transcendentals=0),
        name="regroup_grads",
    )(head, *parts)


def send_by(part, dx, dz):
    pairs = [
        (x * Z_SIZE + z, (x + dx) % X_SIZE * Z_SIZE + (z + dz) % Z_SIZE)
        for x in range(X_SIZE)
        for z in range(Z_SIZE)
    ]
    return lax.ppermute(part, "block", pairs)


def build_bias(rel_ref, head, bias_ref):
    row = rel_ref[pl.ds(head, 1), :]
    wide = jnp.concatenate([row, jnp.zeros((1, 256 - REL), F32)], axis=1)
    wide = jnp.broadcast_to(wide, (BLOCK, 256))
    rolled = pltpu.roll(wide, 256 - (BLOCK - 1), 1, stride=1, stride_axis=0)[:, :NBLEN]
    bias_ref[...] = jnp.concatenate([rolled, rolled], axis=1)


def fold_bias(dscore_sum):
    folded = dscore_sum[:, :NBLEN] + dscore_sum[:, NBLEN:]
    wide = jnp.concatenate([folded, jnp.zeros((BLOCK, NBLEN), F32)], axis=1)
    group = sum(
        pltpu.roll(wide[t : t + 8], BLOCK - 8 - t, 1) if t < BLOCK - 8 else wide[t : t + 8]
        for t in range(0, BLOCK, 8)
    )
    return sum(
        pltpu.roll(group[r : r + 1], 7 - r, 1) if r < 7 else group[r : r + 1] for r in range(8)
    )


def read_ids(x_ref, ids_vmem, ids_smem, sem):
    ids_vmem[...] = x_ref[:, HALF, :].astype(F32).astype(jnp.int32)
    copy = pltpu.make_async_copy(ids_vmem, ids_smem, sem)
    copy.start()
    return copy


BLOCKS_STEP = [(s, c) for s in range(SRC_STEP) for c in range(CH_DEV)]


def softmax_parts(sources, ids_smem, bias_ref, x_ref, keys_ref, values_ref):
    bias = bias_ref[...]
    ids = [[ids_smem[sources[s], c * NEIGH + n] for n in range(NEIGH)] for s, c in BLOCKS_STEP]
    q = [x_ref[sources[s], block_rows(c)] for s, c in BLOCKS_STEP]
    k = [jnp.concatenate([keys_ref[0, i] for i in pair], axis=0) for pair in ids]
    v = [jnp.concatenate([values_ref[0, i] for i in pair], axis=0) for pair in ids]
    scores = [lax.dot_general(a, b, NT, preferred_element_type=F32) for a, b in zip(q, k)]
    scores = [a * SCALE + bias for a in scores]
    tops = [jnp.max(a, axis=-1, keepdims=True) for a in scores]
    expo = [jnp.exp(a - b) for a, b in zip(scores, tops)]
    inverse = [1.0 / jnp.sum(a, axis=-1, keepdims=True) for a in expo]
    probs = [a * b for a, b in zip(expo, inverse)]
    return ids, q, k, v, probs


def forward_kernel(
    head_ref, x_ref, keys_ref, values_ref, rel_ref, y_ref, ids_vmem, ids_smem, bias_ref, sem
):
    copy = read_ids(x_ref, ids_vmem, ids_smem, sem)
    build_bias(rel_ref, head_ref[0], bias_ref)
    copy.wait()

    def step(t, carry):
        sources = [t * SRC_STEP + s for s in range(SRC_STEP)]
        ids, q, k, v, probs = softmax_parts(
            sources, ids_smem, bias_ref, x_ref, keys_ref, values_ref
        )
        for i, (s, c) in enumerate(BLOCKS_STEP):
            attended = jnp.dot(probs[i].astype(BF16), v[i], preferred_element_type=F32)
            y_ref[sources[s], block_rows(c)] = attended.astype(BF16)
        return carry

    lax.fori_loop(0, N_BLOCK // SRC_STEP, step, 0)


def near_sources(index, t):
    x, z = index // Z_SIZE, lax.rem(index, Z_SIZE)
    z_source = lax.rem(z + Z_SIZE - t, Z_SIZE)
    return [lax.rem(x + X_SIZE - s, X_SIZE) * Z_SIZE + z_source for s in range(SRC_STEP)]


def score_grads(sources, t, ids_smem, bias_ref, x_ref, g_buf, keys_ref, values_ref):
    ids, q, k, v, probs = softmax_parts(
        sources, ids_smem, bias_ref, x_ref, keys_ref, values_ref
    )
    g = [g_buf[t, s, block_rows(c)] for s, c in BLOCKS_STEP]
    dprobs = [lax.dot_general(a, b, NT, preferred_element_type=F32) for a, b in zip(g, v)]
    inner = [jnp.sum(a * b, axis=-1, keepdims=True) for a, b in zip(probs, dprobs)]
    dscores = [a * (b - c) for a, b, c in zip(probs, dprobs, inner)]
    return ids, q, k, g, probs, dscores


def query_grad_kernel(head_ref, x_ref, keys_ref, values_ref, rel_ref, *refs):
    g_refs = refs[:Z_SIZE]
    y_ref, bias_out, ids_vmem, ids_smem, bias_ref, dsum_ref, g_buf, sem, g_sems = refs[Z_SIZE:]
    g_copies = [start(g_refs[k], g_buf.at[k], g_sems.at[k]) for k in range(Z_SIZE)]
    copy = read_ids(x_ref, ids_vmem, ids_smem, sem)
    build_bias(rel_ref, head_ref[0], bias_ref)
    dsum_ref[...] = jnp.zeros_like(dsum_ref)
    copy.wait()
    for g_copy in g_copies:
        g_copy.wait()

    def step(t, carry):
        sources = near_sources(head_ref[0], t)
        _, _, k, _, _, dscores = score_grads(
            sources, t, ids_smem, bias_ref, x_ref, g_buf, keys_ref, values_ref
        )
        dsum_ref[...] += sum(dscores)
        for i, (s, c) in enumerate(BLOCKS_STEP):
            low = dscores[i].astype(BF16)
            query_grad = jnp.dot(low, k[i], preferred_element_type=F32) * SCALE
            y_ref[sources[s], block_rows(c)] = query_grad.astype(BF16)
        return carry

    lax.fori_loop(0, Z_SIZE, step, 0)
    bias_out[...] = fold_bias(dsum_ref[...])


def pool_grad_kernel(head_ref, x_ref, keys_ref, values_ref, rel_ref, *refs):
    g_refs = refs[:Z_SIZE]
    dk_out, dv_out, ids_vmem, ids_smem, bias_ref, dk_ref, dv_ref, g_buf, sem, g_sems = refs[Z_SIZE:]
    g_copies = [start(g_refs[k], g_buf.at[k], g_sems.at[k]) for k in range(Z_SIZE)]
    copy = read_ids(x_ref, ids_vmem, ids_smem, sem)
    build_bias(rel_ref, head_ref[0], bias_ref)
    dk_ref[...] = jnp.zeros_like(dk_ref)
    dv_ref[...] = jnp.zeros_like(dv_ref)
    copy.wait()
    for g_copy in g_copies:
        g_copy.wait()

    def step(t, carry):
        sources = near_sources(head_ref[0], t)
        ids, q, _, g, probs, dscores = score_grads(
            sources, t, ids_smem, bias_ref, x_ref, g_buf, keys_ref, values_ref
        )
        dscores_low = [a.astype(BF16) for a in dscores]
        probs_low = [a.astype(BF16) for a in probs]
        dk = [lax.dot_general(a, b, TN, preferred_element_type=F32) for a, b in zip(dscores_low, q)]
        dv = [lax.dot_general(a, b, TN, preferred_element_type=F32) for a, b in zip(probs_low, g)]
        for i in range(len(BLOCKS_STEP)):
            for n in range(NEIGH):
                rows = slice(n * NBLEN, (n + 1) * NBLEN)
                dk_ref[ids[i][n]] += dk[i][rows]
                dv_ref[ids[i][n]] += dv[i][rows]
        return carry

    lax.fori_loop(0, Z_SIZE, step, 0)
    dk_out[0] = (dk_ref[...] * SCALE).astype(BF16)
    dv_out[0] = dv_ref[...].astype(BF16)


POOL_SHAPE = (1, POOL, NBLEN, HEAD_DIM)
BIAS_SHAPE = (BLOCK, NEIGH * NBLEN)
IDS_SCRATCH = [pltpu.VMEM((N_BLOCK, 128), jnp.int32), pltpu.SMEM((N_BLOCK, 128), jnp.int32)]


def forward(head, recv, keys_pool, values_pool, rel_bias):
    return pl.pallas_call(
        forward_kernel,
        in_specs=[SMEM_SPEC] + [VMEM_SPEC] * 4,
        out_specs=VMEM_SPEC,
        out_shape=jax.ShapeDtypeStruct((N_BLOCK, HALF, HEAD_DIM), BF16),
        scratch_shapes=[*IDS_SCRATCH, pltpu.VMEM(BIAS_SHAPE, F32), pltpu.SemaphoreType.DMA],
        compiler_params=vmem_limit(16),
        cost_estimate=pl.CostEstimate(flops=10**11, bytes_accessed=4 * 10**6, transcendentals=10**6),
        name="attention_forward",
    )(head, recv, keys_pool, values_pool, rel_bias)


def query_grads(head, recv, grads, keys_pool, values_pool, rel_bias):
    return pl.pallas_call(
        query_grad_kernel,
        in_specs=[SMEM_SPEC] + [VMEM_SPEC] * 4 + [ANY_SPEC] * Z_SIZE,
        out_specs=[VMEM_SPEC] * 2,
        out_shape=[
            jax.ShapeDtypeStruct((N_BLOCK, HALF + EXTRA, HEAD_DIM), BF16),
            jax.ShapeDtypeStruct((1, 256), F32),
        ],
        scratch_shapes=[
            *IDS_SCRATCH,
            pltpu.VMEM(BIAS_SHAPE, F32),
            pltpu.VMEM(BIAS_SHAPE, F32),
            pltpu.VMEM((Z_SIZE, X_SIZE, HALF, HEAD_DIM), BF16),
            pltpu.SemaphoreType.DMA,
            pltpu.SemaphoreType.DMA((Z_SIZE,)),
        ],
        compiler_params=vmem_limit(16),
        cost_estimate=pl.CostEstimate(flops=10**11, bytes_accessed=5 * 10**6, transcendentals=10**6),
        name="query_grads",
    )(head, recv, keys_pool, values_pool, rel_bias, *grads)


def pool_grads(head, recv, grads, keys_pool, values_pool, rel_bias):
    return pl.pallas_call(
        pool_grad_kernel,
        in_specs=[SMEM_SPEC] + [VMEM_SPEC] * 4 + [ANY_SPEC] * Z_SIZE,
        out_specs=[VMEM_SPEC] * 2,
        out_shape=[jax.ShapeDtypeStruct(POOL_SHAPE, BF16)] * 2,
        scratch_shapes=[
            *IDS_SCRATCH,
            pltpu.VMEM(BIAS_SHAPE, F32),
            pltpu.VMEM(POOL_SHAPE[1:], F32),
            pltpu.VMEM(POOL_SHAPE[1:], F32),
            pltpu.VMEM((Z_SIZE, X_SIZE, HALF, HEAD_DIM), BF16),
            pltpu.SemaphoreType.DMA,
            pltpu.SemaphoreType.DMA((Z_SIZE,)),
        ],
        compiler_params=vmem_limit(24),
        cost_estimate=pl.CostEstimate(flops=10**11, bytes_accessed=6 * 10**6, transcendentals=10**6),
        name="pool_grads",
    )(head, recv, keys_pool, values_pool, rel_bias, *grads)


def add_row_kernel(row_ref, _, y_ref, block_ref, sem):
    row = row_ref[...]
    high = row.astype(BF16)
    rest = row - high.astype(F32)
    middle = rest.astype(BF16)
    low = (rest - middle.astype(F32)).astype(BF16)
    lines = [part.astype(F32)[:, c : c + 128] for part in (high, middle, low) for c in (0, 128)]
    block = jnp.concatenate([*lines, jnp.zeros((EXTRA - 6, 128), F32)], axis=0).astype(BF16)
    block_ref[...] = jnp.broadcast_to(block[None], block_ref.shape)
    copy = pltpu.make_async_copy(block_ref, y_ref.at[:, HALF:], sem)
    copy.start()
    copy.wait()


def add_row(row, y):
    return pl.pallas_call(
        add_row_kernel,
        in_specs=[VMEM_SPEC, ANY_SPEC],
        out_specs=ANY_SPEC,
        out_shape=jax.ShapeDtypeStruct(y.shape, BF16),
        scratch_shapes=[pltpu.VMEM((N_BLOCK, EXTRA, HEAD_DIM), BF16), pltpu.SemaphoreType.DMA],
        input_output_aliases={1: 0},
        compiler_params=vmem_limit(4),
        name="add_bias_row",
    )(row, y)


def unpack_kernel(y_ref, out_ref, buf, sems):
    copies = []
    for i in range(CHUNKS):
        for h in range(i * PACK_HEADS, (i + 1) * PACK_HEADS):
            for c in range(CH_DEV):
                buf[c, :, head_columns(h)] = y_ref[h, block_rows(c)]
        cols = slice(i * CHUNK_WIDTH, (i + 1) * CHUNK_WIDTH)
        copy = pltpu.make_async_copy(buf.at[:, :, cols], out_ref.at[0, :, :, cols], sems.at[i])
        copy.start()
        copies.append(copy)
    for copy in copies:
        copy.wait()


def unpack_bias_kernel(y_ref, out_ref, bias_ref, buf, sems):
    lines = y_ref[:, HALF:, :].astype(F32)
    part = [lines[:, r, :] for r in range(6)]
    left = (part[0] + part[2]) + part[4]
    right = (part[1] + part[3]) + part[5]
    bias_ref[...] = jnp.concatenate([left, right], axis=1)[:, :REL]
    unpack_kernel(y_ref, out_ref, buf, sems)


def unpack(back):
    shape = jax.ShapeDtypeStruct((1, CH_DEV, BLOCK, HD), BF16)
    with_bias = back.shape[1] > HALF
    return pl.pallas_call(
        unpack_bias_kernel if with_bias else unpack_kernel,
        in_specs=[VMEM_SPEC],
        out_specs=[HBM_SPEC] + [VMEM_SPEC] * with_bias,
        out_shape=[shape] + [jax.ShapeDtypeStruct((HEADS, REL), F32)] * with_bias,
        scratch_shapes=[pltpu.VMEM((CH_DEV, BLOCK, HD), BF16), pltpu.SemaphoreType.DMA((CHUNKS,))],
        compiler_params=vmem_limit(8),
        name="unpack_heads",
    )(back)


def sum_groups(part):
    for hop in (1, 2, 4):
        part = part + lax.ppermute(part, "dp", [(d, d ^ hop) for d in range(N_DP)])
    return part


def all_to_all(parts):
    return lax.all_to_all(parts, "block", split_axis=0, concat_axis=0, tiled=True)


def on_device(queries, keys_pool, values_pool, rel_bias, out_grad, fetch_ids, slot_of):
    head = lax.axis_index("block").astype(jnp.int32).reshape(1)
    parts = pack_grads(head, out_grad)
    queries, *parts = lax.optimization_barrier((queries, *parts))
    parts = [parts[0]] + [send_by(parts[dx], dx, 0) for dx in range(1, X_SIZE)]
    sent = pack_queries(fetch_ids, slot_of, queries)
    recv = all_to_all(sent)
    grads = list(regroup(head, parts))
    recv, grads[0] = lax.optimization_barrier((recv, grads[0]))
    y = forward(head, recv, keys_pool, values_pool, rel_bias)
    y, grads[1], grads[7] = lax.optimization_barrier((y, grads[1], grads[7]))
    grads = [grads[0]] + [send_by(grads[dz], 0, dz) for dz in range(1, Z_SIZE)]
    back_y = all_to_all(y)
    recv, _ = lax.optimization_barrier((recv, y))
    dq, bias_part = query_grads(head, recv, grads, keys_pool, values_pool, rel_bias)
    dq = add_row(sum_groups(bias_part), dq)
    back_dq = all_to_all(dq)
    recv, _ = lax.optimization_barrier((recv, dq))
    key_grad, value_grad = pool_grads(head, recv, grads, keys_pool, values_pool, rel_bias)
    (attended,) = unpack(back_y)
    query_grad, bias_grad = unpack(back_dq)
    return (attended, query_grad, key_grad, value_grad, bias_grad)


def solution(mesh):
    in_specs = (
        P("dp", "block", None, None),
        P("dp", None, None, "block"),
        P("dp", None, None, "block"),
        P(),
        P("dp", "block", None, None),
        P("dp", "block", None),
        P("dp", "block", None),
    )
    out_specs = (
        P("dp", "block", None, None),
        P("dp", "block", None, None),
        P("dp", None, None, "block"),
        P("dp", None, None, "block"),
        P(),
    )
    return jax.shard_map(
        on_device, mesh=mesh, in_specs=in_specs, out_specs=out_specs, check_vma=False
    )
```

time: 155 us -> 137 us (0.88)
  waiting for transfers between devices: 89.8 us -> 34.7 us
  starting transfers between devices: 27.1 us -> 55.8 us
  Pallas kernels: 31.5 us -> 38.3 us
  local copies, waits for them, and re-layouts: 4.5 us -> 6.94 us
    all_to_all x3, waiting for transfers between devices: 81.6 us -> 24.3 us  [all_to_all(): lax.all_to_all(parts, 'block', split_axis=0, concat_axis=0, tiled=True)]
    ppermute x0 -> x10, starting transfers between devices: none -> 30.3 us  [send_by(): return lax.ppermute(part, 'block', pairs)]
    pallas_call x6 -> x9, Pallas kernels: 31.5 us -> 38.3 us  [the longest x1 12.2 us: pool_grads(): pl.pallas_call(pool_grad_kernel, in_specs=[SMEM_SPEC] + [VMEM_SPEC] * 4 +...]
    unnamed x12 -> x22, local copies, waits for them, and re-layouts: 4.5 us -> 6.94 us
    ppermute x0 -> x10, waiting for transfers between devices: none -> 2.2 us  [send_by(): return lax.ppermute(part, 'block', pairs)]
    all_to_all x3, starting transfers between devices: 25.4 us -> 23.8 us  [all_to_all(): lax.all_to_all(parts, 'block', split_axis=0, concat_axis=0, tiled=True)]
  transfers between devices with their start and end apart: 6 -> 16, of which waited for: 6 -> 6; matrix products, arithmetic and copies ran while one was open for 0% -> 0% of each run, Pallas kernels for 11% -> 25%
where the time goes in v3:
time: 137 us
  starting transfers between devices  55.8 us (41%)
  Pallas kernels  38.3 us (28%)
  waiting for transfers between devices  34.7 us (25%)
  local copies, waits for them, and re-layouts  6.94 us (5%)
    ppermute x10, starting transfers between devices, send_by(): return lax.ppermute(part, 'block', pairs)  30.3 us
    all_to_all x3, waiting for transfers between devices, all_to_all(): lax.all_to_all(parts, 'block', split_axis=0, concat_axis=0, tiled=True)  24.3 us
    all_to_all x3, starting transfers between devices, all_to_all(): lax.all_to_all(parts, 'block', split_axis=0, concat_axis=0, tiled=True)  23.8 us
    pallas_call x1, Pallas kernels, pool_grads(): pl.pallas_call(pool_grad_kernel, in_specs=[SMEM_SPEC] + [VMEM_SPEC] * 4 +...  12.2 us
    pallas_call x1, Pallas kernels, query_grads(): pl.pallas_call(query_grad_kernel, in_specs=[SMEM_SPEC] + [VMEM_SPEC] * 4...  8.84 us
    ppermute x3, waiting for transfers between devices, sum_groups(): part = part + lax.ppermute(part, 'dp', [(d, d ^ hop) for d in range(N_DP)])  8.16 us
    unnamed x22, local copies, waits for them, and re-layouts  6.94 us
    pallas_call x1, Pallas kernels, forward(): pl.pallas_call(forward_kernel, in_specs=[SMEM_SPEC] + [VMEM_SPEC] * 4, ou...  6.83 us
  transfers between devices with their start and end apart: 16, of which 6 were waited for; matrix products, arithmetic and copies ran while one was open for 0% of the time, Pallas kernels for 25%

profile of v3, /device:TPU:16, one launch (start us, length us, event | category | flops | bytes accessed | tf_op | source)
XLA Modules:
  0.0 136.5 jit_solution(12778901197254245903)
XLA Ops:
  0.6 2.0 %pack_grads.1 = (bf16[8,128,128]{2,1,0:T(8,128)(2,1)}, bf16[8,128,128]{2,1,0:T(8,128)(2,1)}, bf16[8,128,128]{2,1,0:T(8,128)(2,1)}, bf16[8,128,128]{2,1,0:T(8,128)(2,1)}) custom-call(s32[1]{0:T(128)} %bitcast.head_ref, bf16[1,2,64,4096]{3,2,1,0:T(8,128)(2,1)} %g_ref.1), custom_call_target="tpu_custom_call" | custom-call | bytes 2000000 | tf_op jit(solution)/shard_map/pack_grads/pallas_call | solution.py:125
  2.7 1.6 %collective-permute-start = (bf16[8,128,128]{2,1,0:T(8,128)(2,1)}, bf16[8,128,128]{2,1,0:T(8,128)(2,1)S(1)}, u32[]{:S(2)}, u32[]{:S(2)}) collective-permute-start(bf16[8,128,128]{2,1,0:T(8,128)(2,1)} %get-tuple-element.41), channel_id=1, source_target_pairs={{0,8},{1,9},{2,10},{3,11},{4,12},{5,13},{6,14},{7,15},{8,16},{9,17... | collective-permute-start | bytes 786440 | tf_op jit(solution)/shard_map/ppermute | solution.py:179
  4.2 2.7 %collective-permute-start.1 = (bf16[8,128,128]{2,1,0:T(8,128)(2,1)}, bf16[8,128,128]{2,1,0:T(8,128)(2,1)}, u32[]{:S(2)}, u32[]{:S(2)}) collective-permute-start(bf16[8,128,128]{2,1,0:T(8,128)(2,1)} %get-tuple-element.42), channel_id=1, source_target_pairs={{0,16},{1,17},{2,18},{3,19},{4,20},{5,21},{6,22},{7,23},{8,24},{9,... | collective-permute-start | bytes 786440 | tf_op jit(solution)/shard_map/ppermute | solution.py:179
  7.0 1.4 %collective-permute-start.2 = (bf16[8,128,128]{2,1,0:T(8,128)(2,1)}, bf16[8,128,128]{2,1,0:T(8,128)(2,1)}, u32[]{:S(2)}, u32[]{:S(2)}) collective-permute-start(bf16[8,128,128]{2,1,0:T(8,128)(2,1)} %get-tuple-element.43), channel_id=1, source_target_pairs={{0,24},{1,25},{2,26},{3,27},{4,28},{5,29},{6,30},{7,31},{8,0},{9,1... | collective-permute-start | bytes 786440 | tf_op jit(solution)/shard_map/ppermute | solution.py:179
  8.4 2.8 %pack_queries.1 = bf16[32,136,128]{2,1,0:T(8,128)(2,1)} custom-call(s32[1,1,3]{2,1,0:T(1,128)} %fetch_ref.1, s32[1,2,2]{2,1,0:T(2,128)} %slot_ref.1, bf16[1,2,64,4096]{3,2,1,0:T(8,128)(2,1)} %q_ref), custom_call_target="tpu_custom_call" | custom-call | flops 99999997952 | bytes 2000000 | tf_op jit(solution)/shard_map/pack_queries/pallas_call | solution.py:88
  11.2 8.9 %all-to-all-start = ((bf16[32,136,128]{2,1,0:T(8,128)(2,1)}), bf16[32,136,128]{2,1,0:T(8,128)(2,1)S(1)}, u32[]{:S(2)}, u32[]{:S(2)}) async-start(bf16[32,136,128]{2,1,0:T(8,128)(2,1)} %pack_queries.1), calls=%async_computation | async-start | bytes 2228224 | tf_op jit(solution)/shard_map/all_to_all | solution.py:457
  20.8 2.2 %regroup_grads.1 = (bf16[4,128,128]{2,1,0:T(8,128)(2,1)}, bf16[4,128,128]{2,1,0:T(8,128)(2,1)}, bf16[4,128,128]{2,1,0:T(8,128)(2,1)}, bf16[4,128,128]{2,1,0:T(8,...) custom-call(s32[1]{0:T(128)} %bitcast.head_ref, ...), custom_call_target="tpu_custom_call" | custom-call | flops 99999997952 | bytes 2000000 | tf_op jit(solution)/shard_map/regroup_grads/pallas_call | solution.py:157
  23.1 2.8 %collective-permute-start.4 = (bf16[4,128,128]{2,1,0:T(8,128)(2,1)}, bf16[4,128,128]{2,1,0:T(8,128)(2,1)S(1)}, u32[]{:S(2)}, u32[]{:S(2)}) collective-permute-start(bf16[4,128,128]{2,1,0:T(8,128)(2,1)} %get-tuple-element.52), channel_id=1, source_target_pairs={{0,2},{1,3},{2,4},{3,5},{4,6},{5,7},{6,0},{7,1},{8,10},{9,11},{10,... | collective-permute-start | bytes 393224 | tf_op jit(solution)/shard_map/ppermute | solution.py:179
  25.8 3.6 %collective-permute-start.5 = (bf16[4,128,128]{2,1,0:T(8,128)(2,1)}, bf16[4,128,128]{2,1,0:T(8,128)(2,1)S(1)}, u32[]{:S(2)}, u32[]{:S(2)}) collective-permute-start(bf16[4,128,128]{2,1,0:T(8,128)(2,1)} %get-tuple-element.53), channel_id=1, source_target_pairs={{0,3},{1,4},{2,5},{3,6},{4,7},{5,0},{6,1},{7,2},{8,11},{9,12},{10,... | collective-permute-start | bytes 393224 | tf_op jit(solution)/shard_map/ppermute | solution.py:179
  29.5 1.4 %collective-permute-start.6 = (bf16[4,128,128]{2,1,0:T(8,128)(2,1)}, bf16[4,128,128]{2,1,0:T(8,128)(2,1)}, u32[]{:S(2)}, u32[]{:S(2)}) collective-permute-start(bf16[4,128,128]{2,1,0:T(8,128)(2,1)} %get-tuple-element.54), channel_id=1, source_target_pairs={{0,4},{1,5},{2,6},{3,7},{4,0},{5,1},{6,2},{7,3},{8,12},{9,13},{10,... | collective-permute-start | bytes 393224 | tf_op jit(solution)/shard_map/ppermute | solution.py:179
  30.9 4.1 %collective-permute-start.7 = (bf16[4,128,128]{2,1,0:T(8,128)(2,1)}, bf16[4,128,128]{2,1,0:T(8,128)(2,1)}, u32[]{:S(2)}, u32[]{:S(2)}) collective-permute-start(bf16[4,128,128]{2,1,0:T(8,128)(2,1)} %get-tuple-element.55), channel_id=1, source_target_pairs={{0,5},{1,6},{2,7},{3,0},{4,1},{5,2},{6,3},{7,4},{8,13},{9,14},{10,... | collective-permute-start | bytes 393224 | tf_op jit(solution)/shard_map/ppermute | solution.py:179
  35.0 3.1 %collective-permute-start.8 = (bf16[4,128,128]{2,1,0:T(8,128)(2,1)}, bf16[4,128,128]{2,1,0:T(8,128)(2,1)}, u32[]{:S(2)}, u32[]{:S(2)}) collective-permute-start(bf16[4,128,128]{2,1,0:T(8,128)(2,1)} %get-tuple-element.56), channel_id=1, source_target_pairs={{0,6},{1,7},{2,0},{3,1},{4,2},{5,3},{6,4},{7,5},{8,14},{9,15},{10,... | collective-permute-start | bytes 393224 | tf_op jit(solution)/shard_map/ppermute | solution.py:179
  38.0 13.3 %all-to-all-done.x_ref = bf16[32,136,128]{2,1,0:T(8,128)(2,1)S(1)} async-done(((bf16[32,136,128]{2,1,0:T(8,128)(2,1)}), bf16[32,136,128]{2,1,0:T(8,128)(2,1)S(1)}, u32[]{:S(2)}, u32[]{:S(2)}) %all-to-all-start) | async-done | bytes 1114144 | tf_op jit(solution)/shard_map/all_to_all | solution.py:457
  51.3 6.8 %attention_forward.1 = bf16[32,128,128]{2,1,0:T(8,128)(2,1)} custom-call(s32[1]{0:T(128)} %bitcast.head_ref, bf16[32,136,128]{2,1,0:T(8,128)(2,1)S(1)} %all-to-all-done.x_ref, bf16[1,32,128,128]{3,2,1,0:T(8,128)(2,1)S(1)} %copy-done, bf16[1,32,128,128]{3,2,1,0:T(8,128)(2,1)S(1)} %copy-done.2, f32[32,192]{1,0:T(8,128)S(1)} %copy-done.5), custom_call_target="tpu_custom_call" | custom-call | flops 99999997952 | bytes 4000000 | tf_op jit(solution)/shard_map/attention_forward/pallas_call | solution.py:330
  58.2 9.6 %collective-permute-start.3 = (bf16[4,128,128]{2,1,0:T(8,128)(2,1)}, bf16[4,128,128]{2,1,0:T(8,128)(2,1)}, u32[]{:S(2)}, u32[]{:S(2)}) collective-permute-start(bf16[4,128,128]{2,1,0:T(8,128)(2,1)} %get-tuple-element.51), channel_id=1, source_target_pairs={{0,1},{1,2},{2,3},{3,4},{4,5},{5,6},{6,7},{7,0},{8,9},{9,10},{10,1... | collective-permute-start | bytes 393224 | tf_op jit(solution)/shard_map/ppermute | solution.py:179
  67.8 7.3 %all-to-all-start.1 = ((bf16[32,128,128]{2,1,0:T(8,128)(2,1)}), bf16[32,128,128]{2,1,0:T(8,128)(2,1)S(1)}, u32[]{:S(2)}, u32[]{:S(2)}) async-start(bf16[32,128,128]{2,1,0:T(8,128)(2,1)} %attention_forward.1), calls=%async_computation.1 | async-start | bytes 2097152 | tf_op jit(solution)/shard_map/all_to_all | solution.py:457
  75.1 2.2 %collective-permute-done.9.refs_7_ = bf16[4,128,128]{2,1,0:T(8,128)(2,1)} collective-permute-done((bf16[4,128,128]{2,1,0:T(8,128)(2,1)}, bf16[4,128,128]{2,1,0:T(8,128)(2,1)}, u32[]{:S(2)}, u32[]{:S(2)}) %collective-permute-start.9) | collective-permute-done | bytes 131104 | tf_op jit(solution)/shard_map/ppermute | solution.py:179
  77.3 1.2 copy-done.3
  78.5 0.9 copy-done.8
  79.4 8.8 %query_grads.1 = (bf16[32,136,128]{2,1,0:T(8,128)(2,1)}, f32[1,256]{1,0:T(1,128)S(1)}) custom-call(s32[1]{0:T(128)} %bitcast.head_ref, bf16[32,136,128]{2,1,0:T(8,128)(2,1)S(1)} %all-to-all-done.x_ref, bf16[1,32,128,128]{3,2,1,0:T(8,128)(2,1)S(1)} %copy-done, bf16[1,32,128,128]{3,2,1,0:T(8,128)(2,1)S(1)} %copy-done.3, f32[32,192]{1,0:T(8,128)S(1)} %copy-done.6, ...), custom_call_target="tpu_custom_call" | custom-call | flops 99999997952 | bytes 5000000 | tf_op jit(solution)/shard_map/query_grads/pallas_call | solution.py:343
  88.4 1.1 collective-permute-done.10
  89.5 1.3 collective-permute-start.11
  90.8 2.3 %collective-permute-done.11 = f32[1,256]{1,0:T(1,128)S(1)} collective-permute-done((f32[1,256]{1,0:T(1,128)S(1)}, f32[1,256]{1,0:T(1,128)S(1)}, u32[]{:S(2)}, u32[]{:S(2)}) %collective-permute-start.11) | collective-permute-done | bytes 1056 | tf_op jit(solution)/shard_map/ppermute | solution.py:452
  93.4 4.7 %collective-permute-done.12 = f32[1,256]{1,0:T(1,128)S(1)} collective-permute-done((f32[1,256]{1,0:T(1,128)S(1)}, f32[1,256]{1,0:T(1,128)S(1)}, u32[]{:S(2)}, u32[]{:S(2)}) %collective-permute-start.12) | collective-permute-done | bytes 1056 | tf_op jit(solution)/shard_map/ppermute | solution.py:452
  98.9 7.6 %all-to-all-start.2 = ((bf16[32,136,128]{2,1,0:T(8,128)(2,1)}), bf16[32,136,128]{2,1,0:T(8,128)(2,1)S(1)}, u32[]{:S(2)}, u32[]{:S(2)}) async-start(bf16[32,136,128]{2,1,0:T(8,128)(2,1)} %add_bias_row.1), calls=%async_computation.2 | async-start | bytes 2228224 | tf_op jit(solution)/shard_map/all_to_all | solution.py:457
  106.5 1.2 copy-done.1
  107.7 1.2 copy-done.4
  109.7 0.9 copy-done.9
  110.6 12.2 %pool_grads.1 = (bf16[1,32,128,128]{3,2,1,0:T(8,128)(2,1)}, bf16[1,32,128,128]{3,2,1,0:T(8,128)(2,1)}) custom-call(s32[1]{0:T(128)} %bitcast.head_ref, bf16[32,136,128]{2,1,0:T(8,128)(2,1)S(1)} %all-to-all-done.x_ref, bf16[1,32,128,128]{3,2,1,0:T(8,128)(2,1)S(1)} %copy-done.1, bf16[1,32,128,128]{3,2,1,0:T(8,128)(2,1)S(1)} %copy-done.4, ...), custom_call_target="tpu_custom_call" | custom-call | flops 99999997952 | bytes 6000000 | tf_op jit(solution)/shard_map/pool_grads/pallas_call | solution.py:366
  122.8 1.1 unpack_heads.2
  123.9 11.0 %all-to-all-done.2.y_ref = bf16[32,136,128]{2,1,0:T(8,128)(2,1)S(1)} async-done(((bf16[32,136,128]{2,1,0:T(8,128)(2,1)}), bf16[32,136,128]{2,1,0:T(8,128)(2,1)S(1)}, u32[]{:S(2)}, u32[]{:S(2)}) %all-to-all-start.2) | async-done | bytes 1114144 | tf_op jit(solution)/shard_map/all_to_all | solution.py:457
  134.8 1.7 %unpack_heads.3 = (bf16[1,2,64,4096]{3,2,1,0:T(8,128)(2,1)}, f32[32,192]{1,0:T(8,128)}) custom-call(bf16[32,136,128]{2,1,0:T(8,128)(2,1)S(1)} %all-to-all-done.2.y_ref), custom_call_target="tpu_custom_call" | custom-call | tf_op jit(solution)/shard_map/unpack_heads/pallas_call | solution.py:439
  (34 shorter events, 2.6 us)
Async XLA Ops:
  2.7 17.4 %collective-permute-start = (bf16[8,128,128]{2,1,0:T(8,128)(2,1)}, bf16[8,128,128]{2,1,0:T(8,128)(2,1)S(1)}, u32[]{:S(2)}, u32[]{:S(2)}) collective-permute-start(bf16[8,128,128]{2,1,0:T(8,128)(2,1)} %get-tuple-element.41), channel_id=1, source_target_pairs={{0,8},{1,9},{2,10},{3,11},{4,12},{5,13},{6,14},{7,15},{8,16},{9,17... | collective-permute-start | bytes 786440 | tf_op jit(solution)/shard_map/ppermute | solution.py:179
  4.2 15.9 %collective-permute-start.1 = (bf16[8,128,128]{2,1,0:T(8,128)(2,1)}, bf16[8,128,128]{2,1,0:T(8,128)(2,1)}, u32[]{:S(2)}, u32[]{:S(2)}) collective-permute-start(bf16[8,128,128]{2,1,0:T(8,128)(2,1)} %get-tuple-element.42), channel_id=1, source_target_pairs={{0,16},{1,17},{2,18},{3,19},{4,20},{5,21},{6,22},{7,23},{8,24},{9,... | collective-permute-start | bytes 786440 | tf_op jit(solution)/shard_map/ppermute | solution.py:179
  7.0 13.2 %collective-permute-start.2 = (bf16[8,128,128]{2,1,0:T(8,128)(2,1)}, bf16[8,128,128]{2,1,0:T(8,128)(2,1)}, u32[]{:S(2)}, u32[]{:S(2)}) collective-permute-start(bf16[8,128,128]{2,1,0:T(8,128)(2,1)} %get-tuple-element.43), channel_id=1, source_target_pairs={{0,24},{1,25},{2,26},{3,27},{4,28},{5,29},{6,30},{7,31},{8,0},{9,1... | collective-permute-start | bytes 786440 | tf_op jit(solution)/shard_map/ppermute | solution.py:179
  11.2 40.2 %all-to-all-start = ((bf16[32,136,128]{2,1,0:T(8,128)(2,1)}), bf16[32,136,128]{2,1,0:T(8,128)(2,1)S(1)}, u32[]{:S(2)}, u32[]{:S(2)}) async-start(bf16[32,136,128]{2,1,0:T(8,128)(2,1)} %pack_queries.1), calls=%async_computation | async-start | bytes 2228224 | tf_op jit(solution)/shard_map/all_to_all | solution.py:457
  20.1 31.3 %copy-start = (bf16[1,32,128,128]{3,2,1,0:T(8,128)(2,1)S(1)}, bf16[1,32,128,128]{3,2,1,0:T(8,128)(2,1)}, u32[]{:S(2)}) copy-start(bf16[1,32,128,128]{3,2,1,0:T(8,128)(2,1)} %keys_ref.5) | copy-start | bytes 3145732
  20.1 31.3 %copy-start.2 = (bf16[1,32,128,128]{3,2,1,0:T(8,128)(2,1)S(1)}, bf16[1,32,128,128]{3,2,1,0:T(8,128)(2,1)}, u32[]{:S(2)}) copy-start(bf16[1,32,128,128]{3,2,1,0:T(8,128)(2,1)} %values_ref.5) | copy-start | bytes 3145732
  20.1 31.2 %copy-start.5 = (f32[32,192]{1,0:T(8,128)S(1)}, f32[32,192]{1,0:T(8,128)}, u32[]{:S(2)}) copy-start(f32[32,192]{1,0:T(8,128)} %rel_ref.5) | copy-start | bytes 73732
  20.1 0.7 copy-start.10
  23.1 35.1 %collective-permute-start.4 = (bf16[4,128,128]{2,1,0:T(8,128)(2,1)}, bf16[4,128,128]{2,1,0:T(8,128)(2,1)S(1)}, u32[]{:S(2)}, u32[]{:S(2)}) collective-permute-start(bf16[4,128,128]{2,1,0:T(8,128)(2,1)} %get-tuple-element.52), channel_id=1, source_target_pairs={{0,2},{1,3},{2,4},{3,5},{4,6},{5,7},{6,0},{7,1},{8,10},{9,11},{10,... | collective-permute-start | bytes 393224 | tf_op jit(solution)/shard_map/ppermute | solution.py:179
  25.8 42.0 %collective-permute-start.5 = (bf16[4,128,128]{2,1,0:T(8,128)(2,1)}, bf16[4,128,128]{2,1,0:T(8,128)(2,1)S(1)}, u32[]{:S(2)}, u32[]{:S(2)}) collective-permute-start(bf16[4,128,128]{2,1,0:T(8,128)(2,1)} %get-tuple-element.53), channel_id=1, source_target_pairs={{0,3},{1,4},{2,5},{3,6},{4,7},{5,0},{6,1},{7,2},{8,11},{9,12},{10,... | collective-permute-start | bytes 393224 | tf_op jit(solution)/shard_map/ppermute | solution.py:179
  29.5 45.6 %collective-permute-start.6 = (bf16[4,128,128]{2,1,0:T(8,128)(2,1)}, bf16[4,128,128]{2,1,0:T(8,128)(2,1)}, u32[]{:S(2)}, u32[]{:S(2)}) collective-permute-start(bf16[4,128,128]{2,1,0:T(8,128)(2,1)} %get-tuple-element.54), channel_id=1, source_target_pairs={{0,4},{1,5},{2,6},{3,7},{4,0},{5,1},{6,2},{7,3},{8,12},{9,13},{10,... | collective-permute-start | bytes 393224 | tf_op jit(solution)/shard_map/ppermute | solution.py:179
  30.9 44.2 %collective-permute-start.7 = (bf16[4,128,128]{2,1,0:T(8,128)(2,1)}, bf16[4,128,128]{2,1,0:T(8,128)(2,1)}, u32[]{:S(2)}, u32[]{:S(2)}) collective-permute-start(bf16[4,128,128]{2,1,0:T(8,128)(2,1)} %get-tuple-element.55), channel_id=1, source_target_pairs={{0,5},{1,6},{2,7},{3,0},{4,1},{5,2},{6,3},{7,4},{8,13},{9,14},{10,... | collective-permute-start | bytes 393224 | tf_op jit(solution)/shard_map/ppermute | solution.py:179
  35.0 40.2 %collective-permute-start.8 = (bf16[4,128,128]{2,1,0:T(8,128)(2,1)}, bf16[4,128,128]{2,1,0:T(8,128)(2,1)}, u32[]{:S(2)}, u32[]{:S(2)}) collective-permute-start(bf16[4,128,128]{2,1,0:T(8,128)(2,1)} %get-tuple-element.56), channel_id=1, source_target_pairs={{0,6},{1,7},{2,0},{3,1},{4,2},{5,3},{6,4},{7,5},{8,14},{9,15},{10,... | collective-permute-start | bytes 393224 | tf_op jit(solution)/shard_map/ppermute | solution.py:179
  58.2 19.1 %copy-start.6 = (f32[32,192]{1,0:T(8,128)S(1)}, f32[32,192]{1,0:T(8,128)}, u32[]{:S(2)}) copy-start(f32[32,192]{1,0:T(8,128)} %rel_ref.5) | copy-start | bytes 73732
  58.2 16.9 %collective-permute-start.3 = (bf16[4,128,128]{2,1,0:T(8,128)(2,1)}, bf16[4,128,128]{2,1,0:T(8,128)(2,1)}, u32[]{:S(2)}, u32[]{:S(2)}) collective-permute-start(bf16[4,128,128]{2,1,0:T(8,128)(2,1)} %get-tuple-element.51), channel_id=1, source_target_pairs={{0,1},{1,2},{2,3},{3,4},{4,5},{5,6},{6,7},{7,0},{8,9},{9,10},{10,1... | collective-permute-start | bytes 393224 | tf_op jit(solution)/shard_map/ppermute | solution.py:179
  67.8 9.5 %collective-permute-start.9 = (bf16[4,128,128]{2,1,0:T(8,128)(2,1)}, bf16[4,128,128]{2,1,0:T(8,128)(2,1)}, u32[]{:S(2)}, u32[]{:S(2)}) collective-permute-start(bf16[4,128,128]{2,1,0:T(8,128)(2,1)} %get-tuple-element.57), channel_id=1, source_target_pairs={{0,7},{1,0},{2,1},{3,2},{4,3},{5,4},{6,5},{7,6},{8,15},{9,8},{10,9... | collective-permute-start | bytes 393224 | tf_op jit(solution)/shard_map/ppermute | solution.py:179
  67.8 31.1 %all-to-all-start.1 = ((bf16[32,128,128]{2,1,0:T(8,128)(2,1)}), bf16[32,128,128]{2,1,0:T(8,128)(2,1)S(1)}, u32[]{:S(2)}, u32[]{:S(2)}) async-start(bf16[32,128,128]{2,1,0:T(8,128)(2,1)} %attention_forward.1), calls=%async_computation.1 | async-start | bytes 2097152 | tf_op jit(solution)/shard_map/all_to_all | solution.py:457
  77.3 1.2 copy-start.3
  78.5 0.9 copy-start.8
  88.3 1.2 collective-permute-start.10
  89.5 3.6 %collective-permute-start.11 = (f32[1,256]{1,0:T(1,128)S(1)}, f32[1,256]{1,0:T(1,128)S(1)}, u32[]{:S(2)}, u32[]{:S(2)}) collective-permute-start(f32[1,256]{1,0:T(1,128)S(1)} %add.9), channel_id=1, source_target_pairs={{0,64},{32,96},{64,0},{96,32},{128,192},{160,224},{192,128},{224,1... | collective-permute-start | bytes 3080 | tf_op jit(solution)/shard_map/ppermute | solution.py:452
  93.1 5.1 %collective-permute-start.12 = (f32[1,256]{1,0:T(1,128)S(1)}, f32[1,256]{1,0:T(1,128)S(1)}, u32[]{:S(2)}, u32[]{:S(2)}) collective-permute-start(f32[1,256]{1,0:T(1,128)S(1)} %add.10), channel_id=1, source_target_pairs={{0,128},{32,160},{64,192},{96,224},{128,0},{160,32},{192,64},{224,... | collective-permute-start | bytes 3080 | tf_op jit(solution)/shard_map/ppermute | solution.py:452
  98.9 36.0 %all-to-all-start.2 = ((bf16[32,136,128]{2,1,0:T(8,128)(2,1)}), bf16[32,136,128]{2,1,0:T(8,128)(2,1)S(1)}, u32[]{:S(2)}, u32[]{:S(2)}) async-start(bf16[32,136,128]{2,1,0:T(8,128)(2,1)} %add_bias_row.1), calls=%async_computation.2 | async-start | bytes 2228224 | tf_op jit(solution)/shard_map/all_to_all | solution.py:457
  106.5 1.2 copy-start.1
  107.7 1.2 copy-start.4
  109.0 0.8 copy-start.7
  109.7 0.9 copy-start.9

commit v4 on v3

--- a/solution.py
+++ b/solution.py
@@ -24,7 +24,6 @@
 HALF = CH_DEV * BLOCK
 EXTRA = 8
 PACK_HEADS = 8
-SRC_STEP = 4
 SCALE = 1.0 / math.sqrt(HEAD_DIM)
 
 NT = (((1,), (1,)), ((), ()))
@@ -59,11 +58,17 @@
     return copy
 
 
-def pack_queries_kernel(fetch_ref, slot_ref, q_ref, out_ref, q_buf, out_buf, in_sems, out_sems):
-    copies = []
+def pack_kernel(head_ref, fetch_ref, slot_ref, q_ref, g_ref, sent_ref, *refs):
+    part_refs = refs[:X_SIZE]
+    q_buf, g_buf, sent_buf, part_buf, q_sems, g_sems, sent_sems, part_sems = refs[X_SIZE:]
+    g_copies, q_copies, outs = [], [], []
+    for i in range(X_SIZE):
+        column = lax.rem(head_ref[0] // Z_SIZE + i, X_SIZE) * CHUNK_WIDTH
+        cols = pl.ds(pl.multiple_of(column, CHUNK_WIDTH), CHUNK_WIDTH)
+        g_copies.append(start(g_ref.at[0, :, :, cols], g_buf.at[i], g_sems.at[i]))
     for i in range(CHUNKS):
         cols = slice(i * CHUNK_WIDTH, (i + 1) * CHUNK_WIDTH)
-        copies.append(start(q_ref.at[0, :, :, cols], q_buf.at[:, :, cols], in_sems.at[i]))
+        q_copies.append(start(q_ref.at[0, :, :, cols], q_buf.at[:, :, cols], q_sems.at[i]))
     lane = lax.broadcasted_iota(jnp.int32, (EXTRA, 128), 1)
     ids = jnp.zeros((EXTRA, 128), jnp.int32)
     for c in range(CH_DEV):
@@ -71,72 +76,46 @@
             enc = fetch_ref[0, 0, slot_ref[0, c, n]]
             ids = jnp.where(lane == c * NEIGH + n, enc, ids)
     ids = ids.astype(F32).astype(BF16)
-    outs = []
+    for i in range(X_SIZE):
+        g_copies[i].wait()
+        for h in range(Z_SIZE):
+            for c in range(CH_DEV):
+                part_buf[i, h, block_rows(c)] = g_buf[i, c, :, head_columns(h)]
+        outs.append(start(part_buf.at[i], part_refs[i], part_sems.at[i]))
     for i in range(CHUNKS):
         heads = slice(i * PACK_HEADS, (i + 1) * PACK_HEADS)
-        copies[i].wait()
+        q_copies[i].wait()
         for h in range(i * PACK_HEADS, (i + 1) * PACK_HEADS):
             for c in range(CH_DEV):
-                out_buf[h, block_rows(c)] = q_buf[c, :, head_columns(h)]
-            out_buf[h, HALF:] = ids
-        outs.append(start(out_buf.at[heads], out_ref.at[heads], out_sems.at[i]))
+                sent_buf[h, block_rows(c)] = q_buf[c, :, head_columns(h)]
+            sent_buf[h, HALF:] = ids
+        outs.append(start(sent_buf.at[heads], sent_ref.at[heads], sent_sems.at[i]))
     for copy in outs:
         copy.wait()
 
 
-def pack_queries(fetch_ids, slot_of, queries):
-    return pl.pallas_call(
-        pack_queries_kernel,
-        in_specs=[SMEM_SPEC, SMEM_SPEC, ANY_SPEC],
-        out_specs=ANY_SPEC,
-        out_shape=jax.ShapeDtypeStruct((HEADS, HALF + EXTRA, HEAD_DIM), BF16),
+def pack(head, fetch_ids, slot_of, queries, out_grad):
+    part = (Z_SIZE, HALF, HEAD_DIM)
+    sent = (HEADS, HALF + EXTRA, HEAD_DIM)
+    return pl.pallas_call(
+        pack_kernel,
+        in_specs=[SMEM_SPEC] * 3 + [ANY_SPEC] * 2,
+        out_specs=[ANY_SPEC] * (1 + X_SIZE),
+        out_shape=[jax.ShapeDtypeStruct(sent, BF16)] + [jax.ShapeDtypeStruct(part, BF16)] * X_SIZE,
         scratch_shapes=[
             pltpu.VMEM((CH_DEV, BLOCK, HD), BF16),
-            pltpu.VMEM((HEADS, HALF + EXTRA, HEAD_DIM), BF16),
+            pltpu.VMEM((X_SIZE, CH_DEV, BLOCK, CHUNK_WIDTH), BF16),
+            pltpu.VMEM(sent, BF16),
+            pltpu.VMEM((X_SIZE, *part), BF16),
             pltpu.SemaphoreType.DMA((CHUNKS,)),
+            pltpu.SemaphoreType.DMA((X_SIZE,)),
             pltpu.SemaphoreType.DMA((CHUNKS,)),
-        ],
-        compiler_params=vmem_limit(60),
-        cost_estimate=pl.CostEstimate(flops=10**11, bytes_accessed=2 * 10**6, transcendentals=0),
-        name="pack_queries",
-    )(fetch_ids, slot_of, queries)
-
-
-def pack_grads_kernel(head_ref, g_ref, *refs):
-    out_refs, (g_buf, out_buf, in_sems, out_sems) = refs[:X_SIZE], refs[X_SIZE:]
-    copies = []
-    for i in range(X_SIZE):
-        column = lax.rem(head_ref[0] // Z_SIZE + i, X_SIZE) * CHUNK_WIDTH
-        cols = pl.ds(pl.multiple_of(column, CHUNK_WIDTH), CHUNK_WIDTH)
-        copies.append(start(g_ref.at[0, :, :, cols], g_buf.at[i], in_sems.at[i]))
-    outs = []
-    for i in range(X_SIZE):
-        copies[i].wait()
-        for h in range(Z_SIZE):
-            for c in range(CH_DEV):
-                out_buf[i, h, block_rows(c)] = g_buf[i, c, :, head_columns(h)]
-        outs.append(start(out_buf.at[i], out_refs[i], out_sems.at[i]))
-    for copy in outs:
-        copy.wait()
-
-
-def pack_grads(head, out_grad):
-    shape = (Z_SIZE, HALF, HEAD_DIM)
-    return pl.pallas_call(
-        pack_grads_kernel,
-        in_specs=[SMEM_SPEC, ANY_SPEC],
-        out_specs=[ANY_SPEC] * X_SIZE,
-        out_shape=[jax.ShapeDtypeStruct(shape, BF16)] * X_SIZE,
-        scratch_shapes=[
-            pltpu.VMEM((X_SIZE, CH_DEV, BLOCK, CHUNK_WIDTH), BF16),
-            pltpu.VMEM((X_SIZE, *shape), BF16),
-            pltpu.SemaphoreType.DMA((X_SIZE,)),
             pltpu.SemaphoreType.DMA((X_SIZE,)),
         ],
         compiler_params=vmem_limit(60),
-        cost_estimate=pl.CostEstimate(flops=0, bytes_accessed=2 * 10**6, transcendentals=0),
-        name="pack_grads",
-    )(head, out_grad)
+        cost_estimate=pl.CostEstimate(flops=10**11, bytes_accessed=4 * 10**6, transcendentals=0),
+        name="pack_heads",
+    )(head, fetch_ids, slot_of, queries, out_grad)
 
 
 def regroup_kernel(head_ref, *refs):
@@ -206,13 +185,18 @@
     return copy
 
 
-BLOCKS_STEP = [(s, c) for s in range(SRC_STEP) for c in range(CH_DEV)]
+WIDE = 2 * X_SIZE
+
+
+def blocks_of(sources):
+    return [(s, c) for s in range(len(sources)) for c in range(CH_DEV)]
 
 
 def softmax_parts(sources, ids_smem, bias_ref, x_ref, keys_ref, values_ref):
     bias = bias_ref[...]
-    ids = [[ids_smem[sources[s], c * NEIGH + n] for n in range(NEIGH)] for s, c in BLOCKS_STEP]
-    q = [x_ref[sources[s], block_rows(c)] for s, c in BLOCKS_STEP]
+    blocks = blocks_of(sources)
+    ids = [[ids_smem[sources[s], c * NEIGH + n] for n in range(NEIGH)] for s, c in blocks]
+    q = [x_ref[sources[s], block_rows(c)] for s, c in blocks]
     k = [jnp.concatenate([keys_ref[0, i] for i in pair], axis=0) for pair in ids]
     v = [jnp.concatenate([values_ref[0, i] for i in pair], axis=0) for pair in ids]
     scores = [lax.dot_general(a, b, NT, preferred_element_type=F32) for a, b in zip(q, k)]
@@ -232,33 +216,34 @@
     copy.wait()
 
     def step(t, carry):
-        sources = [t * SRC_STEP + s for s in range(SRC_STEP)]
+        sources = [t * WIDE + s for s in range(WIDE)]
         ids, q, k, v, probs = softmax_parts(
             sources, ids_smem, bias_ref, x_ref, keys_ref, values_ref
         )
-        for i, (s, c) in enumerate(BLOCKS_STEP):
+        for i, (s, c) in enumerate(blocks_of(sources)):
             attended = jnp.dot(probs[i].astype(BF16), v[i], preferred_element_type=F32)
             y_ref[sources[s], block_rows(c)] = attended.astype(BF16)
         return carry
 
-    lax.fori_loop(0, N_BLOCK // SRC_STEP, step, 0)
+    lax.fori_loop(0, N_BLOCK // WIDE, step, 0)
 
 
 def near_sources(index, t):
     x, z = index // Z_SIZE, lax.rem(index, Z_SIZE)
     z_source = lax.rem(z + Z_SIZE - t, Z_SIZE)
-    return [lax.rem(x + X_SIZE - s, X_SIZE) * Z_SIZE + z_source for s in range(SRC_STEP)]
-
-
-def score_grads(sources, t, ids_smem, bias_ref, x_ref, g_buf, keys_ref, values_ref):
+    return [lax.rem(x + X_SIZE - s, X_SIZE) * Z_SIZE + z_source for s in range(X_SIZE)]
+
+
+def score_grads(index, times, ids_smem, bias_ref, x_ref, g_buf, keys_ref, values_ref):
+    sources = [source for t in times for source in near_sources(index, t)]
     ids, q, k, v, probs = softmax_parts(
         sources, ids_smem, bias_ref, x_ref, keys_ref, values_ref
     )
-    g = [g_buf[t, s, block_rows(c)] for s, c in BLOCKS_STEP]
+    g = [g_buf[times[s // X_SIZE], s % X_SIZE, block_rows(c)] for s, c in blocks_of(sources)]
     dprobs = [lax.dot_general(a, b, NT, preferred_element_type=F32) for a, b in zip(g, v)]
     inner = [jnp.sum(a * b, axis=-1, keepdims=True) for a, b in zip(probs, dprobs)]
     dscores = [a * (b - c) for a, b, c in zip(probs, dprobs, inner)]
-    return ids, q, k, g, probs, dscores
+    return sources, ids, q, k, g, probs, dscores
 
 
 def query_grad_kernel(head_ref, x_ref, keys_ref, values_ref, rel_ref, *refs):
@@ -273,18 +258,17 @@
         g_copy.wait()
 
     def step(t, carry):
-        sources = near_sources(head_ref[0], t)
-        _, _, k, _, _, dscores = score_grads(
-            sources, t, ids_smem, bias_ref, x_ref, g_buf, keys_ref, values_ref
+        sources, _, _, k, _, _, dscores = score_grads(
+            head_ref[0], [2 * t, 2 * t + 1], ids_smem, bias_ref, x_ref, g_buf, keys_ref, values_ref
         )
         dsum_ref[...] += sum(dscores)
-        for i, (s, c) in enumerate(BLOCKS_STEP):
+        for i, (s, c) in enumerate(blocks_of(sources)):
             low = dscores[i].astype(BF16)
             query_grad = jnp.dot(low, k[i], preferred_element_type=F32) * SCALE
             y_ref[sources[s], block_rows(c)] = query_grad.astype(BF16)
         return carry
 
-    lax.fori_loop(0, Z_SIZE, step, 0)
+    lax.fori_loop(0, Z_SIZE // 2, step, 0)
     bias_out[...] = fold_bias(dsum_ref[...])
 
 
@@ -301,15 +285,14 @@
         g_copy.wait()
 
     def step(t, carry):
-        sources = near_sources(head_ref[0], t)
-        ids, q, _, g, probs, dscores = score_grads(
-            sources, t, ids_smem, bias_ref, x_ref, g_buf, keys_ref, values_ref
+        _, ids, q, _, g, probs, dscores = score_grads(
+            head_ref[0], [t], ids_smem, bias_ref, x_ref, g_buf, keys_ref, values_ref
         )
         dscores_low = [a.astype(BF16) for a in dscores]
         probs_low = [a.astype(BF16) for a in probs]
         dk = [lax.dot_general(a, b, TN, preferred_element_type=F32) for a, b in zip(dscores_low, q)]
         dv = [lax.dot_general(a, b, TN, preferred_element_type=F32) for a, b in zip(probs_low, g)]
-        for i in range(len(BLOCKS_STEP)):
+        for i in range(len(ids)):
             for n in range(NEIGH):
                 rows = slice(n * NBLEN, (n + 1) * NBLEN)
                 dk_ref[ids[i][n]] += dk[i][rows]
@@ -448,9 +431,12 @@
 
 
 def sum_groups(part):
-    for hop in (1, 2, 4):
-        part = part + lax.ppermute(part, "dp", [(d, d ^ hop) for d in range(N_DP)])
-    return part
+    def swap(value, hop):
+        return lax.ppermute(value, "dp", [(d, d ^ hop) for d in range(N_DP)])
+
+    part = part + swap(part, 1)
+    other, third, fourth = swap(part, 2), swap(part, 4), swap(part, 6)
+    return (part + other) + (third + fourth)
 
 
 def all_to_all(parts):
@@ -459,15 +445,13 @@
 
 def on_device(queries, keys_pool, values_pool, rel_bias, out_grad, fetch_ids, slot_of):
     head = lax.axis_index("block").astype(jnp.int32).reshape(1)
-    parts = pack_grads(head, out_grad)
-    queries, *parts = lax.optimization_barrier((queries, *parts))
+    sent, *parts = pack(head, fetch_ids, slot_of, queries, out_grad)
     parts = [parts[0]] + [send_by(parts[dx], dx, 0) for dx in range(1, X_SIZE)]
-    sent = pack_queries(fetch_ids, slot_of, queries)
     recv = all_to_all(sent)
     grads = list(regroup(head, parts))
     recv, grads[0] = lax.optimization_barrier((recv, grads[0]))
     y = forward(head, recv, keys_pool, values_pool, rel_bias)
-    y, grads[1], grads[7] = lax.optimization_barrier((y, grads[1], grads[7]))
+    y, grads[3], grads[5] = lax.optimization_barrier((y, grads[3], grads[5]))
     grads = [grads[0]] + [send_by(grads[dz], 0, dz) for dz in range(1, Z_SIZE)]
     back_y = all_to_all(y)
     recv, _ = lax.optimization_barrier((recv, y))

time: 137 us -> 133 us (0.971)
  Pallas kernels: 38.3 us -> 34.1 us
  waiting for transfers between devices: 34.7 us -> 32.6 us
    ppermute x3 -> x4, waiting for transfers between devices: 8.16 us -> 3.95 us  [swap(): return lax.ppermute(value, 'dp', [(d, d ^ hop) for d in range(N_DP)])]
    ppermute x10, starting transfers between devices: 30.3 us -> 26.7 us  [send_by(): return lax.ppermute(part, 'block', pairs)]
    ppermute x3 -> x4, starting transfers between devices: 1.7 us -> 4.19 us  [swap(): return lax.ppermute(value, 'dp', [(d, d ^ hop) for d in range(N_DP)])]
    ppermute x10, waiting for transfers between devices: 2.2 us -> 4.22 us  [send_by(): return lax.ppermute(part, 'block', pairs)]
    all_to_all x3, starting transfers between devices: 23.8 us -> 25.4 us  [all_to_all(): lax.all_to_all(parts, 'block', split_axis=0, concat_axis=0, tiled=True)]
    pallas_call x1, Pallas kernels: 6.83 us -> 5.29 us  [forward(): pl.pallas_call(forward_kernel, in_specs=[SMEM_SPEC] + [VMEM_SPEC] * 4, ou...]
    pallas_call x1, Pallas kernels: 8.84 us -> 7.39 us  [query_grads(): pl.pallas_call(query_grad_kernel, in_specs=[SMEM_SPEC] + [VMEM_SPEC] * 4...]
    pallas_call x2 -> x1, Pallas kernels: 4.79 us -> 3.38 us  [pack(): pl.pallas_call(pack_kernel, in_specs=[SMEM_SPEC] * 3 + [ANY_SPEC] * 2, ou...]
  transfers between devices with their start and end apart: 16 -> 17, of which waited for: 6 -> 9; matrix products, arithmetic and copies ran while one was open for 0% -> 0% of each run, Pallas kernels for 25% -> 22%
where the time goes in v4:
time: 133 us; the launch traced here: 132 us
  starting transfers between devices  56.3 us (42%)
  Pallas kernels  34.1 us (26%)
  waiting for transfers between devices  32.6 us (25%)
  local copies, waits for them, and re-layouts  7.66 us (6%)
    ppermute x10, starting transfers between devices, send_by(): return lax.ppermute(part, 'block', pairs)  26.7 us
    all_to_all x3, starting transfers between devices, all_to_all(): lax.all_to_all(parts, 'block', split_axis=0, concat_axis=0, tiled=True)  25.4 us
    all_to_all x3, waiting for transfers between devices, all_to_all(): lax.all_to_all(parts, 'block', split_axis=0, concat_axis=0, tiled=True)  24.4 us
    pallas_call x1, Pallas kernels, pool_grads(): pl.pallas_call(pool_grad_kernel, in_specs=[SMEM_SPEC] + [VMEM_SPEC] * 4 +...  12.2 us
    unnamed x26, local copies, waits for them, and re-layouts  7.66 us
    pallas_call x1, Pallas kernels, query_grads(): pl.pallas_call(query_grad_kernel, in_specs=[SMEM_SPEC] + [VMEM_SPEC] * 4...  7.39 us
    pallas_call x1, Pallas kernels, forward(): pl.pallas_call(forward_kernel, in_specs=[SMEM_SPEC] + [VMEM_SPEC] * 4, ou...  5.29 us
    ppermute x10, waiting for transfers between devices, send_by(): return lax.ppermute(part, 'block', pairs)  4.22 us
  transfers between devices with their start and end apart: 17, of which 9 were waited for; matrix products, arithmetic and copies ran while one was open for 0% of the time, Pallas kernels for 22%

profile of v4, /device:TPU:16, one launch (start us, length us, event | category | flops | bytes accessed | tf_op | source)
XLA Modules:
  0.0 131.6 jit_solution(1260258054318983163)
XLA Ops:
  0.6 3.4 %pack_heads.1 = (bf16[32,136,128]{2,1,0:T(8,128)(2,1)}, bf16[8,128,128]{2,1,0:T(8,128)(2,1)}, bf16[8,128,128]{2,1,0:T(8,128)(2,1)}, bf16[8,128,128]{2,1,0:T(8,128)(2,1)}, bf16[8,128,128]{2,1,0:T(8,128)(2,1)}) custom-call(s32[1]{0:T(128)} %bitcast.head_ref, s32[1,1,3]{2,1,0:T(1,128)} %fetch_ref.1, s32[1,2,2]{2,1,0:T(2,128)} %slot_ref.1, ...), custom_call_target="tpu_custom_call" | custom-call | flops 99999997952 | bytes 4000000 | tf_op jit(solution)/shard_map/pack_heads/pallas_call | solution.py:100
  4.0 1.6 %collective-permute-start = (bf16[8,128,128]{2,1,0:T(8,128)(2,1)}, bf16[8,128,128]{2,1,0:T(8,128)(2,1)S(1)}, u32[]{:S(2)}, u32[]{:S(2)}) collective-permute-start(bf16[8,128,128]{2,1,0:T(8,128)(2,1)} %get-tuple-element.33), channel_id=1, source_target_pairs={{0,8},{1,9},{2,10},{3,11},{4,12},{5,13},{6,14},{7,15},{8,16},{9,17... | collective-permute-start | bytes 786440 | tf_op jit(solution)/shard_map/ppermute | solution.py:158
  5.6 2.7 %collective-permute-start.1 = (bf16[8,128,128]{2,1,0:T(8,128)(2,1)}, bf16[8,128,128]{2,1,0:T(8,128)(2,1)S(1)}, u32[]{:S(2)}, u32[]{:S(2)}) collective-permute-start(bf16[8,128,128]{2,1,0:T(8,128)(2,1)} %get-tuple-element.34), channel_id=1, source_target_pairs={{0,16},{1,17},{2,18},{3,19},{4,20},{5,21},{6,22},{7,23},{8,24},{9,... | collective-permute-start | bytes 786440 | tf_op jit(solution)/shard_map/ppermute | solution.py:158
  8.3 1.4 %collective-permute-start.2 = (bf16[8,128,128]{2,1,0:T(8,128)(2,1)}, bf16[8,128,128]{2,1,0:T(8,128)(2,1)S(1)}, u32[]{:S(2)}, u32[]{:S(2)}) collective-permute-start(bf16[8,128,128]{2,1,0:T(8,128)(2,1)} %get-tuple-element.35), channel_id=1, source_target_pairs={{0,24},{1,25},{2,26},{3,27},{4,28},{5,29},{6,30},{7,31},{8,0},{9,1... | collective-permute-start | bytes 786440 | tf_op jit(solution)/shard_map/ppermute | solution.py:158
  9.8 8.9 %all-to-all-start = ((bf16[32,136,128]{2,1,0:T(8,128)(2,1)}), bf16[32,136,128]{2,1,0:T(8,128)(2,1)S(1)}, u32[]{:S(2)}, u32[]{:S(2)}) async-start(bf16[32,136,128]{2,1,0:T(8,128)(2,1)} %get-tuple-element.31), calls=%async_computation | async-start | bytes 2228224 | tf_op jit(solution)/shard_map/all_to_all | solution.py:443
  18.7 1.5 %collective-permute-done.1.refs_2_ = bf16[8,128,128]{2,1,0:T(8,128)(2,1)S(1)} collective-permute-done((bf16[8,128,128]{2,1,0:T(8,128)(2,1)}, bf16[8,128,128]{2,1,0:T(8,128)(2,1)S(1)}, u32[]{:S(2)}, u32[]{:S(2)}) %collective-permute-start.1) | collective-permute-done | bytes 262176 | tf_op jit(solution)/shard_map/ppermute | solution.py:158
  21.6 2.4 %regroup_grads.1 = (bf16[4,128,128]{2,1,0:T(8,128)(2,1)}, bf16[4,128,128]{2,1,0:T(8,128)(2,1)}, bf16[4,128,128]{2,1,0:T(8,128)(2,1)}, bf16[4,128,128]{2,1,0:T(8,...) custom-call(s32[1]{0:T(128)} %bitcast.head_ref, ...), custom_call_target="tpu_custom_call" | custom-call | flops 99999997952 | bytes 2000000 | tf_op jit(solution)/shard_map/regroup_grads/pallas_call | solution.py:136
  24.0 2.0 %collective-permute-start.3 = (bf16[4,128,128]{2,1,0:T(8,128)(2,1)}, bf16[4,128,128]{2,1,0:T(8,128)(2,1)S(1)}, u32[]{:S(2)}, u32[]{:S(2)}) collective-permute-start(bf16[4,128,128]{2,1,0:T(8,128)(2,1)} %get-tuple-element.43), channel_id=1, source_target_pairs={{0,1},{1,2},{2,3},{3,4},{4,5},{5,6},{6,7},{7,0},{8,9},{9,10},{10,1... | collective-permute-start | bytes 393224 | tf_op jit(solution)/shard_map/ppermute | solution.py:158
  26.0 4.1 %collective-permute-start.4 = (bf16[4,128,128]{2,1,0:T(8,128)(2,1)}, bf16[4,128,128]{2,1,0:T(8,128)(2,1)S(1)}, u32[]{:S(2)}, u32[]{:S(2)}) collective-permute-start(bf16[4,128,128]{2,1,0:T(8,128)(2,1)} %get-tuple-element.44), channel_id=1, source_target_pairs={{0,2},{1,3},{2,4},{3,5},{4,6},{5,7},{6,0},{7,1},{8,10},{9,11},{10,... | collective-permute-start | bytes 393224 | tf_op jit(solution)/shard_map/ppermute | solution.py:158
  30.1 5.0 %collective-permute-start.6 = (bf16[4,128,128]{2,1,0:T(8,128)(2,1)}, bf16[4,128,128]{2,1,0:T(8,128)(2,1)}, u32[]{:S(2)}, u32[]{:S(2)}) collective-permute-start(bf16[4,128,128]{2,1,0:T(8,128)(2,1)} %get-tuple-element.46), channel_id=1, source_target_pairs={{0,4},{1,5},{2,6},{3,7},{4,0},{5,1},{6,2},{7,3},{8,12},{9,13},{10,... | collective-permute-start | bytes 393224 | tf_op jit(solution)/shard_map/ppermute | solution.py:158
  35.2 2.9 %collective-permute-start.8 = (bf16[4,128,128]{2,1,0:T(8,128)(2,1)}, bf16[4,128,128]{2,1,0:T(8,128)(2,1)}, u32[]{:S(2)}, u32[]{:S(2)}) collective-permute-start(bf16[4,128,128]{2,1,0:T(8,128)(2,1)} %get-tuple-element.48), channel_id=1, source_target_pairs={{0,6},{1,7},{2,0},{3,1},{4,2},{5,3},{6,4},{7,5},{8,14},{9,15},{10,... | collective-permute-start | bytes 393224 | tf_op jit(solution)/shard_map/ppermute | solution.py:158
  38.0 1.4 %collective-permute-start.9 = (bf16[4,128,128]{2,1,0:T(8,128)(2,1)}, bf16[4,128,128]{2,1,0:T(8,128)(2,1)}, u32[]{:S(2)}, u32[]{:S(2)}) collective-permute-start(bf16[4,128,128]{2,1,0:T(8,128)(2,1)} %get-tuple-element.49), channel_id=1, source_target_pairs={{0,7},{1,0},{2,1},{3,2},{4,3},{5,4},{6,5},{7,6},{8,15},{9,8},{10,9... | collective-permute-start | bytes 393224 | tf_op jit(solution)/shard_map/ppermute | solution.py:158
  39.4 9.6 %all-to-all-done.x_ref = bf16[32,136,128]{2,1,0:T(8,128)(2,1)S(1)} async-done(((bf16[32,136,128]{2,1,0:T(8,128)(2,1)}), bf16[32,136,128]{2,1,0:T(8,128)(2,1)S(1)}, u32[]{:S(2)}, u32[]{:S(2)}) %all-to-all-start) | async-done | bytes 1114144 | tf_op jit(solution)/shard_map/all_to_all | solution.py:443
  49.0 5.3 %attention_forward.1 = bf16[32,128,128]{2,1,0:T(8,128)(2,1)} custom-call(s32[1]{0:T(128)} %bitcast.head_ref, bf16[32,136,128]{2,1,0:T(8,128)(2,1)S(1)} %all-to-all-done.x_ref, bf16[1,32,128,128]{3,2,1,0:T(8,128)(2,1)S(1)} %copy-done, bf16[1,32,128,128]{3,2,1,0:T(8,128)(2,1)S(1)} %copy-done.2, f32[32,192]{1,0:T(8,128)S(1)} %copy-done.5), custom_call_target="tpu_custom_call" | custom-call | flops 99999997952 | bytes 4000000 | tf_op jit(solution)/shard_map/attention_forward/pallas_call | solution.py:313
  54.4 3.3 %collective-permute-start.5 = (bf16[4,128,128]{2,1,0:T(8,128)(2,1)}, bf16[4,128,128]{2,1,0:T(8,128)(2,1)}, u32[]{:S(2)}, u32[]{:S(2)}) collective-permute-start(bf16[4,128,128]{2,1,0:T(8,128)(2,1)} %get-tuple-element.45), channel_id=1, source_target_pairs={{0,3},{1,4},{2,5},{3,6},{4,7},{5,0},{6,1},{7,2},{8,11},{9,12},{10,... | collective-permute-start | bytes 393224 | tf_op jit(solution)/shard_map/ppermute | solution.py:158
  57.8 2.4 %collective-permute-start.7 = (bf16[4,128,128]{2,1,0:T(8,128)(2,1)}, bf16[4,128,128]{2,1,0:T(8,128)(2,1)}, u32[]{:S(2)}, u32[]{:S(2)}) collective-permute-start(bf16[4,128,128]{2,1,0:T(8,128)(2,1)} %get-tuple-element.47), channel_id=1, source_target_pairs={{0,5},{1,6},{2,7},{3,0},{4,1},{5,2},{6,3},{7,4},{8,13},{9,14},{10,... | collective-permute-start | bytes 393224 | tf_op jit(solution)/shard_map/ppermute | solution.py:158
  60.2 7.8 %all-to-all-start.1 = ((bf16[32,128,128]{2,1,0:T(8,128)(2,1)}), bf16[32,128,128]{2,1,0:T(8,128)(2,1)S(1)}, u32[]{:S(2)}, u32[]{:S(2)}) async-start(bf16[32,128,128]{2,1,0:T(8,128)(2,1)} %attention_forward.1), calls=%async_computation.1 | async-start | bytes 2097152 | tf_op jit(solution)/shard_map/all_to_all | solution.py:443
  68.0 2.5 %collective-permute-done.5.refs_3_ = bf16[4,128,128]{2,1,0:T(8,128)(2,1)} collective-permute-done((bf16[4,128,128]{2,1,0:T(8,128)(2,1)}, bf16[4,128,128]{2,1,0:T(8,128)(2,1)}, u32[]{:S(2)}, u32[]{:S(2)}) %collective-permute-start.5) | collective-permute-done | bytes 131104 | tf_op jit(solution)/shard_map/ppermute | solution.py:158
  70.5 1.2 copy-done.3
  72.6 7.4 %query_grads.1 = (bf16[32,136,128]{2,1,0:T(8,128)(2,1)}, f32[1,256]{1,0:T(1,128)S(1)}) custom-call(s32[1]{0:T(128)} %bitcast.head_ref, bf16[32,136,128]{2,1,0:T(8,128)(2,1)S(1)} %all-to-all-done.x_ref, bf16[1,32,128,128]{3,2,1,0:T(8,128)(2,1)S(1)} %copy-done, bf16[1,32,128,128]{3,2,1,0:T(8,128)(2,1)S(1)} %copy-done.3, f32[32,192]{1,0:T(8,128)S(1)} %copy-done.6, ...), custom_call_target="tpu_custom_call" | custom-call | flops 99999997952 | bytes 5000000 | tf_op jit(solution)/shard_map/query_grads/pallas_call | solution.py:326
  80.1 1.1 collective-permute-done.10
  81.7 2.9 %collective-permute-start.12 = (f32[1,256]{1,0:T(1,128)S(1)}, f32[1,256]{1,0:T(1,128)S(1)}, u32[]{:S(2)}, u32[]{:S(2)}) collective-permute-start(f32[1,256]{1,0:T(1,128)S(1)} %add.12), channel_id=1, source_target_pairs={{0,128},{32,160},{64,192},{96,224},{128,0},{160,32},{192,64},{224,... | collective-permute-start | bytes 3080 | tf_op jit(solution)/shard_map/ppermute | solution.py:435
  85.3 1.4 %collective-permute-done.12 = f32[1,256]{1,0:T(1,128)S(1)} collective-permute-done((f32[1,256]{1,0:T(1,128)S(1)}, f32[1,256]{1,0:T(1,128)S(1)}, u32[]{:S(2)}, u32[]{:S(2)}) %collective-permute-start.12) | collective-permute-done | bytes 1056 | tf_op jit(solution)/shard_map/ppermute | solution.py:435
  86.8 1.4 %collective-permute-done.11 = f32[1,256]{1,0:T(1,128)S(1)} collective-permute-done((f32[1,256]{1,0:T(1,128)S(1)}, f32[1,256]{1,0:T(1,128)S(1)}, u32[]{:S(2)}, u32[]{:S(2)}) %collective-permute-start.11) | collective-permute-done | bytes 1056 | tf_op jit(solution)/shard_map/ppermute | solution.py:435
  88.8 3.1 %all-to-all-done.1.y_ref = bf16[32,128,128]{2,1,0:T(8,128)(2,1)S(1)} async-done(((bf16[32,128,128]{2,1,0:T(8,128)(2,1)}), bf16[32,128,128]{2,1,0:T(8,128)(2,1)S(1)}, u32[]{:S(2)}, u32[]{:S(2)}) %all-to-all-start.1) | async-done | bytes 1048608 | tf_op jit(solution)/shard_map/all_to_all | solution.py:443
  92.0 8.7 %all-to-all-start.2 = ((bf16[32,136,128]{2,1,0:T(8,128)(2,1)}), bf16[32,136,128]{2,1,0:T(8,128)(2,1)S(1)}, u32[]{:S(2)}, u32[]{:S(2)}) async-start(bf16[32,136,128]{2,1,0:T(8,128)(2,1)} %add_bias_row.1), calls=%async_computation.2 | async-start | bytes 2228224 | tf_op jit(solution)/shard_map/all_to_all | solution.py:443
  100.7 1.2 copy-done.1
  101.9 1.2 copy-done.4
  104.8 12.2 %pool_grads.1 = (bf16[1,32,128,128]{3,2,1,0:T(8,128)(2,1)}, bf16[1,32,128,128]{3,2,1,0:T(8,128)(2,1)}) custom-call(s32[1]{0:T(128)} %bitcast.head_ref, bf16[32,136,128]{2,1,0:T(8,128)(2,1)S(1)} %all-to-all-done.x_ref, bf16[1,32,128,128]{3,2,1,0:T(8,128)(2,1)S(1)} %copy-done.1, bf16[1,32,128,128]{3,2,1,0:T(8,128)(2,1)S(1)} %copy-done.4, ...), custom_call_target="tpu_custom_call" | custom-call | flops 99999997952 | bytes 6000000 | tf_op jit(solution)/shard_map/pool_grads/pallas_call | solution.py:349
  117.0 1.1 unpack_heads.2
  118.1 11.7 %all-to-all-done.2.y_ref = bf16[32,136,128]{2,1,0:T(8,128)(2,1)S(1)} async-done(((bf16[32,136,128]{2,1,0:T(8,128)(2,1)}), bf16[32,136,128]{2,1,0:T(8,128)(2,1)S(1)}, u32[]{:S(2)}, u32[]{:S(2)}) %all-to-all-start.2) | async-done | bytes 1114144 | tf_op jit(solution)/shard_map/all_to_all | solution.py:443
  129.8 1.7 %unpack_heads.3 = (bf16[1,2,64,4096]{3,2,1,0:T(8,128)(2,1)}, f32[32,192]{1,0:T(8,128)}) custom-call(bf16[32,136,128]{2,1,0:T(8,128)(2,1)S(1)} %all-to-all-done.2.y_ref), custom_call_target="tpu_custom_call" | custom-call | tf_op jit(solution)/shard_map/unpack_heads/pallas_call | solution.py:422
  (38 shorter events, 6.2 us)
Async XLA Ops:
  4.0 14.6 %collective-permute-start = (bf16[8,128,128]{2,1,0:T(8,128)(2,1)}, bf16[8,128,128]{2,1,0:T(8,128)(2,1)S(1)}, u32[]{:S(2)}, u32[]{:S(2)}) collective-permute-start(bf16[8,128,128]{2,1,0:T(8,128)(2,1)} %get-tuple-element.33), channel_id=1, source_target_pairs={{0,8},{1,9},{2,10},{3,11},{4,12},{5,13},{6,14},{7,15},{8,16},{9,17... | collective-permute-start | bytes 786440 | tf_op jit(solution)/shard_map/ppermute | solution.py:158
  5.6 14.6 %collective-permute-start.1 = (bf16[8,128,128]{2,1,0:T(8,128)(2,1)}, bf16[8,128,128]{2,1,0:T(8,128)(2,1)S(1)}, u32[]{:S(2)}, u32[]{:S(2)}) collective-permute-start(bf16[8,128,128]{2,1,0:T(8,128)(2,1)} %get-tuple-element.34), channel_id=1, source_target_pairs={{0,16},{1,17},{2,18},{3,19},{4,20},{5,21},{6,22},{7,23},{8,24},{9,... | collective-permute-start | bytes 786440 | tf_op jit(solution)/shard_map/ppermute | solution.py:158
  8.3 11.9 %collective-permute-start.2 = (bf16[8,128,128]{2,1,0:T(8,128)(2,1)}, bf16[8,128,128]{2,1,0:T(8,128)(2,1)S(1)}, u32[]{:S(2)}, u32[]{:S(2)}) collective-permute-start(bf16[8,128,128]{2,1,0:T(8,128)(2,1)} %get-tuple-element.35), channel_id=1, source_target_pairs={{0,24},{1,25},{2,26},{3,27},{4,28},{5,29},{6,30},{7,31},{8,0},{9,1... | collective-permute-start | bytes 786440 | tf_op jit(solution)/shard_map/ppermute | solution.py:158
  9.8 39.3 %all-to-all-start = ((bf16[32,136,128]{2,1,0:T(8,128)(2,1)}), bf16[32,136,128]{2,1,0:T(8,128)(2,1)S(1)}, u32[]{:S(2)}, u32[]{:S(2)}) async-start(bf16[32,136,128]{2,1,0:T(8,128)(2,1)} %get-tuple-element.31), calls=%async_computation | async-start | bytes 2228224 | tf_op jit(solution)/shard_map/all_to_all | solution.py:443
  18.7 2.9 %copy-start.10 = (bf16[8,128,128]{2,1,0:T(8,128)(2,1)}, bf16[8,128,128]{2,1,0:T(8,128)(2,1)S(1)}, u32[]{:S(2)}) copy-start(bf16[8,128,128]{2,1,0:T(8,128)(2,1)S(1)} %collective-permute-done.refs_1_) | copy-start | bytes 786436
  20.2 0.7 copy-start.11
  20.9 0.7 copy-start.12
  21.6 27.4 %copy-start = (bf16[1,32,128,128]{3,2,1,0:T(8,128)(2,1)S(1)}, bf16[1,32,128,128]{3,2,1,0:T(8,128)(2,1)}, u32[]{:S(2)}) copy-start(bf16[1,32,128,128]{3,2,1,0:T(8,128)(2,1)} %keys_ref.5) | copy-start | bytes 3145732
  21.6 27.4 %copy-start.2 = (bf16[1,32,128,128]{3,2,1,0:T(8,128)(2,1)S(1)}, bf16[1,32,128,128]{3,2,1,0:T(8,128)(2,1)}, u32[]{:S(2)}) copy-start(bf16[1,32,128,128]{3,2,1,0:T(8,128)(2,1)} %values_ref.5) | copy-start | bytes 3145732
  21.6 27.4 %copy-start.5 = (f32[32,192]{1,0:T(8,128)S(1)}, f32[32,192]{1,0:T(8,128)}, u32[]{:S(2)}) copy-start(f32[32,192]{1,0:T(8,128)} %rel_ref.5) | copy-start | bytes 73732
  24.0 30.3 %collective-permute-start.3 = (bf16[4,128,128]{2,1,0:T(8,128)(2,1)}, bf16[4,128,128]{2,1,0:T(8,128)(2,1)S(1)}, u32[]{:S(2)}, u32[]{:S(2)}) collective-permute-start(bf16[4,128,128]{2,1,0:T(8,128)(2,1)} %get-tuple-element.43), channel_id=1, source_target_pairs={{0,1},{1,2},{2,3},{3,4},{4,5},{5,6},{6,7},{7,0},{8,9},{9,10},{10,1... | collective-permute-start | bytes 393224 | tf_op jit(solution)/shard_map/ppermute | solution.py:158
  26.0 31.8 %collective-permute-start.4 = (bf16[4,128,128]{2,1,0:T(8,128)(2,1)}, bf16[4,128,128]{2,1,0:T(8,128)(2,1)S(1)}, u32[]{:S(2)}, u32[]{:S(2)}) collective-permute-start(bf16[4,128,128]{2,1,0:T(8,128)(2,1)} %get-tuple-element.44), channel_id=1, source_target_pairs={{0,2},{1,3},{2,4},{3,5},{4,6},{5,7},{6,0},{7,1},{8,10},{9,11},{10,... | collective-permute-start | bytes 393224 | tf_op jit(solution)/shard_map/ppermute | solution.py:158
  30.1 37.8 %collective-permute-start.6 = (bf16[4,128,128]{2,1,0:T(8,128)(2,1)}, bf16[4,128,128]{2,1,0:T(8,128)(2,1)}, u32[]{:S(2)}, u32[]{:S(2)}) collective-permute-start(bf16[4,128,128]{2,1,0:T(8,128)(2,1)} %get-tuple-element.46), channel_id=1, source_target_pairs={{0,4},{1,5},{2,6},{3,7},{4,0},{5,1},{6,2},{7,3},{8,12},{9,13},{10,... | collective-permute-start | bytes 393224 | tf_op jit(solution)/shard_map/ppermute | solution.py:158
  35.2 32.8 %collective-permute-start.8 = (bf16[4,128,128]{2,1,0:T(8,128)(2,1)}, bf16[4,128,128]{2,1,0:T(8,128)(2,1)}, u32[]{:S(2)}, u32[]{:S(2)}) collective-permute-start(bf16[4,128,128]{2,1,0:T(8,128)(2,1)} %get-tuple-element.48), channel_id=1, source_target_pairs={{0,6},{1,7},{2,0},{3,1},{4,2},{5,3},{6,4},{7,5},{8,14},{9,15},{10,... | collective-permute-start | bytes 393224 | tf_op jit(solution)/shard_map/ppermute | solution.py:158
  38.0 29.9 %collective-permute-start.9 = (bf16[4,128,128]{2,1,0:T(8,128)(2,1)}, bf16[4,128,128]{2,1,0:T(8,128)(2,1)}, u32[]{:S(2)}, u32[]{:S(2)}) collective-permute-start(bf16[4,128,128]{2,1,0:T(8,128)(2,1)} %get-tuple-element.49), channel_id=1, source_target_pairs={{0,7},{1,0},{2,1},{3,2},{4,3},{5,4},{6,5},{7,6},{8,15},{9,8},{10,9... | collective-permute-start | bytes 393224 | tf_op jit(solution)/shard_map/ppermute | solution.py:158
  54.3 16.1 %copy-start.6 = (f32[32,192]{1,0:T(8,128)S(1)}, f32[32,192]{1,0:T(8,128)}, u32[]{:S(2)}) copy-start(f32[32,192]{1,0:T(8,128)} %rel_ref.5) | copy-start | bytes 73732
  54.4 16.1 %collective-permute-start.5 = (bf16[4,128,128]{2,1,0:T(8,128)(2,1)}, bf16[4,128,128]{2,1,0:T(8,128)(2,1)}, u32[]{:S(2)}, u32[]{:S(2)}) collective-permute-start(bf16[4,128,128]{2,1,0:T(8,128)(2,1)} %get-tuple-element.45), channel_id=1, source_target_pairs={{0,3},{1,4},{2,5},{3,6},{4,7},{5,0},{6,1},{7,2},{8,11},{9,12},{10,... | collective-permute-start | bytes 393224 | tf_op jit(solution)/shard_map/ppermute | solution.py:158
  57.8 12.6 %collective-permute-start.7 = (bf16[4,128,128]{2,1,0:T(8,128)(2,1)}, bf16[4,128,128]{2,1,0:T(8,128)(2,1)}, u32[]{:S(2)}, u32[]{:S(2)}) collective-permute-start(bf16[4,128,128]{2,1,0:T(8,128)(2,1)} %get-tuple-element.47), channel_id=1, source_target_pairs={{0,5},{1,6},{2,7},{3,0},{4,1},{5,2},{6,3},{7,4},{8,13},{9,14},{10,... | collective-permute-start | bytes 393224 | tf_op jit(solution)/shard_map/ppermute | solution.py:158
  60.2 31.8 %all-to-all-start.1 = ((bf16[32,128,128]{2,1,0:T(8,128)(2,1)}), bf16[32,128,128]{2,1,0:T(8,128)(2,1)S(1)}, u32[]{:S(2)}, u32[]{:S(2)}) async-start(bf16[32,128,128]{2,1,0:T(8,128)(2,1)} %attention_forward.1), calls=%async_computation.1 | async-start | bytes 2097152 | tf_op jit(solution)/shard_map/all_to_all | solution.py:443
  70.5 1.2 copy-start.3
  71.7 0.9 copy-start.8
  80.0 1.2 collective-permute-start.10
  81.2 4.1 %collective-permute-start.13 = (f32[1,256]{1,0:T(1,128)S(1)}, f32[1,256]{1,0:T(1,128)S(1)}, u32[]{:S(2)}, u32[]{:S(2)}) collective-permute-start(f32[1,256]{1,0:T(1,128)S(1)} %add.12), channel_id=1, source_target_pairs={{0,192},{32,224},{64,128},{96,160},{128,64},{160,96},{192,0},{224,... | collective-permute-start | bytes 3080 | tf_op jit(solution)/shard_map/ppermute | solution.py:435
  81.7 5.1 %collective-permute-start.12 = (f32[1,256]{1,0:T(1,128)S(1)}, f32[1,256]{1,0:T(1,128)S(1)}, u32[]{:S(2)}, u32[]{:S(2)}) collective-permute-start(f32[1,256]{1,0:T(1,128)S(1)} %add.12), channel_id=1, source_target_pairs={{0,128},{32,160},{64,192},{96,224},{128,0},{160,32},{192,64},{224,... | collective-permute-start | bytes 3080 | tf_op jit(solution)/shard_map/ppermute | solution.py:435
  84.6 3.6 %collective-permute-start.11 = (f32[1,256]{1,0:T(1,128)S(1)}, f32[1,256]{1,0:T(1,128)S(1)}, u32[]{:S(2)}, u32[]{:S(2)}) collective-permute-start(f32[1,256]{1,0:T(1,128)S(1)} %add.12), channel_id=1, source_target_pairs={{0,64},{32,96},{64,0},{96,32},{128,192},{160,224},{192,128},{224,1... | collective-permute-start | bytes 3080 | tf_op jit(solution)/shard_map/ppermute | solution.py:435
  92.0 37.8 %all-to-all-start.2 = ((bf16[32,136,128]{2,1,0:T(8,128)(2,1)}), bf16[32,136,128]{2,1,0:T(8,128)(2,1)S(1)}, u32[]{:S(2)}, u32[]{:S(2)}) async-start(bf16[32,136,128]{2,1,0:T(8,128)(2,1)} %add_bias_row.1), calls=%async_computation.2 | async-start | bytes 2228224 | tf_op jit(solution)/shard_map/all_to_all | solution.py:443
  100.7 1.2 copy-start.1
  101.9 1.2 copy-start.4
  103.1 0.8 copy-start.7
  103.9 0.9 copy-start.9

commit v5 on v4

--- a/solution.py
+++ b/solution.py
@@ -259,7 +259,7 @@
 
     def step(t, carry):
         sources, _, _, k, _, _, dscores = score_grads(
-            head_ref[0], [2 * t, 2 * t + 1], ids_smem, bias_ref, x_ref, g_buf, keys_ref, values_ref
+            head_ref[0], [4 * t + u for u in range(4)], ids_smem, bias_ref, x_ref, g_buf, keys_ref, values_ref
         )
         dsum_ref[...] += sum(dscores)
         for i, (s, c) in enumerate(blocks_of(sources)):
@@ -268,7 +268,7 @@
             y_ref[sources[s], block_rows(c)] = query_grad.astype(BF16)
         return carry
 
-    lax.fori_loop(0, Z_SIZE // 2, step, 0)
+    lax.fori_loop(0, Z_SIZE // 4, step, 0)
     bias_out[...] = fold_bias(dsum_ref[...])
 
 

time: 133 us -> 133 us (level)
  no operation moved by 1% of the time
where the time goes in v5:
time: 133 us; the launch traced here: 131 us
  starting transfers between devices  55.7 us (42%)
  Pallas kernels  33.6 us (25%)
  waiting for transfers between devices  33.1 us (25%)
  local copies, waits for them, and re-layouts  7.66 us (6%)
    ppermute x10, starting transfers between devices, send_by(): return lax.ppermute(part, 'block', pairs)  26.7 us
    all_to_all x3, waiting for transfers between devices, all_to_all(): lax.all_to_all(parts, 'block', split_axis=0, concat_axis=0, tiled=True)  24.9 us
    all_to_all x3, starting transfers between devices, all_to_all(): lax.all_to_all(parts, 'block', split_axis=0, concat_axis=0, tiled=True)  24.8 us
    pallas_call x1, Pallas kernels, pool_grads(): pl.pallas_call(pool_grad_kernel, in_specs=[SMEM_SPEC] + [VMEM_SPEC] * 4 +...  12.2 us
    unnamed x26, local copies, waits for them, and re-layouts  7.66 us
    pallas_call x1, Pallas kernels, query_grads(): pl.pallas_call(query_grad_kernel, in_specs=[SMEM_SPEC] + [VMEM_SPEC] * 4...  6.86 us
    pallas_call x1, Pallas kernels, forward(): pl.pallas_call(forward_kernel, in_specs=[SMEM_SPEC] + [VMEM_SPEC] * 4, ou...  5.29 us
    ppermute x10, waiting for transfers between devices, send_by(): return lax.ppermute(part, 'block', pairs)  4.22 us
  transfers between devices with their start and end apart: 17, of which 9 were waited for; matrix products, arithmetic and copies ran while one was open for 0% of the time, Pallas kernels for 22%

profile of v5, /device:TPU:16, one launch (start us, length us, event | category | flops | bytes accessed | tf_op | source)
XLA Modules:
  0.0 131.1 jit_solution(291014225248668013)
XLA Ops:
  0.6 3.4 %pack_heads.1 = (bf16[32,136,128]{2,1,0:T(8,128)(2,1)}, bf16[8,128,128]{2,1,0:T(8,128)(2,1)}, bf16[8,128,128]{2,1,0:T(8,128)(2,1)}, bf16[8,128,128]{2,1,0:T(8,128)(2,1)}, bf16[8,128,128]{2,1,0:T(8,128)(2,1)}) custom-call(s32[1]{0:T(128)} %bitcast.head_ref, s32[1,1,3]{2,1,0:T(1,128)} %fetch_ref.1, s32[1,2,2]{2,1,0:T(2,128)} %slot_ref.1, ...), custom_call_target="tpu_custom_call" | custom-call | flops 99999997952 | bytes 4000000 | tf_op jit(solution)/shard_map/pack_heads/pallas_call | solution.py:100
  4.0 1.6 %collective-permute-start = (bf16[8,128,128]{2,1,0:T(8,128)(2,1)}, bf16[8,128,128]{2,1,0:T(8,128)(2,1)S(1)}, u32[]{:S(2)}, u32[]{:S(2)}) collective-permute-start(bf16[8,128,128]{2,1,0:T(8,128)(2,1)} %get-tuple-element.33), channel_id=1, source_target_pairs={{0,8},{1,9},{2,10},{3,11},{4,12},{5,13},{6,14},{7,15},{8,16},{9,17... | collective-permute-start | bytes 786440 | tf_op jit(solution)/shard_map/ppermute | solution.py:158
  5.6 2.7 %collective-permute-start.1 = (bf16[8,128,128]{2,1,0:T(8,128)(2,1)}, bf16[8,128,128]{2,1,0:T(8,128)(2,1)S(1)}, u32[]{:S(2)}, u32[]{:S(2)}) collective-permute-start(bf16[8,128,128]{2,1,0:T(8,128)(2,1)} %get-tuple-element.34), channel_id=1, source_target_pairs={{0,16},{1,17},{2,18},{3,19},{4,20},{5,21},{6,22},{7,23},{8,24},{9,... | collective-permute-start | bytes 786440 | tf_op jit(solution)/shard_map/ppermute | solution.py:158
  8.3 1.4 %collective-permute-start.2 = (bf16[8,128,128]{2,1,0:T(8,128)(2,1)}, bf16[8,128,128]{2,1,0:T(8,128)(2,1)S(1)}, u32[]{:S(2)}, u32[]{:S(2)}) collective-permute-start(bf16[8,128,128]{2,1,0:T(8,128)(2,1)} %get-tuple-element.35), channel_id=1, source_target_pairs={{0,24},{1,25},{2,26},{3,27},{4,28},{5,29},{6,30},{7,31},{8,0},{9,1... | collective-permute-start | bytes 786440 | tf_op jit(solution)/shard_map/ppermute | solution.py:158
  9.8 8.9 %all-to-all-start = ((bf16[32,136,128]{2,1,0:T(8,128)(2,1)}), bf16[32,136,128]{2,1,0:T(8,128)(2,1)S(1)}, u32[]{:S(2)}, u32[]{:S(2)}) async-start(bf16[32,136,128]{2,1,0:T(8,128)(2,1)} %get-tuple-element.31), calls=%async_computation | async-start | bytes 2228224 | tf_op jit(solution)/shard_map/all_to_all | solution.py:443
  18.7 1.5 %collective-permute-done.1.refs_2_ = bf16[8,128,128]{2,1,0:T(8,128)(2,1)S(1)} collective-permute-done((bf16[8,128,128]{2,1,0:T(8,128)(2,1)}, bf16[8,128,128]{2,1,0:T(8,128)(2,1)S(1)}, u32[]{:S(2)}, u32[]{:S(2)}) %collective-permute-start.1) | collective-permute-done | bytes 262176 | tf_op jit(solution)/shard_map/ppermute | solution.py:158
  21.6 2.4 %regroup_grads.1 = (bf16[4,128,128]{2,1,0:T(8,128)(2,1)}, bf16[4,128,128]{2,1,0:T(8,128)(2,1)}, bf16[4,128,128]{2,1,0:T(8,128)(2,1)}, bf16[4,128,128]{2,1,0:T(8,...) custom-call(s32[1]{0:T(128)} %bitcast.head_ref, ...), custom_call_target="tpu_custom_call" | custom-call | flops 99999997952 | bytes 2000000 | tf_op jit(solution)/shard_map/regroup_grads/pallas_call | solution.py:136
  24.0 2.0 %collective-permute-start.3 = (bf16[4,128,128]{2,1,0:T(8,128)(2,1)}, bf16[4,128,128]{2,1,0:T(8,128)(2,1)S(1)}, u32[]{:S(2)}, u32[]{:S(2)}) collective-permute-start(bf16[4,128,128]{2,1,0:T(8,128)(2,1)} %get-tuple-element.43), channel_id=1, source_target_pairs={{0,1},{1,2},{2,3},{3,4},{4,5},{5,6},{6,7},{7,0},{8,9},{9,10},{10,1... | collective-permute-start | bytes 393224 | tf_op jit(solution)/shard_map/ppermute | solution.py:158
  26.0 4.1 %collective-permute-start.4 = (bf16[4,128,128]{2,1,0:T(8,128)(2,1)}, bf16[4,128,128]{2,1,0:T(8,128)(2,1)S(1)}, u32[]{:S(2)}, u32[]{:S(2)}) collective-permute-start(bf16[4,128,128]{2,1,0:T(8,128)(2,1)} %get-tuple-element.44), channel_id=1, source_target_pairs={{0,2},{1,3},{2,4},{3,5},{4,6},{5,7},{6,0},{7,1},{8,10},{9,11},{10,... | collective-permute-start | bytes 393224 | tf_op jit(solution)/shard_map/ppermute | solution.py:158
  30.1 5.0 %collective-permute-start.6 = (bf16[4,128,128]{2,1,0:T(8,128)(2,1)}, bf16[4,128,128]{2,1,0:T(8,128)(2,1)}, u32[]{:S(2)}, u32[]{:S(2)}) collective-permute-start(bf16[4,128,128]{2,1,0:T(8,128)(2,1)} %get-tuple-element.46), channel_id=1, source_target_pairs={{0,4},{1,5},{2,6},{3,7},{4,0},{5,1},{6,2},{7,3},{8,12},{9,13},{10,... | collective-permute-start | bytes 393224 | tf_op jit(solution)/shard_map/ppermute | solution.py:158
  35.2 2.9 %collective-permute-start.8 = (bf16[4,128,128]{2,1,0:T(8,128)(2,1)}, bf16[4,128,128]{2,1,0:T(8,128)(2,1)}, u32[]{:S(2)}, u32[]{:S(2)}) collective-permute-start(bf16[4,128,128]{2,1,0:T(8,128)(2,1)} %get-tuple-element.48), channel_id=1, source_target_pairs={{0,6},{1,7},{2,0},{3,1},{4,2},{5,3},{6,4},{7,5},{8,14},{9,15},{10,... | collective-permute-start | bytes 393224 | tf_op jit(solution)/shard_map/ppermute | solution.py:158
  38.0 1.4 %collective-permute-start.9 = (bf16[4,128,128]{2,1,0:T(8,128)(2,1)}, bf16[4,128,128]{2,1,0:T(8,128)(2,1)}, u32[]{:S(2)}, u32[]{:S(2)}) collective-permute-start(bf16[4,128,128]{2,1,0:T(8,128)(2,1)} %get-tuple-element.49), channel_id=1, source_target_pairs={{0,7},{1,0},{2,1},{3,2},{4,3},{5,4},{6,5},{7,6},{8,15},{9,8},{10,9... | collective-permute-start | bytes 393224 | tf_op jit(solution)/shard_map/ppermute | solution.py:158
  39.4 9.6 %all-to-all-done.x_ref = bf16[32,136,128]{2,1,0:T(8,128)(2,1)S(1)} async-done(((bf16[32,136,128]{2,1,0:T(8,128)(2,1)}), bf16[32,136,128]{2,1,0:T(8,128)(2,1)S(1)}, u32[]{:S(2)}, u32[]{:S(2)}) %all-to-all-start) | async-done | bytes 1114144 | tf_op jit(solution)/shard_map/all_to_all | solution.py:443
  49.0 5.3 %attention_forward.1 = bf16[32,128,128]{2,1,0:T(8,128)(2,1)} custom-call(s32[1]{0:T(128)} %bitcast.head_ref, bf16[32,136,128]{2,1,0:T(8,128)(2,1)S(1)} %all-to-all-done.x_ref, bf16[1,32,128,128]{3,2,1,0:T(8,128)(2,1)S(1)} %copy-done, bf16[1,32,128,128]{3,2,1,0:T(8,128)(2,1)S(1)} %copy-done.2, f32[32,192]{1,0:T(8,128)S(1)} %copy-done.5), custom_call_target="tpu_custom_call" | custom-call | flops 99999997952 | bytes 4000000 | tf_op jit(solution)/shard_map/attention_forward/pallas_call | solution.py:313
  54.4 3.3 %collective-permute-start.5 = (bf16[4,128,128]{2,1,0:T(8,128)(2,1)}, bf16[4,128,128]{2,1,0:T(8,128)(2,1)}, u32[]{:S(2)}, u32[]{:S(2)}) collective-permute-start(bf16[4,128,128]{2,1,0:T(8,128)(2,1)} %get-tuple-element.45), channel_id=1, source_target_pairs={{0,3},{1,4},{2,5},{3,6},{4,7},{5,0},{6,1},{7,2},{8,11},{9,12},{10,... | collective-permute-start | bytes 393224 | tf_op jit(solution)/shard_map/ppermute | solution.py:158
  57.8 2.4 %collective-permute-start.7 = (bf16[4,128,128]{2,1,0:T(8,128)(2,1)}, bf16[4,128,128]{2,1,0:T(8,128)(2,1)}, u32[]{:S(2)}, u32[]{:S(2)}) collective-permute-start(bf16[4,128,128]{2,1,0:T(8,128)(2,1)} %get-tuple-element.47), channel_id=1, source_target_pairs={{0,5},{1,6},{2,7},{3,0},{4,1},{5,2},{6,3},{7,4},{8,13},{9,14},{10,... | collective-permute-start | bytes 393224 | tf_op jit(solution)/shard_map/ppermute | solution.py:158
  60.2 7.8 %all-to-all-start.1 = ((bf16[32,128,128]{2,1,0:T(8,128)(2,1)}), bf16[32,128,128]{2,1,0:T(8,128)(2,1)S(1)}, u32[]{:S(2)}, u32[]{:S(2)}) async-start(bf16[32,128,128]{2,1,0:T(8,128)(2,1)} %attention_forward.1), calls=%async_computation.1 | async-start | bytes 2097152 | tf_op jit(solution)/shard_map/all_to_all | solution.py:443
  68.0 2.5 %collective-permute-done.5.refs_3_ = bf16[4,128,128]{2,1,0:T(8,128)(2,1)} collective-permute-done((bf16[4,128,128]{2,1,0:T(8,128)(2,1)}, bf16[4,128,128]{2,1,0:T(8,128)(2,1)}, u32[]{:S(2)}, u32[]{:S(2)}) %collective-permute-start.5) | collective-permute-done | bytes 131104 | tf_op jit(solution)/shard_map/ppermute | solution.py:158
  70.5 1.2 copy-done.3
  72.6 6.9 %query_grads.1 = (bf16[32,136,128]{2,1,0:T(8,128)(2,1)}, f32[1,256]{1,0:T(1,128)S(1)}) custom-call(s32[1]{0:T(128)} %bitcast.head_ref, bf16[32,136,128]{2,1,0:T(8,128)(2,1)S(1)} %all-to-all-done.x_ref, bf16[1,32,128,128]{3,2,1,0:T(8,128)(2,1)S(1)} %copy-done, bf16[1,32,128,128]{3,2,1,0:T(8,128)(2,1)S(1)} %copy-done.3, f32[32,192]{1,0:T(8,128)S(1)} %copy-done.6, ...), custom_call_target="tpu_custom_call" | custom-call | flops 99999997952 | bytes 5000000 | tf_op jit(solution)/shard_map/query_grads/pallas_call | solution.py:326
  79.6 1.1 collective-permute-done.10
  81.2 2.9 %collective-permute-start.12 = (f32[1,256]{1,0:T(1,128)S(1)}, f32[1,256]{1,0:T(1,128)S(1)}, u32[]{:S(2)}, u32[]{:S(2)}) collective-permute-start(f32[1,256]{1,0:T(1,128)S(1)} %add.12), channel_id=1, source_target_pairs={{0,128},{32,160},{64,192},{96,224},{128,0},{160,32},{192,64},{224,... | collective-permute-start | bytes 3080 | tf_op jit(solution)/shard_map/ppermute | solution.py:435
  84.8 1.4 %collective-permute-done.12 = f32[1,256]{1,0:T(1,128)S(1)} collective-permute-done((f32[1,256]{1,0:T(1,128)S(1)}, f32[1,256]{1,0:T(1,128)S(1)}, u32[]{:S(2)}, u32[]{:S(2)}) %collective-permute-start.12) | collective-permute-done | bytes 1056 | tf_op jit(solution)/shard_map/ppermute | solution.py:435
  86.2 1.4 %collective-permute-done.11 = f32[1,256]{1,0:T(1,128)S(1)} collective-permute-done((f32[1,256]{1,0:T(1,128)S(1)}, f32[1,256]{1,0:T(1,128)S(1)}, u32[]{:S(2)}, u32[]{:S(2)}) %collective-permute-start.11) | collective-permute-done | bytes 1056 | tf_op jit(solution)/shard_map/ppermute | solution.py:435
  88.3 3.7 %all-to-all-done.1.y_ref = bf16[32,128,128]{2,1,0:T(8,128)(2,1)S(1)} async-done(((bf16[32,128,128]{2,1,0:T(8,128)(2,1)}), bf16[32,128,128]{2,1,0:T(8,128)(2,1)S(1)}, u32[]{:S(2)}, u32[]{:S(2)}) %all-to-all-start.1) | async-done | bytes 1048608 | tf_op jit(solution)/shard_map/all_to_all | solution.py:443
  92.0 8.2 %all-to-all-start.2 = ((bf16[32,136,128]{2,1,0:T(8,128)(2,1)}), bf16[32,136,128]{2,1,0:T(8,128)(2,1)S(1)}, u32[]{:S(2)}, u32[]{:S(2)}) async-start(bf16[32,136,128]{2,1,0:T(8,128)(2,1)} %add_bias_row.1), calls=%async_computation.2 | async-start | bytes 2228224 | tf_op jit(solution)/shard_map/all_to_all | solution.py:443
  100.2 1.2 copy-done.1
  101.4 1.2 copy-done.4
  104.3 12.2 %pool_grads.1 = (bf16[1,32,128,128]{3,2,1,0:T(8,128)(2,1)}, bf16[1,32,128,128]{3,2,1,0:T(8,128)(2,1)}) custom-call(s32[1]{0:T(128)} %bitcast.head_ref, bf16[32,136,128]{2,1,0:T(8,128)(2,1)S(1)} %all-to-all-done.x_ref, bf16[1,32,128,128]{3,2,1,0:T(8,128)(2,1)S(1)} %copy-done.1, bf16[1,32,128,128]{3,2,1,0:T(8,128)(2,1)S(1)} %copy-done.4, ...), custom_call_target="tpu_custom_call" | custom-call | flops 99999997952 | bytes 6000000 | tf_op jit(solution)/shard_map/pool_grads/pallas_call | solution.py:349
  116.5 1.1 unpack_heads.2
  117.6 11.7 %all-to-all-done.2.y_ref = bf16[32,136,128]{2,1,0:T(8,128)(2,1)S(1)} async-done(((bf16[32,136,128]{2,1,0:T(8,128)(2,1)}), bf16[32,136,128]{2,1,0:T(8,128)(2,1)S(1)}, u32[]{:S(2)}, u32[]{:S(2)}) %all-to-all-start.2) | async-done | bytes 1114144 | tf_op jit(solution)/shard_map/all_to_all | solution.py:443
  129.2 1.7 %unpack_heads.3 = (bf16[1,2,64,4096]{3,2,1,0:T(8,128)(2,1)}, f32[32,192]{1,0:T(8,128)}) custom-call(bf16[32,136,128]{2,1,0:T(8,128)(2,1)S(1)} %all-to-all-done.2.y_ref), custom_call_target="tpu_custom_call" | custom-call | tf_op jit(solution)/shard_map/unpack_heads/pallas_call | solution.py:422
  (38 shorter events, 6.2 us)
Async XLA Ops:
  4.0 14.6 %collective-permute-start = (bf16[8,128,128]{2,1,0:T(8,128)(2,1)}, bf16[8,128,128]{2,1,0:T(8,128)(2,1)S(1)}, u32[]{:S(2)}, u32[]{:S(2)}) collective-permute-start(bf16[8,128,128]{2,1,0:T(8,128)(2,1)} %get-tuple-element.33), channel_id=1, source_target_pairs={{0,8},{1,9},{2,10},{3,11},{4,12},{5,13},{6,14},{7,15},{8,16},{9,17... | collective-permute-start | bytes 786440 | tf_op jit(solution)/shard_map/ppermute | solution.py:158
  5.6 14.6 %collective-permute-start.1 = (bf16[8,128,128]{2,1,0:T(8,128)(2,1)}, bf16[8,128,128]{2,1,0:T(8,128)(2,1)S(1)}, u32[]{:S(2)}, u32[]{:S(2)}) collective-permute-start(bf16[8,128,128]{2,1,0:T(8,128)(2,1)} %get-tuple-element.34), channel_id=1, source_target_pairs={{0,16},{1,17},{2,18},{3,19},{4,20},{5,21},{6,22},{7,23},{8,24},{9,... | collective-permute-start | bytes 786440 | tf_op jit(solution)/shard_map/ppermute | solution.py:158
  8.3 11.9 %collective-permute-start.2 = (bf16[8,128,128]{2,1,0:T(8,128)(2,1)}, bf16[8,128,128]{2,1,0:T(8,128)(2,1)S(1)}, u32[]{:S(2)}, u32[]{:S(2)}) collective-permute-start(bf16[8,128,128]{2,1,0:T(8,128)(2,1)} %get-tuple-element.35), channel_id=1, source_target_pairs={{0,24},{1,25},{2,26},{3,27},{4,28},{5,29},{6,30},{7,31},{8,0},{9,1... | collective-permute-start | bytes 786440 | tf_op jit(solution)/shard_map/ppermute | solution.py:158
  9.8 39.3 %all-to-all-start = ((bf16[32,136,128]{2,1,0:T(8,128)(2,1)}), bf16[32,136,128]{2,1,0:T(8,128)(2,1)S(1)}, u32[]{:S(2)}, u32[]{:S(2)}) async-start(bf16[32,136,128]{2,1,0:T(8,128)(2,1)} %get-tuple-element.31), calls=%async_computation | async-start | bytes 2228224 | tf_op jit(solution)/shard_map/all_to_all | solution.py:443
  18.7 2.9 %copy-start.10 = (bf16[8,128,128]{2,1,0:T(8,128)(2,1)}, bf16[8,128,128]{2,1,0:T(8,128)(2,1)S(1)}, u32[]{:S(2)}) copy-start(bf16[8,128,128]{2,1,0:T(8,128)(2,1)S(1)} %collective-permute-done.refs_1_) | copy-start | bytes 786436
  20.2 0.7 copy-start.11
  20.9 0.7 copy-start.12
  21.6 27.4 %copy-start = (bf16[1,32,128,128]{3,2,1,0:T(8,128)(2,1)S(1)}, bf16[1,32,128,128]{3,2,1,0:T(8,128)(2,1)}, u32[]{:S(2)}) copy-start(bf16[1,32,128,128]{3,2,1,0:T(8,128)(2,1)} %keys_ref.5) | copy-start | bytes 3145732
  21.6 27.4 %copy-start.2 = (bf16[1,32,128,128]{3,2,1,0:T(8,128)(2,1)S(1)}, bf16[1,32,128,128]{3,2,1,0:T(8,128)(2,1)}, u32[]{:S(2)}) copy-start(bf16[1,32,128,128]{3,2,1,0:T(8,128)(2,1)} %values_ref.5) | copy-start | bytes 3145732
  21.6 27.4 %copy-start.5 = (f32[32,192]{1,0:T(8,128)S(1)}, f32[32,192]{1,0:T(8,128)}, u32[]{:S(2)}) copy-start(f32[32,192]{1,0:T(8,128)} %rel_ref.5) | copy-start | bytes 73732
  24.0 30.3 %collective-permute-start.3 = (bf16[4,128,128]{2,1,0:T(8,128)(2,1)}, bf16[4,128,128]{2,1,0:T(8,128)(2,1)S(1)}, u32[]{:S(2)}, u32[]{:S(2)}) collective-permute-start(bf16[4,128,128]{2,1,0:T(8,128)(2,1)} %get-tuple-element.43), channel_id=1, source_target_pairs={{0,1},{1,2},{2,3},{3,4},{4,5},{5,6},{6,7},{7,0},{8,9},{9,10},{10,1... | collective-permute-start | bytes 393224 | tf_op jit(solution)/shard_map/ppermute | solution.py:158
  26.0 31.8 %collective-permute-start.4 = (bf16[4,128,128]{2,1,0:T(8,128)(2,1)}, bf16[4,128,128]{2,1,0:T(8,128)(2,1)S(1)}, u32[]{:S(2)}, u32[]{:S(2)}) collective-permute-start(bf16[4,128,128]{2,1,0:T(8,128)(2,1)} %get-tuple-element.44), channel_id=1, source_target_pairs={{0,2},{1,3},{2,4},{3,5},{4,6},{5,7},{6,0},{7,1},{8,10},{9,11},{10,... | collective-permute-start | bytes 393224 | tf_op jit(solution)/shard_map/ppermute | solution.py:158
  30.1 37.8 %collective-permute-start.6 = (bf16[4,128,128]{2,1,0:T(8,128)(2,1)}, bf16[4,128,128]{2,1,0:T(8,128)(2,1)}, u32[]{:S(2)}, u32[]{:S(2)}) collective-permute-start(bf16[4,128,128]{2,1,0:T(8,128)(2,1)} %get-tuple-element.46), channel_id=1, source_target_pairs={{0,4},{1,5},{2,6},{3,7},{4,0},{5,1},{6,2},{7,3},{8,12},{9,13},{10,... | collective-permute-start | bytes 393224 | tf_op jit(solution)/shard_map/ppermute | solution.py:158
  35.2 32.8 %collective-permute-start.8 = (bf16[4,128,128]{2,1,0:T(8,128)(2,1)}, bf16[4,128,128]{2,1,0:T(8,128)(2,1)}, u32[]{:S(2)}, u32[]{:S(2)}) collective-permute-start(bf16[4,128,128]{2,1,0:T(8,128)(2,1)} %get-tuple-element.48), channel_id=1, source_target_pairs={{0,6},{1,7},{2,0},{3,1},{4,2},{5,3},{6,4},{7,5},{8,14},{9,15},{10,... | collective-permute-start | bytes 393224 | tf_op jit(solution)/shard_map/ppermute | solution.py:158
  38.0 29.9 %collective-permute-start.9 = (bf16[4,128,128]{2,1,0:T(8,128)(2,1)}, bf16[4,128,128]{2,1,0:T(8,128)(2,1)}, u32[]{:S(2)}, u32[]{:S(2)}) collective-permute-start(bf16[4,128,128]{2,1,0:T(8,128)(2,1)} %get-tuple-element.49), channel_id=1, source_target_pairs={{0,7},{1,0},{2,1},{3,2},{4,3},{5,4},{6,5},{7,6},{8,15},{9,8},{10,9... | collective-permute-start | bytes 393224 | tf_op jit(solution)/shard_map/ppermute | solution.py:158
  54.3 16.1 %copy-start.6 = (f32[32,192]{1,0:T(8,128)S(1)}, f32[32,192]{1,0:T(8,128)}, u32[]{:S(2)}) copy-start(f32[32,192]{1,0:T(8,128)} %rel_ref.5) | copy-start | bytes 73732
  54.4 16.1 %collective-permute-start.5 = (bf16[4,128,128]{2,1,0:T(8,128)(2,1)}, bf16[4,128,128]{2,1,0:T(8,128)(2,1)}, u32[]{:S(2)}, u32[]{:S(2)}) collective-permute-start(bf16[4,128,128]{2,1,0:T(8,128)(2,1)} %get-tuple-element.45), channel_id=1, source_target_pairs={{0,3},{1,4},{2,5},{3,6},{4,7},{5,0},{6,1},{7,2},{8,11},{9,12},{10,... | collective-permute-start | bytes 393224 | tf_op jit(solution)/shard_map/ppermute | solution.py:158
  57.8 12.6 %collective-permute-start.7 = (bf16[4,128,128]{2,1,0:T(8,128)(2,1)}, bf16[4,128,128]{2,1,0:T(8,128)(2,1)}, u32[]{:S(2)}, u32[]{:S(2)}) collective-permute-start(bf16[4,128,128]{2,1,0:T(8,128)(2,1)} %get-tuple-element.47), channel_id=1, source_target_pairs={{0,5},{1,6},{2,7},{3,0},{4,1},{5,2},{6,3},{7,4},{8,13},{9,14},{10,... | collective-permute-start | bytes 393224 | tf_op jit(solution)/shard_map/ppermute | solution.py:158
  60.2 31.8 %all-to-all-start.1 = ((bf16[32,128,128]{2,1,0:T(8,128)(2,1)}), bf16[32,128,128]{2,1,0:T(8,128)(2,1)S(1)}, u32[]{:S(2)}, u32[]{:S(2)}) async-start(bf16[32,128,128]{2,1,0:T(8,128)(2,1)} %attention_forward.1), calls=%async_computation.1 | async-start | bytes 2097152 | tf_op jit(solution)/shard_map/all_to_all | solution.py:443
  70.5 1.2 copy-start.3
  71.7 0.9 copy-start.8
  79.5 1.2 collective-permute-start.10
  80.7 4.1 %collective-permute-start.13 = (f32[1,256]{1,0:T(1,128)S(1)}, f32[1,256]{1,0:T(1,128)S(1)}, u32[]{:S(2)}, u32[]{:S(2)}) collective-permute-start(f32[1,256]{1,0:T(1,128)S(1)} %add.12), channel_id=1, source_target_pairs={{0,192},{32,224},{64,128},{96,160},{128,64},{160,96},{192,0},{224,... | collective-permute-start | bytes 3080 | tf_op jit(solution)/shard_map/ppermute | solution.py:435
  81.2 5.1 %collective-permute-start.12 = (f32[1,256]{1,0:T(1,128)S(1)}, f32[1,256]{1,0:T(1,128)S(1)}, u32[]{:S(2)}, u32[]{:S(2)}) collective-permute-start(f32[1,256]{1,0:T(1,128)S(1)} %add.12), channel_id=1, source_target_pairs={{0,128},{32,160},{64,192},{96,224},{128,0},{160,32},{192,64},{224,... | collective-permute-start | bytes 3080 | tf_op jit(solution)/shard_map/ppermute | solution.py:435
  84.1 3.6 %collective-permute-start.11 = (f32[1,256]{1,0:T(1,128)S(1)}, f32[1,256]{1,0:T(1,128)S(1)}, u32[]{:S(2)}, u32[]{:S(2)}) collective-permute-start(f32[1,256]{1,0:T(1,128)S(1)} %add.12), channel_id=1, source_target_pairs={{0,64},{32,96},{64,0},{96,32},{128,192},{160,224},{192,128},{224,1... | collective-permute-start | bytes 3080 | tf_op jit(solution)/shard_map/ppermute | solution.py:435
  92.0 37.3 %all-to-all-start.2 = ((bf16[32,136,128]{2,1,0:T(8,128)(2,1)}), bf16[32,136,128]{2,1,0:T(8,128)(2,1)S(1)}, u32[]{:S(2)}, u32[]{:S(2)}) async-start(bf16[32,136,128]{2,1,0:T(8,128)(2,1)} %add_bias_row.1), calls=%async_computation.2 | async-start | bytes 2228224 | tf_op jit(solution)/shard_map/all_to_all | solution.py:443
  100.2 1.2 copy-start.1
  101.4 1.2 copy-start.4
  102.6 0.8 copy-start.7
  103.4 0.9 copy-start.9
